TPU v7x, 32 devices: a whole 2x2x4 slice. The times are simulated.
32 devices in a mesh: gx: 4 (over y, core), gy: 8 (over z, x).
Axes of the slice: x: 2, y: 2, z: 4, core: 2. Of those that a mesh axis runs over, the one named last changes fastest.
Arguments:
- text_tokens: bfloat16 [256, 100, 768], P(('gx', 'gy')), may hold values from -6 to 6
- image_regions: bfloat16 [256, 36, 1024], P(('gx', 'gy')), may hold values from -6 to 6
- caption_lengths: int32 [256], P(('gx', 'gy')), may hold values from 8 to 100, as said below
- region_mask: int32 [256, 36], P(('gx', 'gy')), may hold values 0 or 1
- text_cotangent: bfloat16 [256, 100, 768], P(('gx', 'gy')), may hold values from -6 to 6
- image_cotangent: bfloat16 [256, 36, 1024], P(('gx', 'gy')), may hold values from -6 to 6
- text_query: bfloat16 [768, 1024], P(('gx', 'gy')), may hold values from -0.21875 to 0.21875
- image_key: bfloat16 [1024, 1024], P(('gx', 'gy')), may hold values from -0.1875 to 0.1875
- image_value: bfloat16 [1024, 1024], P(('gx', 'gy')), may hold values from -0.1875 to 0.1875
- text_merge: bfloat16 [1024, 768], P(('gx', 'gy')), may hold values from -1 to 1
- text_gain_cross: bfloat16 [768], P(('gx', 'gy')), may hold values from 0.5 to 1.5
- image_query: bfloat16 [1024, 1024], P(('gx', 'gy')), may hold values from -0.1875 to 0.1875
- text_key: bfloat16 [768, 1024], P(('gx', 'gy')), may hold values from -0.21875 to 0.21875
- text_value: bfloat16 [768, 1024], P(('gx', 'gy')), may hold values from -0.21875 to 0.21875
- image_merge: bfloat16 [1024, 1024], P(('gx', 'gy')), may hold values from -1.25 to 1.25
- image_gain_cross: bfloat16 [1024], P(('gx', 'gy')), may hold values from 0.5 to 1.5
- text_up: bfloat16 [768, 3072], P(('gx', 'gy')), may hold values from -0.21875 to 0.21875
- text_bias: bfloat16 [3072], P(('gx', 'gy')), may hold values from -3 to 3
- text_down: bfloat16 [3072, 768], P(('gx', 'gy')), may hold values from -0.109375 to 0.109375
- text_gain_ffn: bfloat16 [768], P(('gx', 'gy')), may hold values from 0.5 to 1.5
- image_up: bfloat16 [1024, 1024], P(('gx', 'gy')), may hold values from -0.1875 to 0.1875
- image_bias: bfloat16 [1024], P(('gx', 'gy')), may hold values from -3 to 3
- image_down: bfloat16 [1024, 1024], P(('gx', 'gy')), may hold values from -0.1875 to 0.1875
- image_gain_ffn: bfloat16 [1024], P(('gx', 'gy')), may hold values from 0.5 to 1.5
- text_self: bfloat16 [768, 2304], P(('gx', 'gy')), may hold values from -0.21875 to 0.21875
- text_mix: bfloat16 [768, 768], P(('gx', 'gy')), may hold values from -1.5 to 1.5
- text_gain_self: bfloat16 [768], P(('gx', 'gy')), may hold values from 0.5 to 1.5
- image_self: bfloat16 [1024, 3072], P(('gx', 'gy')), may hold values from -0.1875 to 0.1875
- image_mix: bfloat16 [1024, 1024], P(('gx', 'gy')), may hold values from -1 to 1
- image_gain_self: bfloat16 [1024], P(('gx', 'gy')), may hold values from 0.5 to 1.5
Outputs:
- text_output: bfloat16 [256, 100, 768], P(('gx', 'gy'))
- image_output: bfloat16 [256, 36, 1024], P(('gx', 'gy'))
- grad_text: float32 [256, 100, 768], P(('gx', 'gy'))
- grad_image: float32 [256, 36, 1024], P(('gx', 'gy'))
- grad_text_query: float32 [768, 1024], P(('gx', 'gy'))
- grad_image_key: float32 [1024, 1024], P(('gx', 'gy'))
- grad_image_value: float32 [1024, 1024], P(('gx', 'gy'))
- grad_text_merge: float32 [1024, 768], P(('gx', 'gy'))
- grad_text_gain_cross: float32 [768], P(('gx', 'gy'))
- grad_image_query: float32 [1024, 1024], P(('gx', 'gy'))
- grad_text_key: float32 [768, 1024], P(('gx', 'gy'))
- grad_text_value: float32 [768, 1024], P(('gx', 'gy'))
- grad_image_merge: float32 [1024, 1024], P(('gx', 'gy'))
- grad_image_gain_cross: float32 [1024], P(('gx', 'gy'))
- grad_text_up: float32 [768, 3072], P(('gx', 'gy'))
- grad_text_bias: float32 [3072], P(('gx', 'gy'))
- grad_text_down: float32 [3072, 768], P(('gx', 'gy'))
- grad_text_gain_ffn: float32 [768], P(('gx', 'gy'))
- grad_image_up: float32 [1024, 1024], P(('gx', 'gy'))
- grad_image_bias: float32 [1024], P(('gx', 'gy'))
- grad_image_down: float32 [1024, 1024], P(('gx', 'gy'))
- grad_image_gain_ffn: float32 [1024], P(('gx', 'gy'))
- grad_text_self: float32 [768, 2304], P(('gx', 'gy'))
- grad_text_mix: float32 [768, 768], P(('gx', 'gy'))
- grad_text_gain_self: float32 [768], P(('gx', 'gy'))
- grad_image_self: float32 [1024, 3072], P(('gx', 'gy'))
- grad_image_mix: float32 [1024, 1024], P(('gx', 'gy'))
- grad_image_gain_self: float32 [1024], P(('gx', 'gy'))
Inputs may be any that keep to these rules, and one draw needn't show every extreme that they name: `caption_lengths`: each caption has between 8 and 100 tokens; some caption has each of these two lengths.
All inputs are finite; a program needn't handle non-finite values. No bound on the sum of `region_mask` on one device may be relied on, other than what follows from the above.
Results may differ from a plain program's by a relative error of at most 0.024.
Values may be sent and summed in bfloat16 or wider, within the bound.
No kernel may reach another device: no remote copies, remote signals or barrier semaphores. Data moves between devices by JAX's collectives and lax.ppermute only.
A program may use at most 320 MiB of HBM per device.

v0:
```python
import functools
import math

import jax
import jax.numpy as jnp
from jax import lax
from jax.experimental import pallas as pl
from jax.experimental.pallas import tpu as pltpu
from jax.sharding import PartitionSpec as P

HEADS = 8
TEXT_HEADS = 12
IMAGE_HEADS = 8
EPSILON = 1e-05
MASKED = -1000000000.0
PADDED = -2000000000.0
LANES = 128
AXES = ("gx", "gy")
F32 = jnp.float32
BF16 = jnp.bfloat16
VECTOR_NAMES = (
    "text_gain_cross",
    "image_gain_cross",
    "text_bias",
    "text_gain_ffn",
    "image_bias",
    "image_gain_ffn",
    "text_gain_self",
    "image_gain_self",
)


def project(left, right):
    return jnp.dot(left, right, preferred_element_type=F32)


def project_back(left, right):
    return lax.dot_general(left, right, (((1,), (1,)), ((), ())), preferred_element_type=F32)


def weight_grad(left, right):
    return lax.dot_general(left, right, (((0,), (0,)), ((), ())), preferred_element_type=F32)


def round_up(size, step):
    return -(-size // step) * step


def stack_halves(rows):
    wide = rows.astype(F32)
    first = lax.broadcasted_iota(jnp.int32, wide.shape, 1) < LANES // 2
    zero = jnp.zeros_like(wide)
    return jnp.concatenate([jnp.where(first, wide, zero), jnp.where(first, zero, wide)], 0).astype(BF16)


def join_halves(rows):
    count = rows.shape[0] // 2
    first = lax.broadcasted_iota(jnp.int32, (count, LANES), 1) < LANES // 2
    return jnp.where(first, rows[:count], rows[count:])


def softmax_rows(queries, keys, fill, scale):
    scores = project_back(queries, keys) * scale
    scores = jnp.where(fill < 0.0, fill, scores)
    powers = jnp.exp(scores - jnp.max(scores, -1, keepdims=True))
    return powers / jnp.sum(powers, -1, keepdims=True)


def head_forward(queries, keys, values, fill, size):
    scale = 1.0 / math.sqrt(size)
    split = size < LANES
    probs = softmax_rows(stack_halves(queries) if split else queries, keys, fill, scale)
    mixed = project(probs.astype(BF16), values)
    return (join_halves(mixed) if split else mixed).astype(BF16)


def head_backward(queries, keys, values, fill, size, d_mixed):
    scale = 1.0 / math.sqrt(size)
    split = size < LANES
    if split:
        queries, d_mixed = stack_halves(queries), stack_halves(d_mixed)
    probs = softmax_rows(queries, keys, fill, scale)
    d_probs = project_back(d_mixed, values)
    d_values = weight_grad(probs.astype(BF16), d_mixed)
    d_scores = probs * (d_probs - jnp.sum(probs * d_probs, -1, keepdims=True))
    d_scores = jnp.where(fill < 0.0, 0.0, d_scores).astype(BF16)
    d_queries = project(d_scores, keys) * scale
    d_keys = weight_grad(d_scores, queries) * scale
    if split:
        d_queries = join_halves(d_queries)
    return d_queries.astype(BF16), d_keys.astype(BF16), d_values.astype(BF16)


def lane_blocks(width):
    return [slice(at, at + LANES) for at in range(0, width, LANES)]


def shifted(block, by):
    return slice(block.start + by, block.stop + by)


def cross_forward_kernel(size, text_ref, image_ref, text_fill_ref, image_fill_ref, mixed_text_ref, mixed_image_ref):
    width = text_ref.shape[-1] // 3
    text_fill, image_fill = text_fill_ref[0], image_fill_ref[0]
    for own in lane_blocks(width):
        key, value = shifted(own, width), shifted(own, 2 * width)
        mixed_text_ref[0, :, own] = head_forward(
            text_ref[0, :, own], image_ref[0, :, key], image_ref[0, :, value], image_fill, size
        )
        mixed_image_ref[0, :, own] = head_forward(
            image_ref[0, :, own], text_ref[0, :, key], text_ref[0, :, value], text_fill, size
        )


def cross_backward_kernel(
    size, text_ref, image_ref, text_fill_ref, image_fill_ref, d_text_ref, d_image_ref, out_text_ref, out_image_ref
):
    width = text_ref.shape[-1] // 3
    text_fill, image_fill = text_fill_ref[0], image_fill_ref[0]
    for own in lane_blocks(width):
        key, value = shifted(own, width), shifted(own, 2 * width)
        d_query, d_key, d_value = head_backward(
            text_ref[0, :, own], image_ref[0, :, key], image_ref[0, :, value], image_fill, size, d_text_ref[0, :, own]
        )
        out_text_ref[0, :, own] = d_query
        out_image_ref[0, :, key] = d_key
        out_image_ref[0, :, value] = d_value
        d_query, d_key, d_value = head_backward(
            image_ref[0, :, own], text_ref[0, :, key], text_ref[0, :, value], text_fill, size, d_image_ref[0, :, own]
        )
        out_image_ref[0, :, own] = d_query
        out_text_ref[0, :, key] = d_key
        out_text_ref[0, :, value] = d_value


def self_forward_kernel(size, triple_ref, fill_ref, mixed_ref):
    width = triple_ref.shape[-1] // 3
    fill = fill_ref[0]
    for own in lane_blocks(width):
        key, value = shifted(own, width), shifted(own, 2 * width)
        mixed_ref[0, :, own] = head_forward(
            triple_ref[0, :, own], triple_ref[0, :, key], triple_ref[0, :, value], fill, size
        )


def self_backward_kernel(size, triple_ref, fill_ref, d_mixed_ref, out_ref):
    width = triple_ref.shape[-1] // 3
    fill = fill_ref[0]
    for own in lane_blocks(width):
        key, value = shifted(own, width), shifted(own, 2 * width)
        d_query, d_key, d_value = head_backward(
            triple_ref[0, :, own], triple_ref[0, :, key], triple_ref[0, :, value], fill, size, d_mixed_ref[0, :, own]
        )
        out_ref[0, :, own] = d_query
        out_ref[0, :, key] = d_key
        out_ref[0, :, value] = d_value


def per_pair(kernel, inputs, out_widths, flops):
    pairs = inputs[0].shape[0]

    def spec(rows, width):
        return pl.BlockSpec((1, rows, width), lambda pair: (pair, 0, 0))

    moved = sum(array.size * array.dtype.itemsize for array in inputs)
    moved += sum(pairs * rows * width * 2 for rows, width in out_widths)
    return pl.pallas_call(
        kernel,
        grid=(pairs,),
        in_specs=[spec(*array.shape[1:]) for array in inputs],
        out_specs=[spec(rows, width) for rows, width in out_widths],
        out_shape=[jax.ShapeDtypeStruct((pairs, rows, width), BF16) for rows, width in out_widths],
        compiler_params=pltpu.CompilerParams(vmem_limit_bytes=48 * 1024 * 1024),
        cost_estimate=pl.CostEstimate(flops=flops, bytes_accessed=moved, transcendentals=0),
    )(*inputs)


def beside(array, parts):
    rows, width = array.shape
    return jnp.concatenate([array[at * (rows // parts) : (at + 1) * (rows // parts)] for at in range(parts)], 1)


def gather(packed):
    return lax.all_gather(packed, AXES, axis=0, tiled=False)


def whole(block, parts=1):
    devices, rows, width = block.shape
    if parts > 1:
        block = block.reshape(devices, rows, parts, width // parts).transpose(0, 2, 1, 3)
    return block.reshape(devices * rows * parts, width // parts)


def owned_rows(matrix, devices, parts=1):
    rows, width = matrix.shape
    rows //= devices
    if parts == 1:
        return matrix.reshape(devices, rows, width)
    block = matrix.reshape(devices, parts, rows // parts, width).transpose(0, 2, 1, 3)
    return block.reshape(devices, rows // parts, parts * width)


def mesh_bits(sizes):
    bits = []
    for axis in AXES:
        bits += [(axis, bit) for bit in reversed(range(sizes[axis].bit_length() - 1))]
    return bits


def halve(total, bits, which):
    axis, bit = which
    place = bits.index(which)
    own = (lax.axis_index(axis) >> bit) & 1
    count = lax.axis_size(axis)
    away = lax.dynamic_index_in_dim(total, 1 - own, place, keepdims=False)
    kept = lax.dynamic_index_in_dim(total, own, place, keepdims=False)
    got = lax.ppermute(away, axis, [(at, at ^ (1 << bit)) for at in range(count)])
    left = [one for one in bits if one != which]
    return kept.astype(F32) + got.astype(F32), left


def sum_to_owners(packed, sizes):
    bits = mesh_bits(sizes)
    low = (sizes["gy"].bit_length() - 1) // 2
    core = [("gx", 0)] if sizes["gx"] > 1 else []
    rows = [one for one in bits if one[0] == "gx" and one not in core]
    columns = [one for one in bits if one[0] == "gy" and one[1] < low]
    rest = [one for one in bits if one[0] == "gy" and one[1] >= low]
    width = packed.shape[-1]
    total = packed.reshape((2,) * len(bits) + packed.shape[1:])
    for which in core:
        total, bits = halve(total, bits, which)
        total = total.astype(BF16)
    halves = []
    for part, order in ((0, columns + rows), (1, rows + columns)):
        part_total, part_bits = total[..., part * width // 2 : (part + 1) * width // 2], bits
        for which in order:
            part_total, part_bits = halve(part_total, part_bits, which)
            part_total = part_total.astype(BF16)
        halves.append(part_total)
    total, bits = jnp.concatenate(halves, -1), part_bits
    for which in rest:
        total, bits = halve(total.astype(BF16), bits, which)
    return total.astype(F32)


def normed_rows(values_in):
    centred = values_in - jnp.mean(values_in, -1, keepdims=True)
    rate = lax.rsqrt(jnp.mean(centred * centred, -1, keepdims=True) + EPSILON)
    return centred * rate, rate


def normed_back(unit, rate, gain, d_out):
    d_unit = d_out * gain
    mean_unit = jnp.mean(d_unit, -1, keepdims=True)
    mean_cross = jnp.mean(d_unit * unit, -1, keepdims=True)
    return rate * (d_unit - mean_unit - unit * mean_cross), jnp.sum(d_out * unit, 0)


GELU_RATE = math.sqrt(2.0 / math.pi)
GELU_CUBE = 0.044715


def gelu(values_in):
    inner = jnp.tanh(GELU_RATE * (values_in + GELU_CUBE * values_in * values_in * values_in))
    return 0.5 * values_in * (1.0 + inner)


def gelu_slope(values_in):
    square = values_in * values_in
    inner = jnp.tanh(GELU_RATE * values_in * (1.0 + GELU_CUBE * square))
    return 0.5 * (1.0 + inner) + 0.5 * values_in * (1.0 - inner * inner) * GELU_RATE * (1.0 + 3.0 * GELU_CUBE * square)


def per_device(sizes, *given):
    (
        text_tokens,
        image_regions,
        caption_lengths,
        region_mask,
        text_cotangent,
        image_cotangent,
        text_query,
        image_key,
        image_value,
        text_merge,
        text_gain_cross,
        image_query,
        text_key,
        text_value,
        image_merge,
        image_gain_cross,
        text_up,
        text_bias,
        text_down,
        text_gain_ffn,
        image_up,
        image_bias,
        image_down,
        image_gain_ffn,
        text_self,
        text_mix,
        text_gain_self,
        image_self,
        image_mix,
        image_gain_self,
    ) = given
    devices = sizes["gx"] * sizes["gy"]
    pairs, length, text_width = text_tokens.shape
    regions, image_width = image_regions.shape[1:]
    inner = text_query.shape[1]

    vectors = (
        text_gain_cross,
        image_gain_cross,
        text_bias,
        text_gain_ffn,
        image_bias,
        image_gain_ffn,
        text_gain_self,
        image_gain_self,
    )
    vector = jnp.concatenate(vectors)
    half_rows = image_merge.shape[0] // 2
    row_text, row_image = text_query.shape[0], image_query.shape[0]
    merge_rows = text_merge.shape[0] // 4
    vector_block = jnp.pad(vector[None, :], ((0, half_rows - 1), (0, image_width - vector.shape[0])))
    packed_cross = jnp.concatenate(
        [
            jnp.concatenate([text_query, text_key, text_value], 1),
            jnp.concatenate([image_query, image_key, image_value], 1),
            jnp.concatenate([beside(image_merge, 2), vector_block], 1),
            beside(text_merge, 4),
        ],
        0,
    )
    packed_text = jnp.concatenate([text_up, beside(text_down, 4), jnp.concatenate([text_self, text_mix], 1)], 0)
    packed_image = jnp.concatenate([image_self, jnp.concatenate([image_up, image_down, image_mix], 1)], 0)
    all_cross = gather(packed_cross)
    all_text = gather(packed_text)
    all_image = gather(packed_image)

    at = row_text
    weight_text = whole(all_cross[:, :at])
    weight_image = whole(all_cross[:, at : at + row_image])
    at += row_image
    full_image_merge = whole(all_cross[:, at : at + half_rows, : 2 * image_width], 2)
    all_vectors = all_cross[:, at, 2 * image_width :]
    at += half_rows
    full_text_merge = whole(all_cross[:, at : at + merge_rows], 4)
    full = {}
    at = 0
    for name, piece in zip(VECTOR_NAMES, vectors):
        full[name] = all_vectors[:, at : at + piece.shape[0]].reshape(-1).astype(F32)
        at += piece.shape[0]
    full_text_up = whole(all_text[:, :row_text])
    full_text_down = whole(all_text[:, row_text : 2 * row_text], 4)
    full_text_self = whole(all_text[:, 2 * row_text :, : 3 * text_width])
    full_text_mix = whole(all_text[:, 2 * row_text :, 3 * text_width :])
    full_image_self = whole(all_image[:, :row_image])
    full_image_up = whole(all_image[:, row_image:, :image_width])
    full_image_down = whole(all_image[:, row_image:, image_width : 2 * image_width])
    full_image_mix = whole(all_image[:, row_image:, 2 * image_width :])

    text_slots, image_slots = round_up(length, 8), round_up(regions, 8)

    def padded(array, slots):
        array = jnp.pad(array, ((0, 0), (0, slots - array.shape[1]), (0, 0)))
        return array.reshape(pairs * slots, array.shape[2])

    def rows_of(array):
        return array.reshape(-1, array.shape[-1])

    def pairs_of(array):
        return array.reshape(pairs, array.shape[0] // pairs, array.shape[1])

    text_rows, image_rows = padded(text_tokens, text_slots), padded(image_regions, image_slots)
    d_text_out = padded(text_cotangent, text_slots).astype(F32)
    d_image_out = padded(image_cotangent, image_slots).astype(F32)
    text_at = jnp.arange(text_slots)[None, :]
    text_live = text_at < caption_lengths[:, None]
    image_live = jnp.pad(region_mask, ((0, 0), (0, image_slots - regions))) > 0
    text_fill = jnp.where(text_live, 0.0, jnp.where(text_at < length, MASKED, PADDED))[:, None, :]
    image_at = jnp.arange(image_slots)[None, :]
    image_fill = jnp.where(image_live, 0.0, jnp.where(image_at < regions, MASKED, PADDED))[:, None, :]
    text_keep = text_live.astype(F32).reshape(-1, 1)
    image_keep = image_live.astype(F32).reshape(-1, 1)

    triple_text = project(text_rows, weight_text).astype(BF16)
    triple_image = project(image_rows, weight_image).astype(BF16)
    cross_size = inner // HEADS
    cross_flops = 4 * pairs * text_slots * image_slots * inner * 2
    cross_text, cross_image = per_pair(
        functools.partial(cross_forward_kernel, cross_size),
        [pairs_of(triple_text), pairs_of(triple_image), text_fill, image_fill],
        [(text_slots, inner), (image_slots, inner)],
        cross_flops,
    )
    cross_text, cross_image = rows_of(cross_text), rows_of(cross_image)
    unit_text_1, rate_text_1 = normed_rows(text_rows.astype(F32) + project(cross_text, full_text_merge))
    unit_image_1, rate_image_1 = normed_rows(image_rows.astype(F32) + project(cross_image, full_image_merge))

    def stream(
        unit_1, rate_1, gain_1, up, bias, down, gain_2, joint, mix, gain_3, fill, keep, d_out, size, slots, flops
    ):
        width = unit_1.shape[1]
        first = unit_1 * gain_1
        first_low = first.astype(BF16)
        hidden = project(first_low, up) + bias
        active = gelu(hidden).astype(BF16)
        hidden = hidden.astype(BF16)
        unit_2, rate_2 = normed_rows(first + project(active, down))
        second = unit_2 * gain_2
        second_low = second.astype(BF16)
        triple = project(second_low, joint).astype(BF16)
        (mixed,) = per_pair(
            functools.partial(self_forward_kernel, size), [pairs_of(triple), fill], [(slots, width)], flops
        )
        mixed = rows_of(mixed)
        unit_3, rate_3 = normed_rows(second + project(mixed, mix))
        out = (unit_3 * gain_3 * keep).astype(BF16)

        d_third, g_gain_3 = normed_back(unit_3, rate_3, gain_3, d_out * keep)
        d_branch = d_third.astype(BF16)
        g_mix = weight_grad(mixed, d_branch).astype(BF16)
        d_mixed = project_back(d_branch, mix).astype(BF16)
        (d_triple,) = per_pair(
            functools.partial(self_backward_kernel, size),
            [pairs_of(triple), fill, pairs_of(d_mixed)],
            [(slots, 3 * width)],
            flops * 5 // 2,
        )
        d_triple = rows_of(d_triple)
        g_joint = weight_grad(second_low, d_triple).astype(BF16)
        d_second = d_third + project_back(d_triple, joint)
        d_sum, g_gain_2 = normed_back(unit_2, rate_2, gain_2, d_second)
        d_sum_low = d_sum.astype(BF16)
        g_down = weight_grad(active, d_sum_low).astype(BF16)
        d_hidden = (gelu_slope(hidden.astype(F32)) * project_back(d_sum_low, down)).astype(BF16)
        g_bias = jnp.sum(d_hidden.astype(F32), 0)
        g_up = weight_grad(first_low, d_hidden).astype(BF16)
        d_first = d_sum + project_back(d_hidden, up)
        d_resid, g_gain_1 = normed_back(unit_1, rate_1, gain_1, d_first)
        return out, d_resid, (g_mix, g_joint, g_down, g_up), (g_gain_1, g_bias, g_gain_2, g_gain_3)

    out_text, d_resid_text, (g_text_mix, g_text_self, g_text_down, g_text_up), vectors_text = stream(
        unit_text_1,
        rate_text_1,
        full["text_gain_cross"],
        full_text_up,
        full["text_bias"],
        full_text_down,
        full["text_gain_ffn"],
        full_text_self,
        full_text_mix,
        full["text_gain_self"],
        text_fill,
        text_keep,
        d_text_out,
        text_width // TEXT_HEADS,
        text_slots,
        4 * pairs * text_slots * text_slots * text_width * 2,
    )
    packed_text_grad = jnp.concatenate(
        [
            owned_rows(g_text_up, devices),
            owned_rows(g_text_down, devices, 4),
            jnp.concatenate([owned_rows(g_text_self, devices), owned_rows(g_text_mix, devices)], 2),
        ],
        1,
    )
    sum_text = sum_to_owners(packed_text_grad, sizes)
    out_image, d_resid_image, (g_image_mix, g_image_self, g_image_down, g_image_up), vectors_image = stream(
        unit_image_1,
        rate_image_1,
        full["image_gain_cross"],
        full_image_up,
        full["image_bias"],
        full_image_down,
        full["image_gain_ffn"],
        full_image_self,
        full_image_mix,
        full["image_gain_self"],
        image_fill,
        image_keep,
        d_image_out,
        image_width // IMAGE_HEADS,
        image_slots,
        4 * pairs * image_slots * image_slots * image_width,
    )
    packed_image_grad = jnp.concatenate(
        [
            owned_rows(g_image_self, devices),
            jnp.concatenate(
                [
                    owned_rows(g_image_up, devices),
                    owned_rows(g_image_down, devices),
                    owned_rows(g_image_mix, devices),
                ],
                2,
            ),
        ],
        1,
    )
    sum_image = sum_to_owners(packed_image_grad, sizes)

    d_merge_text = d_resid_text.astype(BF16)
    d_merge_image = d_resid_image.astype(BF16)
    g_text_merge = weight_grad(cross_text, d_merge_text).astype(BF16)
    g_image_merge = weight_grad(cross_image, d_merge_image).astype(BF16)
    d_heads_text = project_back(d_merge_text, full_text_merge).astype(BF16)
    d_heads_image = project_back(d_merge_image, full_image_merge).astype(BF16)
    d_triple_text, d_triple_image = per_pair(
        functools.partial(cross_backward_kernel, cross_size),
        [
            pairs_of(triple_text),
            pairs_of(triple_image),
            text_fill,
            image_fill,
            pairs_of(d_heads_text),
            pairs_of(d_heads_image),
        ],
        [(text_slots, 3 * inner), (image_slots, 3 * inner)],
        cross_flops * 5 // 2,
    )
    d_triple_text, d_triple_image = rows_of(d_triple_text), rows_of(d_triple_image)
    g_weight_text = weight_grad(text_rows, d_triple_text).astype(BF16)
    g_weight_image = weight_grad(image_rows, d_triple_image).astype(BF16)
    grad_text = d_resid_text + project_back(d_triple_text, weight_text)
    grad_image = d_resid_image + project_back(d_triple_image, weight_image)
    g_vectors = (
        vectors_text[0],
        vectors_image[0],
        vectors_text[1],
        vectors_text[2],
        vectors_image[1],
        vectors_image[2],
        vectors_text[3],
        vectors_image[3],
    )
    vector_rows = jnp.concatenate([piece.reshape(devices, -1) for piece in g_vectors], 1).astype(BF16)
    vector_rows = jnp.pad(
        vector_rows[:, None, :], ((0, 0), (0, half_rows - 1), (0, image_width - vector_rows.shape[1]))
    )
    packed_cross_grad = jnp.concatenate(
        [
            owned_rows(g_weight_text, devices),
            owned_rows(g_weight_image, devices),
            jnp.concatenate([owned_rows(g_image_merge, devices, 2), vector_rows], 2),
            owned_rows(g_text_merge, devices, 4),
        ],
        1,
    )
    sum_cross = sum_to_owners(packed_cross_grad, sizes)

    def apart(block, parts):
        return jnp.concatenate(jnp.split(block, parts, 1), 0)

    at = row_text
    sum_text_query, sum_text_key, sum_text_value = jnp.split(sum_cross[:at], 3, 1)
    sum_image_query, sum_image_key, sum_image_value = jnp.split(sum_cross[at : at + row_image], 3, 1)
    at += row_image
    sum_image_merge = apart(sum_cross[at : at + half_rows, : 2 * image_width], 2)
    sum_vectors = sum_cross[at, 2 * image_width :]
    at += half_rows
    sum_text_merge = apart(sum_cross[at:], 4)
    owned_vector = {}
    at = 0
    for name, piece in zip(VECTOR_NAMES, vectors):
        owned_vector[name] = sum_vectors[at : at + piece.shape[0]]
        at += piece.shape[0]
    return (
        pairs_of(out_text)[:, :length],
        pairs_of(out_image)[:, :regions],
        pairs_of(grad_text)[:, :length],
        pairs_of(grad_image)[:, :regions],
        sum_text_query,
        sum_image_key,
        sum_image_value,
        sum_text_merge,
        owned_vector["text_gain_cross"],
        sum_image_query,
        sum_text_key,
        sum_text_value,
        sum_image_merge,
        owned_vector["image_gain_cross"],
        sum_text[:row_text],
        owned_vector["text_bias"],
        apart(sum_text[row_text : 2 * row_text], 4),
        owned_vector["text_gain_ffn"],
        sum_image[row_image:, :image_width],
        owned_vector["image_bias"],
        sum_image[row_image:, image_width : 2 * image_width],
        owned_vector["image_gain_ffn"],
        sum_text[2 * row_text :, : 3 * text_width],
        sum_text[2 * row_text :, 3 * text_width :],
        owned_vector["text_gain_self"],
        sum_image[:row_image],
        sum_image[row_image:, 2 * image_width :],
        owned_vector["image_gain_self"],
    )


def solution(mesh):
    split = {1: P(AXES), 2: P(AXES, None), 3: P(AXES, None, None)}
    in_ranks = (3, 3, 1, 2, 3, 3) + tuple(
        1 if at in (4, 9, 11, 13, 15, 17, 20, 23) else 2 for at in range(24)
    )
    out_ranks = (3, 3, 3, 3) + in_ranks[6:]
    return jax.shard_map(
        functools.partial(per_device, dict(mesh.shape)),
        mesh=mesh,
        in_specs=tuple(split[rank] for rank in in_ranks),
        out_specs=tuple(split[rank] for rank in out_ranks),
        check_vma=False,
    )
```

profile of v0, /device:TPU:0, one launch (start us, length us, event | category | flops | bytes accessed | tf_op | source)
XLA Modules:
  0.0 1035.1 jit_solution(232667184782758755)
XLA Ops:
  24.8 85.7 %all-gather.11.cloned.1.call-done = bf16[2048,3072]{1,0:T(8,128)(2,1)} async-done(((bf16[64,3072]{1,0:T(8,128)(2,1)}), bf16[2048,3072]{1,0:T(8,128)(2,1)}) %all-gather.11.cloned.1.call-update) | async-done | bytes 12582928 | tf_op jit(solution)/shard_map/all_gather | solution.py:184
  122.1 93.5 %all-gather.9.cloned.1.call-done = bf16[2304,3072]{1,0:T(8,128)(2,1)} async-done(((bf16[72,3072]{1,0:T(8,128)(2,1)}), bf16[2304,3072]{1,0:T(8,128)(2,1)}) %all-gather.9.cloned.1.call-update) | async-done | bytes 14155792 | tf_op jit(solution)/shard_map/all_gather | solution.py:184
  230.6 9.9 reshape.718
  245.9 81.5 %all-gather.7.cloned.1.call-done = bf16[2560,3072]{1,0:T(8,128)(2,1)} async-done(((bf16[80,3072]{1,0:T(8,128)(2,1)}), bf16[2560,3072]{1,0:T(8,128)(2,1)}) %all-gather.7.cloned.1.call-update) | async-done | bytes 15728656 | tf_op jit(solution)/shard_map/all_gather | solution.py:184
  357.1 11.6 %shard_map.501 = (bf16[8,104,1024]{2,1,0:T(8,128)(2,1)S(1)}, bf16[8,40,1024]{2,1,0:T(8,128)(2,1)S(1)}) custom-call(bf16[8,104,3072]{2,1,0:T(8,128)(2,1)} %bitcast.304, bf16[8,40,3072]{2,1,0:T(8,128)(2,1)S(1)} %bitcast.281, f32[8,1,104]{2,1,0:T(1,128)S(1)} %compare_select_fusion.text_fill_ref.fill_ref, f32[8,1,40]{2,1,0:T(1,128)S(1)} %bitcast.297), custom_call_target="tpu_custom_call" | custom-call | flops 272629760 | bytes 9441792 | tf_op jit(solution)/shard_map/pallas_call | solution.py:167
  392.2 26.4 %shard_map.505 = bf16[8,40,3072]{2,1,0:T(8,128)(2,1)S(1)} custom-call(bf16[8,40,3072]{2,1,0:T(8,128)(2,1)S(1)} %bitcast.280, f32[8,1,40]{2,1,0:T(1,128)S(1)} %bitcast.299, bf16[8,40,1024]{2,1,0:T(8,128)(2,1)S(1)} %bitcast.296), custom_call_target="tpu_custom_call" | custom-call | flops 131072000 | bytes 4588800 | tf_op jit(solution)/shard_map/pallas_call | solution.py:167
  464.7 9.8 shard_map.502
  485.2 25.5 %shard_map.504 = bf16[8,104,2304]{2,1,0:T(8,128)(2,1)S(1)} custom-call(bf16[8,104,2304]{2,1,0:T(8,128)(2,1)} %bitcast.278, f32[8,1,104]{2,1,0:T(1,128)S(1)} %compare_select_fusion.text_fill_ref.fill_ref, bf16[8,104,768]{2,1,0:T(8,128)(2,1)S(1)} %bitcast.292), custom_call_target="tpu_custom_call" | custom-call | flops 1329070080 | bytes 8948992 | tf_op jit(solution)/shard_map/pallas_call | solution.py:167
  523.8 13.1 %fusion.111 = (bf16[3072]{0:T(1024)(128)(2,1)S(1)}, bf16[832,3072]{1,0:T(8,128)(2,1)}) fusion(bf16[3072,768]{1,0:T(8,128)(2,1)S(1)} %bitcast.351, f32[832,768]{1,0:T(8,128)S(1)} %subtract_multiply_fusion.1, f32[832,3072]{1,0:T(8,128)} %copy-done.77, f32[3072]{0:T(1024)S(1)} %reshape.749), kind=kOutput, calls=%fused_computation.315 | convolution fusion | flops 3982734336 | bytes 22628352 | tf_op jit(solution)/shard_map/dot_general | solution.py:38
  536.9 11.8 %convolution_convert_fusion.4 = bf16[3072,768]{1,0:T(8,128)(2,1)} fusion(f32[832,768]{1,0:T(8,128)S(1)} %subtract_multiply_fusion.1, f32[832,3072]{1,0:T(8,128)} %copy-done.77, f32[3072]{0:T(1024)S(1)} %reshape.749), kind=kOutput, calls=%fused_computation.42 | convolution fusion | flops 3954425856 | bytes 17510400 | tf_op jit(solution)/shard_map/dot_general | solution.py:42
  568.1 11.3 %maximum_maximum_fusion.1 = bf16[2,2,2,2,2,64,3072]{6,5,4,3,2,1,0:T(8,128)(2,1)} fusion(bf16[2,2,2,2,2,32,1024]{6,5,4,3,2,1,0:T(8,128)(2,1)} %bitcast.320, bf16[2,2,2,2,2,32,1024]{6,5,4,3,2,1,0:T(8,128)(2,1)} %bitcast.368, bf16[2,2,2,2,2,32,1024]{6,5,4,3,2,1,0:T(8,128)(2,1)} %bitcast.369, bf16[2,2,2,2,2,32,3072]{6,5,4,3,2,1,0:T(8,128)(2,1)} %bitcast.336), kind=kLoop, calls=%fused_computation.10 | loop fusion | flops 50331648 | bytes 25165824 | tf_op jit(solution)/shard_map/concatenate | solution.py:491
  579.4 11.2 %constant_dynamic-slice_fusion.1 = (bf16[2,1,2,2,2,64,3072]{6,5,4,3,2,1,0:T(8,128)(2,1)}, bf16[2,1,2,2,2,64,3072]{6,5,4,3,2,1,0:T(8,128)(2,1)}) fusion(bf16[2,2,2,2,2,64,3072]{6,5,4,3,2,1,0:T(8,128)(2,1)} %maximum_maximum_fusion.1, s32[]{:T(128)S(6)} %select_n.120, s32[]{:T(128)S(6)} %select_n.121), kind=kLoop, calls=%fused_computation.242 | loop fusion | bytes 25165832 | tf_op jit(solution)/shard_map/jit(dynamic_index_in_dim)/dynamic_slice | solution.py:216
  601.5 9.5 concatenate.159
  615.6 54.0 %shard_map.506 = (bf16[8,104,3072]{2,1,0:T(8,128)(2,1)}, bf16[8,40,3072]{2,1,0:T(8,128)(2,1)S(1)}) custom-call(bf16[8,104,3072]{2,1,0:T(8,128)(2,1)} %bitcast.305, bf16[8,40,3072]{2,1,0:T(8,128)(2,1)} %bitcast.282, f32[8,1,104]{2,1,0:T(1,128)S(1)} %compare_select_fusion.text_fill_ref.fill_ref, f32[8,1,40]{2,1,0:T(1,128)S(1)} %bitcast.300, ...), custom_call_target="tpu_custom_call" | custom-call | flops 681574400 | bytes 16519680 | tf_op jit(solution)/shard_map/pallas_call | solution.py:167
  669.7 9.3 bitcast_convert_fusion.1
  768.0 11.2 %fusion.1 = bf16[2,2,2,2,72,3072]{5,4,3,2,1,0:T(8,128)(2,1)} fusion(bf16[2,2,2,2,72,3072]{5,4,3,2,1,0:T(8,128)(2,1)} %collective-permute-done.7, bf16[2,2,2,2,2,72,3072]{6,5,4,3,2,1,0:T(8,128)(2,1)} %maximum_maximum_fusion, s32[]{:T(128)S(6)} %select_n.120), kind=kLoop, calls=%fused_computation.9 | loop fusion | flops 14155776 | bytes 21233668 | tf_op jit(solution)/shard_map/convert_element_type | solution.py:233
  787.9 14.1 %collective-permute-done.15 = bf16[2,2,2,64,1536]{4,3,2,1,0:T(8,128)(2,1)} collective-permute-done((bf16[2,2,2,64,1536]{4,3,2,1,0:T(8,128)(2,1)}, bf16[2,2,2,64,1536]{4,3,2,1,0:T(8,128)(2,1)}, u32[]{:S(2)}, u32[]{:S(2)}) %collective-permute-start.15) | collective-permute-done | bytes 1572896 | tf_op jit(solution)/shard_map/ppermute | solution.py:217
  810.4 12.5 %fusion = bf16[2,2,2,2,80,3072]{5,4,2,1,3,0:T(8,128)(2,1)} fusion(bf16[2,2,2,2,80,3072]{5,4,2,1,3,0:T(8,128)(2,1)} %collective-permute-done, bf16[2,1,2,2,2,80,3072]{6,5,4,3,2,1,0:T(8,128)(2,1)} %get-tuple-element.54), kind=kLoop, calls=%fused_computation.2 | loop fusion | flops 15728640 | bytes 23592960 | tf_op jit(solution)/shard_map/convert_element_type | solution.py:233
  828.4 30.2 %collective-permute-done.16 = bf16[2,2,64,1536]{3,2,1,0:T(8,128)(2,1)} collective-permute-done((bf16[2,2,64,1536]{3,2,1,0:T(8,128)(2,1)}, bf16[2,2,64,1536]{3,2,1,0:T(8,128)(2,1)}, u32[]{:S(2)}, u32[]{:S(2)}) %collective-permute-start.16) | collective-permute-done | bytes 786464 | tf_op jit(solution)/shard_map/ppermute | solution.py:217
  870.3 28.6 %collective-permute-done.19 = bf16[2,64,3072]{2,1,0:T(8,128)(2,1)S(1)} collective-permute-done((bf16[2,64,3072]{2,1,0:T(8,128)(2,1)S(1)}, bf16[2,64,3072]{2,1,0:T(8,128)(2,1)S(1)}, u32[]{:S(2)}, u32[]{:S(2)}) %collective-permute-start.19) | collective-permute-done | bytes 786464 | tf_op jit(solution)/shard_map/ppermute | solution.py:217
  899.3 22.1 %collective-permute-done.9 = bf16[2,2,72,1536]{3,2,1,0:T(8,128)(2,1)S(1)} collective-permute-done((bf16[2,2,72,1536]{3,2,1,0:T(8,128)(2,1)S(1)}, bf16[2,2,72,1536]{3,2,1,0:T(8,128)(2,1)S(1)}, u32[]{:S(2)}, u32[]{:S(2)}) %collective-permute-start.9) | collective-permute-done | bytes 884768 | tf_op jit(solution)/shard_map/ppermute | solution.py:217
  928.7 17.1 %collective-permute-done.2 = bf16[2,2,80,1536]{3,2,1,0:T(8,128)(2,1)S(1)} collective-permute-done((bf16[2,2,80,1536]{3,2,1,0:T(8,128)(2,1)S(1)}, bf16[2,2,80,1536]{3,2,1,0:T(8,128)(2,1)S(1)}, u32[]{:S(2)}, u32[]{:S(2)}) %collective-permute-start.2) | collective-permute-done | bytes 983072 | tf_op jit(solution)/shard_map/ppermute | solution.py:217
  949.9 32.8 %collective-permute-done.12 = bf16[2,72,3072]{2,1,0:T(8,128)(2,1)S(1)} collective-permute-done((bf16[2,72,3072]{2,1,0:T(8,128)(2,1)S(1)}, bf16[2,72,3072]{2,1,0:T(8,128)(2,1)S(1)}, u32[]{:S(2)}, u32[]{:S(2)}) %collective-permute-start.12) | collective-permute-done | bytes 884768 | tf_op jit(solution)/shard_map/ppermute | solution.py:217
  983.0 20.7 %collective-permute-done.5 = bf16[2,80,3072]{2,1,0:T(8,128)(2,1)S(1)} collective-permute-done((bf16[2,80,3072]{2,1,0:T(8,128)(2,1)S(1)}, bf16[2,80,3072]{2,1,0:T(8,128)(2,1)S(1)}, u32[]{:S(2)}, u32[]{:S(2)}) %collective-permute-start.5) | collective-permute-done | bytes 983072 | tf_op jit(solution)/shard_map/ppermute | solution.py:217
  (456 shorter events, 365.8 us)
Async XLA Ops:
  7.4 103.1 %all-gather.11.cloned.1.call-start = ((), (), s32[]{:S(2)}) async-start(), calls=%async_computation.2 | async-start | bytes 12976128 | tf_op jit(solution)/shard_map/all_gather | solution.py:184
  9.4 206.2 %all-gather.9.cloned.1.call-start = ((), (), s32[]{:S(2)}) async-start(), calls=%async_computation.1 | async-start | bytes 14598144 | tf_op jit(solution)/shard_map/all_gather | solution.py:184
  12.3 315.1 %all-gather.7.cloned.1.call-start = ((), (), s32[]{:S(2)}) async-start(), calls=%async_computation | async-start | bytes 16220160 | tf_op jit(solution)/shard_map/all_gather | solution.py:184
  596.8 157.9 %collective-permute-start.14 = (bf16[2,2,2,2,64,3072]{5,4,2,1,3,0:T(8,128)(2,1)}, bf16[2,2,2,2,64,3072]{5,4,2,1,3,0:T(8,128)(2,1)}, u32[]{:S(2)}, u32[]{:S(2)}) collective-permute-start(bf16[2,2,2,2,64,3072]{5,4,2,1,3,0:T(8,128)(2,1)} %bitcast.267), channel_id=1, source_target_pairs={{0,8},{8,0},{16,24},{24,16},{1,9},{9,1},{17,25},{25,17},{2,10},{10... | collective-permute-start | bytes 18874376 | tf_op jit(solution)/shard_map/ppermute | solution.py:217
  692.3 75.7 %collective-permute-start.7 = (bf16[2,2,2,2,72,3072]{5,4,3,2,1,0:T(8,128)(2,1)}, bf16[2,2,2,2,72,3072]{5,4,3,2,1,0:T(8,128)(2,1)}, u32[]{:S(2)}, u32[]{:S(2)}) collective-permute-start(bf16[2,2,2,2,72,3072]{5,4,3,2,1,0:T(8,128)(2,1)} %dynamic-slice_bitcast_fusion), channel_id=1, source_target_pairs={{0,8},{8,0},{16,24},{24,16},{1,9},{9,1},{17,25},{25,17},{2,10},{10... | collective-permute-start | bytes 21233672 | tf_op jit(solution)/shard_map/ppermute | solution.py:217
  739.1 71.3 %collective-permute-start = (bf16[2,2,2,2,80,3072]{5,4,2,1,3,0:T(8,128)(2,1)}, bf16[2,2,2,2,80,3072]{5,4,2,1,3,0:T(8,128)(2,1)}, u32[]{:S(2)}, u32[]{:S(2)}) collective-permute-start(bf16[2,2,2,2,80,3072]{5,4,2,1,3,0:T(8,128)(2,1)} %bitcast.326), channel_id=1, source_target_pairs={{0,8},{8,0},{16,24},{24,16},{1,9},{9,1},{17,25},{25,17},{2,10},{10... | collective-permute-start | bytes 23592968 | tf_op jit(solution)/shard_map/ppermute | solution.py:217
  764.4 37.5 %collective-permute-start.15 = (bf16[2,2,2,64,1536]{4,3,2,1,0:T(8,128)(2,1)}, bf16[2,2,2,64,1536]{4,3,2,1,0:T(8,128)(2,1)}, u32[]{:S(2)}, u32[]{:S(2)}) collective-permute-start(bf16[2,2,2,64,1536]{4,3,2,1,0:T(8,128)(2,1)} %dynamic-slice_bitcast_fusion.6), channel_id=1, source_target_pairs={{0,1},{1,0},{2,3},{3,2},{4,5},{5,4},{6,7},{7,6},{8,9},{9,8},{10,11... | collective-permute-start | bytes 4718600 | tf_op jit(solution)/shard_map/ppermute | solution.py:217
  767.2 39.4 %collective-permute-start.17 = (bf16[2,2,2,64,1536]{4,3,1,0,2:T(8,128)(2,1)}, bf16[2,2,2,64,1536]{4,3,1,0,2:T(8,128)(2,1)}, u32[]{:S(2)}, u32[]{:S(2)}) collective-permute-start(bf16[2,2,2,64,1536]{4,3,1,0,2:T(8,128)(2,1)} %dynamic-slice_bitcast_fusion.5), channel_id=1, source_target_pairs={{0,16},{8,24},{16,0},{24,8},{1,17},{9,25},{17,1},{25,9},{2,18},{10... | collective-permute-start | bytes 4718600 | tf_op jit(solution)/shard_map/ppermute | solution.py:217
  784.6 79.6 %collective-permute-start.8 = (bf16[2,2,2,72,1536]{4,3,2,1,0:T(8,128)(2,1)}, bf16[2,2,2,72,1536]{4,3,2,1,0:T(8,128)(2,1)}, u32[]{:S(2)}, u32[]{:S(2)}) collective-permute-start(bf16[2,2,2,72,1536]{4,3,2,1,0:T(8,128)(2,1)} %dynamic-slice_bitcast_fusion.4), channel_id=1, source_target_pairs={{0,1},{1,0},{2,3},{3,2},{4,5},{5,4},{6,7},{7,6},{8,9},{9,8},{10,11... | collective-permute-start | bytes 5308424 | tf_op jit(solution)/shard_map/ppermute | solution.py:217
  787.2 80.0 %collective-permute-start.10 = (bf16[2,2,2,72,1536]{4,3,2,1,0:T(8,128)(2,1)}, bf16[2,2,2,72,1536]{4,3,2,1,0:T(8,128)(2,1)}, u32[]{:S(2)}, u32[]{:S(2)}) collective-permute-start(bf16[2,2,2,72,1536]{4,3,2,1,0:T(8,128)(2,1)} %dynamic-slice_bitcast_fusion.3), channel_id=1, source_target_pairs={{0,16},{8,24},{16,0},{24,8},{1,17},{9,25},{17,1},{25,9},{2,18},{10... | collective-permute-start | bytes 5308424 | tf_op jit(solution)/shard_map/ppermute | solution.py:217
  805.1 53.5 %collective-permute-start.16 = (bf16[2,2,64,1536]{3,2,1,0:T(8,128)(2,1)}, bf16[2,2,64,1536]{3,2,1,0:T(8,128)(2,1)}, u32[]{:S(2)}, u32[]{:S(2)}) collective-permute-start(bf16[2,2,64,1536]{3,2,1,0:T(8,128)(2,1)} %dynamic-slice_bitcast_fusion.12), channel_id=1, source_target_pairs={{0,16},{8,24},{16,0},{24,8},{1,17},{9,25},{17,1},{25,9},{2,18},{10... | collective-permute-start | bytes 2359304 | tf_op jit(solution)/shard_map/ppermute | solution.py:217
  809.8 51.2 %collective-permute-start.18 = (bf16[2,2,64,1536]{3,2,1,0:T(8,128)(2,1)}, bf16[2,2,64,1536]{3,2,1,0:T(8,128)(2,1)}, u32[]{:S(2)}, u32[]{:S(2)}) collective-permute-start(bf16[2,2,64,1536]{3,2,1,0:T(8,128)(2,1)} %dynamic-slice_bitcast_fusion.11), channel_id=1, source_target_pairs={{0,1},{1,0},{2,3},{3,2},{4,5},{5,4},{6,7},{7,6},{8,9},{9,8},{10,11... | collective-permute-start | bytes 2359304 | tf_op jit(solution)/shard_map/ppermute | solution.py:217
  826.7 96.8 %collective-permute-start.1 = (bf16[2,2,2,80,1536]{4,3,2,1,0:T(8,128)(2,1)S(1)}, bf16[2,2,2,80,1536]{4,3,2,1,0:T(8,128)(2,1)S(1)}, u32[]{:S(2)}, u32[]{:S(2)}) collective-permute-start(bf16[2,2,2,80,1536]{4,3,2,1,0:T(8,128)(2,1)S(1)} %dynamic-slice_bitcast_fusion.2), channel_id=1, source_target_pairs={{0,1},{1,0},{2,3},{3,2},{4,5},{5,4},{6,7},{7,6},{8,9},{9,8},{10,11... | collective-permute-start | bytes 5898248 | tf_op jit(solution)/shard_map/ppermute | solution.py:217
  858.5 67.1 %collective-permute-start.3 = (bf16[2,2,2,80,1536]{4,3,1,0,2:T(8,128)(2,1)S(1)}, bf16[2,2,2,80,1536]{4,3,1,0,2:T(8,128)(2,1)S(1)}, u32[]{:S(2)}, u32[]{:S(2)}) collective-permute-start(bf16[2,2,2,80,1536]{4,3,1,0,2:T(8,128)(2,1)S(1)} %dynamic-slice_bitcast_fusion.1), channel_id=1, source_target_pairs={{0,16},{8,24},{16,0},{24,8},{1,17},{9,25},{17,1},{25,9},{2,18},{10... | collective-permute-start | bytes 5898248 | tf_op jit(solution)/shard_map/ppermute | solution.py:217
  862.6 36.3 %collective-permute-start.19 = (bf16[2,64,3072]{2,1,0:T(8,128)(2,1)S(1)}, bf16[2,64,3072]{2,1,0:T(8,128)(2,1)S(1)}, u32[]{:S(2)}, u32[]{:S(2)}) collective-permute-start(bf16[2,64,3072]{2,1,0:T(8,128)(2,1)S(1)} %fusion.63), channel_id=1, source_target_pairs={{0,4},{1,5},{2,6},{3,7},{4,0},{5,1},{6,2},{7,3},{8,12},{9,13},{10,... | collective-permute-start | bytes 2359304 | tf_op jit(solution)/shard_map/ppermute | solution.py:217
  866.2 55.1 %collective-permute-start.9 = (bf16[2,2,72,1536]{3,2,1,0:T(8,128)(2,1)S(1)}, bf16[2,2,72,1536]{3,2,1,0:T(8,128)(2,1)S(1)}, u32[]{:S(2)}, u32[]{:S(2)}) collective-permute-start(bf16[2,2,72,1536]{3,2,1,0:T(8,128)(2,1)S(1)} %dynamic-slice_bitcast_fusion.10), channel_id=1, source_target_pairs={{0,16},{8,24},{16,0},{24,8},{1,17},{9,25},{17,1},{25,9},{2,18},{10... | collective-permute-start | bytes 2654216 | tf_op jit(solution)/shard_map/ppermute | solution.py:217
  869.2 52.4 %collective-permute-start.11 = (bf16[2,2,72,1536]{3,2,1,0:T(8,128)(2,1)S(1)}, bf16[2,2,72,1536]{3,2,1,0:T(8,128)(2,1)S(1)}, u32[]{:S(2)}, u32[]{:S(2)}) collective-permute-start(bf16[2,2,72,1536]{3,2,1,0:T(8,128)(2,1)S(1)} %dynamic-slice_bitcast_fusion.9), channel_id=1, source_target_pairs={{0,1},{1,0},{2,3},{3,2},{4,5},{5,4},{6,7},{7,6},{8,9},{9,8},{10,11... | collective-permute-start | bytes 2654216 | tf_op jit(solution)/shard_map/ppermute | solution.py:217
  899.2 27.9 %collective-permute-start.20 = (bf16[64,3072]{1,0:T(8,128)(2,1)S(1)}, bf16[64,3072]{1,0:T(8,128)(2,1)S(1)}, u32[]{:S(2)}, u32[]{:S(2)}) collective-permute-start(bf16[64,3072]{1,0:T(8,128)(2,1)S(1)} %dynamic-slice_bitcast_fusion.15), channel_id=1, source_target_pairs={{0,2},{1,3},{2,0},{3,1},{4,6},{5,7},{6,4},{7,5},{8,10},{9,11},{10,... | collective-permute-start | bytes 1179656 | tf_op jit(solution)/shard_map/ppermute | solution.py:217
  921.9 60.7 %collective-permute-start.12 = (bf16[2,72,3072]{2,1,0:T(8,128)(2,1)S(1)}, bf16[2,72,3072]{2,1,0:T(8,128)(2,1)S(1)}, u32[]{:S(2)}, u32[]{:S(2)}) collective-permute-start(bf16[2,72,3072]{2,1,0:T(8,128)(2,1)S(1)} %fusion.59), channel_id=1, source_target_pairs={{0,4},{1,5},{2,6},{3,7},{4,0},{5,1},{6,2},{7,3},{8,12},{9,13},{10,... | collective-permute-start | bytes 2654216 | tf_op jit(solution)/shard_map/ppermute | solution.py:217
  924.2 21.6 %collective-permute-start.2 = (bf16[2,2,80,1536]{3,2,1,0:T(8,128)(2,1)S(1)}, bf16[2,2,80,1536]{3,2,1,0:T(8,128)(2,1)S(1)}, u32[]{:S(2)}, u32[]{:S(2)}) collective-permute-start(bf16[2,2,80,1536]{3,2,1,0:T(8,128)(2,1)S(1)} %dynamic-slice_bitcast_fusion.8), channel_id=1, source_target_pairs={{0,16},{8,24},{16,0},{24,8},{1,17},{9,25},{17,1},{25,9},{2,18},{10... | collective-permute-start | bytes 2949128 | tf_op jit(solution)/shard_map/ppermute | solution.py:217
  926.3 21.7 %collective-permute-start.4 = (bf16[2,2,80,1536]{3,2,1,0:T(8,128)(2,1)S(1)}, bf16[2,2,80,1536]{3,2,1,0:T(8,128)(2,1)S(1)}, u32[]{:S(2)}, u32[]{:S(2)}) collective-permute-start(bf16[2,2,80,1536]{3,2,1,0:T(8,128)(2,1)S(1)} %dynamic-slice_bitcast_fusion.7), channel_id=1, source_target_pairs={{0,1},{1,0},{2,3},{3,2},{4,5},{5,4},{6,7},{7,6},{8,9},{9,8},{10,11... | collective-permute-start | bytes 2949128 | tf_op jit(solution)/shard_map/ppermute | solution.py:217
  948.3 55.4 %collective-permute-start.5 = (bf16[2,80,3072]{2,1,0:T(8,128)(2,1)S(1)}, bf16[2,80,3072]{2,1,0:T(8,128)(2,1)S(1)}, u32[]{:S(2)}, u32[]{:S(2)}) collective-permute-start(bf16[2,80,3072]{2,1,0:T(8,128)(2,1)S(1)} %fusion.52), channel_id=1, source_target_pairs={{0,4},{1,5},{2,6},{3,7},{4,0},{5,1},{6,2},{7,3},{8,12},{9,13},{10,... | collective-permute-start | bytes 2949128 | tf_op jit(solution)/shard_map/ppermute | solution.py:217
  983.0 30.2 %collective-permute-start.13 = (bf16[72,3072]{1,0:T(8,128)(2,1)S(1)}, bf16[72,3072]{1,0:T(8,128)(2,1)S(1)}, u32[]{:S(2)}, u32[]{:S(2)}) collective-permute-start(bf16[72,3072]{1,0:T(8,128)(2,1)S(1)} %dynamic-slice_bitcast_fusion.14), channel_id=1, source_target_pairs={{0,2},{1,3},{2,0},{3,1},{4,6},{5,7},{6,4},{7,5},{8,10},{9,11},{10,... | collective-permute-start | bytes 1327112 | tf_op jit(solution)/shard_map/ppermute | solution.py:217
  1004.0 19.6 %collective-permute-start.6 = (bf16[80,3072]{1,0:T(8,128)(2,1)S(1)}, bf16[80,3072]{1,0:T(8,128)(2,1)S(1)}, u32[]{:S(2)}, u32[]{:S(2)}) collective-permute-start(bf16[80,3072]{1,0:T(8,128)(2,1)S(1)} %dynamic-slice_bitcast_fusion.13), channel_id=1, source_target_pairs={{0,2},{1,3},{2,0},{3,1},{4,6},{5,7},{6,4},{7,5},{8,10},{9,11},{10,... | collective-permute-start | bytes 1474568 | tf_op jit(solution)/shard_map/ppermute | solution.py:217
  (98 other events, 1239.0 us)
Sparse Core Ops, SparseCore 0:
  11.8 98.6 all-gather.10
  114.1 101.4 all-gather.8
  219.1 108.2 all-gather.6
where the time goes:
time: 1040 us
  waiting for transfers between devices  445 us (43%)
  local copies, waits for them, and re-layouts  174 us (17%)
  matrix products  150 us (14%)
  Pallas kernels  134 us (13%)
  other arithmetic  97.4 us (9%)
  starting transfers between devices  18.9 us (2%)
  between operations  15.8 us (2%)
    all_gather x3, waiting for transfers between devices, gather(): return lax.all_gather(packed, AXES, axis=0, tiled=False)  261 us
    ppermute x21, waiting for transfers between devices, halve(): got = lax.ppermute(away, axis, [(at, at ^ 1 << bit) for at in range(count)])  184 us
    pallas_call x6, Pallas kernels, per_pair(): pl.pallas_call(kernel, grid=(pairs,), in_specs=[spec(*array.shape[1:]) fo...  134 us
    dot_general x12, matrix products, weight_grad(): lax.dot_general(left, right, (((0,), (0,)), ((), ())), preferred_element_...  60.6 us
    dot_general x12, matrix products, project_back(): lax.dot_general(left, right, (((1,), (1,)), ((), ())), preferred_element_...  49.6 us
    dot_general x12, matrix products, project(): return jnp.dot(left, right, preferred_element_type=F32)  39.6 us
    unnamed x206, local copies, waits for them, and re-layouts  31.4 us
    convert_element_type x3, other arithmetic, sum_to_owners(): total = total.astype(BF16)  31.2 us
  transfers between devices with their start and end apart: 24, of which 13 were waited for; matrix products, arithmetic and copies ran while one was open for 22% of the time, Pallas kernels for 5%

commit v1 on v0

v1 whole, which is shorter than its diff:
```python
import functools
import math

import jax
import jax.numpy as jnp
from jax import lax
from jax.experimental import pallas as pl
from jax.experimental.pallas import tpu as pltpu
from jax.sharding import PartitionSpec as P

HEADS = 8
TEXT_HEADS = 12
IMAGE_HEADS = 8
EPSILON = 1e-05
MASKED = -1000000000.0
PADDED = -2000000000.0
LANES = 128
AXES = ("gx", "gy")
F32 = jnp.float32
BF16 = jnp.bfloat16
VMEM_BYTES = 48 * 1024 * 1024
VECTOR_NAMES = (
    "text_gain_cross",
    "image_gain_cross",
    "text_bias",
    "text_gain_ffn",
    "image_bias",
    "image_gain_ffn",
    "text_gain_self",
    "image_gain_self",
)


def project(left, right):
    return jnp.dot(left, right, preferred_element_type=F32)


def project_back(left, right):
    return lax.dot_general(left, right, (((1,), (1,)), ((), ())), preferred_element_type=F32)


def weight_grad(left, right):
    return lax.dot_general(left, right, (((0,), (0,)), ((), ())), preferred_element_type=F32)


def round_up(size, step):
    return -(-size // step) * step


def stack_halves(rows):
    wide = rows.astype(F32)
    first = lax.broadcasted_iota(jnp.int32, wide.shape, 1) < LANES // 2
    zero = jnp.zeros_like(wide)
    return jnp.concatenate([jnp.where(first, wide, zero), jnp.where(first, zero, wide)], 0).astype(BF16)


def join_halves(rows):
    count = rows.shape[0] // 2
    first = lax.broadcasted_iota(jnp.int32, (count, LANES), 1) < LANES // 2
    return jnp.where(first, rows[:count], rows[count:])


def probabilities(keys, queries, fill, scale):
    scores = project_back(keys, queries) * scale
    scores = jnp.where(fill < 0.0, fill, scores)
    powers = jnp.exp(scores - jnp.max(scores, 0, keepdims=True))
    return powers * (1.0 / jnp.sum(powers, 0, keepdims=True))


def head_blocks(queries_ref, size):
    count, _, width = queries_ref.shape
    return [(pair, slice(at, at + LANES)) for pair in range(count) for at in range(0, width, LANES)], size < LANES


def attend_kernel(size, queries_ref, keys_ref, values_ref, fill_ref, mixed_ref):
    scale = 1.0 / math.sqrt(size)
    blocks, split = head_blocks(queries_ref, size)
    queries = [stack_halves(queries_ref[p, :, b]) if split else queries_ref[p, :, b] for p, b in blocks]
    probs = [
        probabilities(keys_ref[p, :, b], query, fill_ref[p][:, :1], scale).astype(BF16)
        for (p, b), query in zip(blocks, queries)
    ]
    mixed = [weight_grad(prob, values_ref[p, :, b]) for (p, b), prob in zip(blocks, probs)]
    for (p, b), rows in zip(blocks, mixed):
        mixed_ref[p, :, b] = (join_halves(rows) if split else rows).astype(BF16)


def attend_back_kernel(
    size, queries_ref, keys_ref, values_ref, fill_ref, d_mixed_ref, d_queries_ref, d_keys_ref, d_values_ref
):
    scale = 1.0 / math.sqrt(size)
    blocks, split = head_blocks(queries_ref, size)
    fills = [fill_ref[p][:, :1] for p, _ in blocks]
    queries = [stack_halves(queries_ref[p, :, b]) if split else queries_ref[p, :, b] for p, b in blocks]
    grads = [stack_halves(d_mixed_ref[p, :, b]) if split else d_mixed_ref[p, :, b] for p, b in blocks]
    probs = [
        probabilities(keys_ref[p, :, b], query, fill, scale) for (p, b), query, fill in zip(blocks, queries, fills)
    ]
    d_probs = [project_back(values_ref[p, :, b], grad) for (p, b), grad in zip(blocks, grads)]
    for (p, b), prob, grad in zip(blocks, probs, grads):
        d_values_ref[p, :, b] = project(prob.astype(BF16), grad).astype(BF16)
    d_scores = [
        prob * (d_prob - jnp.sum(prob * d_prob, 0, keepdims=True)) for prob, d_prob in zip(probs, d_probs)
    ]
    d_scores = [jnp.where(fill < 0.0, 0.0, one).astype(BF16) for fill, one in zip(fills, d_scores)]
    for (p, b), one, query in zip(blocks, d_scores, queries):
        d_keys_ref[p, :, b] = (project(one, query) * scale).astype(BF16)
    for (p, b), one in zip(blocks, d_scores):
        rows = weight_grad(one, keys_ref[p, :, b]) * scale
        d_queries_ref[p, :, b] = (join_halves(rows) if split else rows).astype(BF16)


def attention_call(kernel, together, inputs, outputs, flops):
    pairs = inputs[0][0].shape[0]
    together = math.gcd(pairs, together)

    def spec(rows, width, column):
        return pl.BlockSpec((together, rows, width), lambda step: (step, 0, column))

    moved = sum(pairs * array.shape[1] * width * array.dtype.itemsize for array, width, _ in inputs)
    moved += sum(pairs * rows * width * 2 for rows, width in outputs)
    return pl.pallas_call(
        kernel,
        grid=(pairs // together,),
        in_specs=[spec(array.shape[1], width, column) for array, width, column in inputs],
        out_specs=[spec(rows, width, 0) for rows, width in outputs],
        out_shape=[jax.ShapeDtypeStruct((pairs, rows, width), BF16) for rows, width in outputs],
        compiler_params=pltpu.CompilerParams(vmem_limit_bytes=VMEM_BYTES),
        cost_estimate=pl.CostEstimate(flops=flops, bytes_accessed=moved, transcendentals=0),
    )(*[array for array, _, _ in inputs])


def attend(queries, keys, values, fill, width, heads):
    pairs, count = queries[0].shape[:2]
    inputs = [(array, width, column) for array, column in (queries, keys, values)] + [(fill, LANES, 0)]
    flops = 4 * pairs * count * keys[0].shape[1] * max(width, heads * LANES)
    kernel = functools.partial(attend_kernel, width // heads)
    return attention_call(kernel, 4, inputs, [(count, width)], flops)[0]


def attend_back(queries, keys, values, fill, d_mixed, width, heads):
    pairs, count = queries[0].shape[:2]
    inputs = [(array, width, column) for array, column in (queries, keys, values)]
    inputs += [(fill, LANES, 0), (d_mixed, width, 0)]
    keyed = keys[0].shape[1]
    flops = 10 * pairs * count * keyed * max(width, heads * LANES)
    kernel = functools.partial(attend_back_kernel, width // heads)
    return attention_call(kernel, 2, inputs, [(count, width), (keyed, width), (keyed, width)], flops)


def tie(*values):
    return lax.optimization_barrier(values)


def gather(packed):
    return lax.all_gather(packed, AXES, axis=0, tiled=False)


def whole(block):
    return block.reshape(-1, block.shape[-1])


def owned_rows(matrix, devices):
    return matrix.reshape(devices, matrix.shape[0] // devices, matrix.shape[1])


def mesh_bits(sizes):
    bits = []
    for axis in AXES:
        bits += [(axis, bit) for bit in reversed(range(sizes[axis].bit_length() - 1))]
    return bits


class OwnerSum:
    def __init__(self, packed, sizes):
        bits = mesh_bits(sizes)
        low = (sizes["gy"].bit_length() - 1) // 2
        core = [("gx", 0)] if sizes["gx"] > 1 else []
        rows = [one for one in bits if one[0] == "gx" and one not in core]
        columns = [one for one in bits if one[0] == "gy" and one[1] < low]
        rest = [one for one in bits if one[0] == "gy" and one[1] >= low]
        self.width = packed.shape[-1]
        self.parts = [(packed.reshape((2,) * len(bits) + packed.shape[1:]), bits)]
        self.plan = [[which] for which in core]
        self.plan += [list(pair) for pair in zip(columns + rows, rows + columns)]
        self.plan += [[which] for which in rest]
        self.flying = None

    def advance(self, *others):
        if self.flying is not None:
            last = not self.plan
            self.parts = [
                ((kept.astype(F32) + got.astype(F32)).astype(F32 if last else BF16), bits)
                for kept, got, bits in self.flying
            ]
            self.flying = None
        if self.plan:
            step = self.plan.pop(0)
            if len(step) == 2 and len(self.parts) == 1:
                total, bits = self.parts[0]
                self.parts = [(total[..., : self.width // 2], bits), (total[..., self.width // 2 :], bits)]
            if len(step) == 1 and len(self.parts) == 2:
                self.parts = [(jnp.concatenate([self.parts[0][0], self.parts[1][0]], -1), self.parts[0][1])]
            sends = []
            for (total, bits), (axis, bit) in zip(self.parts, step):
                place = bits.index((axis, bit))
                own = (lax.axis_index(axis) >> bit) & 1
                away = lax.dynamic_index_in_dim(total, 1 - own, place, keepdims=False)
                kept = lax.dynamic_index_in_dim(total, own, place, keepdims=False)
                sends.append((away, kept, axis, bit, [one for one in bits if one != (axis, bit)]))
            held = tie(*[one[0] for one in sends], *others)
            others = held[len(sends) :]
            self.flying = []
            for away, (_, kept, axis, bit, left) in zip(held, sends):
                count = lax.axis_size(axis)
                got = lax.ppermute(away, axis, [(at, at ^ (1 << bit)) for at in range(count)])
                self.flying.append((kept, got, left))
        return others[0] if len(others) == 1 else others

    def result(self):
        while self.plan or self.flying is not None:
            self.advance()
        return self.parts[0][0].astype(F32)


def normed_rows(values_in):
    centred = values_in - jnp.mean(values_in, -1, keepdims=True)
    rate = lax.rsqrt(jnp.mean(centred * centred, -1, keepdims=True) + EPSILON)
    return centred * rate, rate


def normed_back(unit, rate, gain, d_out):
    d_unit = d_out * gain
    mean_unit = jnp.mean(d_unit, -1, keepdims=True)
    mean_cross = jnp.mean(d_unit * unit, -1, keepdims=True)
    return rate * (d_unit - mean_unit - unit * mean_cross), jnp.sum(d_out * unit, 0)


GELU_RATE = math.sqrt(2.0 / math.pi)
GELU_CUBE = 0.044715


def gelu(values_in):
    inner = jnp.tanh(GELU_RATE * (values_in + GELU_CUBE * values_in * values_in * values_in))
    return 0.5 * values_in * (1.0 + inner)


def gelu_slope(values_in):
    square = values_in * values_in
    inner = jnp.tanh(GELU_RATE * values_in * (1.0 + GELU_CUBE * square))
    return 0.5 * (1.0 + inner) + 0.5 * values_in * (1.0 - inner * inner) * GELU_RATE * (1.0 + 3.0 * GELU_CUBE * square)


def per_device(sizes, *given):
    (
        text_tokens,
        image_regions,
        caption_lengths,
        region_mask,
        text_cotangent,
        image_cotangent,
        text_query,
        image_key,
        image_value,
        text_merge,
        text_gain_cross,
        image_query,
        text_key,
        text_value,
        image_merge,
        image_gain_cross,
        text_up,
        text_bias,
        text_down,
        text_gain_ffn,
        image_up,
        image_bias,
        image_down,
        image_gain_ffn,
        text_self,
        text_mix,
        text_gain_self,
        image_self,
        image_mix,
        image_gain_self,
    ) = given
    devices = sizes["gx"] * sizes["gy"]
    pairs, length, text_width = text_tokens.shape
    regions, image_width = image_regions.shape[1:]
    inner = text_query.shape[1]

    vectors = (
        text_gain_cross,
        image_gain_cross,
        text_bias,
        text_gain_ffn,
        image_bias,
        image_gain_ffn,
        text_gain_self,
        image_gain_self,
    )
    vector = jnp.concatenate(vectors)
    vector_rows = 8
    vector_block = jnp.pad(vector[None, :], ((0, vector_rows - 1), (0, inner - vector.shape[0])))
    cross_pieces = [text_query, text_key, text_value, image_query, image_key, image_value, image_merge]
    packed_cross = jnp.concatenate(
        cross_pieces + [jnp.pad(text_merge, ((0, 0), (0, inner - text_width))), vector_block], 0
    )
    text_pieces = jnp.split(text_up, text_up.shape[1] // text_width, 1) + [text_down]
    text_pieces += jnp.split(text_self, 3, 1) + [text_mix]
    packed_text = jnp.concatenate(text_pieces, 0)
    image_pieces = [image_up, image_down] + jnp.split(image_self, 3, 1) + [image_mix]
    packed_image = jnp.concatenate(image_pieces, 0)

    def starts(pieces):
        marks = [0]
        for piece in pieces:
            marks.append(marks[-1] + piece.shape[0])
        return list(zip(marks[:-1], marks[1:]))

    cross_at = starts(cross_pieces + [text_merge, vector_block])
    text_at, image_at = starts(text_pieces), starts(image_pieces)
    all_cross = gather(packed_cross)
    all_cross, packed_text = tie(all_cross, packed_text)
    all_text = gather(packed_text)
    all_text, packed_image = tie(all_text, packed_image)
    all_image = gather(packed_image)

    def taken(block, at):
        return whole(block[:, at[0] : at[1]])

    def side_by_side(block, spans):
        return jnp.concatenate([taken(block, at) for at in spans], 1)

    weight_text = side_by_side(all_cross, cross_at[:3])
    weight_image = side_by_side(all_cross, cross_at[3:6])
    full_image_merge = taken(all_cross, cross_at[6])
    full_text_merge = taken(all_cross, cross_at[7])[:, :text_width]
    all_vectors = all_cross[:, cross_at[8][0]]
    full = {}
    at = 0
    for name, piece in zip(VECTOR_NAMES, vectors):
        full[name] = all_vectors[:, at : at + piece.shape[0]].reshape(-1).astype(F32)
        at += piece.shape[0]
    full_text_up = side_by_side(all_text, text_at[:-5])
    full_text_down = taken(all_text, text_at[-5])
    full_text_self = side_by_side(all_text, text_at[-4:-1])
    full_text_mix = taken(all_text, text_at[-1])
    full_image_up = taken(all_image, image_at[0])
    full_image_down = taken(all_image, image_at[1])
    full_image_self = side_by_side(all_image, image_at[2:5])
    full_image_mix = taken(all_image, image_at[5])

    text_slots, image_slots = round_up(length, 8), round_up(regions, 8)

    def padded(array, slots):
        array = jnp.pad(array, ((0, 0), (0, slots - array.shape[1]), (0, 0)))
        return array.reshape(pairs * slots, array.shape[2])

    def rows_of(array):
        return array.reshape(-1, array.shape[-1])

    def pairs_of(array):
        return array.reshape(pairs, array.shape[0] // pairs, array.shape[1])

    def fill_of(live, count):
        slots = live.shape[1]
        fill = jnp.where(live, 0.0, jnp.where(jnp.arange(slots)[None, :] < count, MASKED, PADDED))
        return jnp.broadcast_to(fill[:, :, None], (pairs, slots, LANES)).astype(F32)

    text_rows, image_rows = padded(text_tokens, text_slots), padded(image_regions, image_slots)
    d_text_out = padded(text_cotangent, text_slots)
    d_image_out = padded(image_cotangent, image_slots)
    text_live = jnp.arange(text_slots)[None, :] < caption_lengths[:, None]
    image_live = jnp.pad(region_mask, ((0, 0), (0, image_slots - regions))) > 0
    text_fill, image_fill = fill_of(text_live, length), fill_of(image_live, regions)
    text_keep = text_live.astype(F32).reshape(-1, 1)
    image_keep = image_live.astype(F32).reshape(-1, 1)

    triple_text = pairs_of(project(text_rows, weight_text).astype(BF16))
    triple_image = pairs_of(project(image_rows, weight_image).astype(BF16))
    cross_text = rows_of(
        attend((triple_text, 0), (triple_image, 1), (triple_image, 2), image_fill, inner, HEADS)
    )
    cross_image = rows_of(attend((triple_image, 0), (triple_text, 1), (triple_text, 2), text_fill, inner, HEADS))
    unit_text_1, rate_text_1 = normed_rows(text_rows.astype(F32) + project(cross_text, full_text_merge))
    unit_image_1, rate_image_1 = normed_rows(image_rows.astype(F32) + project(cross_image, full_image_merge))

    def forward(unit_1, gain_1, up, bias, down, gain_2, joint, mix, gain_3, fill, keep, heads):
        width = unit_1.shape[1]
        first = unit_1 * gain_1
        first_low = first.astype(BF16)
        hidden = project(first_low, up) + bias
        active = gelu(hidden).astype(BF16)
        slope = gelu_slope(hidden).astype(BF16)
        unit_2, rate_2 = normed_rows(first + project(active, down))
        second = unit_2 * gain_2
        second_low = second.astype(BF16)
        triple = pairs_of(project(second_low, joint).astype(BF16))
        mixed = rows_of(attend((triple, 0), (triple, 1), (triple, 2), fill, width, heads))
        unit_3, rate_3 = normed_rows(second + project(mixed, mix))
        out = (unit_3 * gain_3 * keep).astype(BF16)
        return out, (first_low, active, slope, unit_2, rate_2, second_low, triple, mixed, unit_3, rate_3)

    def self_backward(saved, gain_2, joint, mix, gain_3, fill, keep, d_out, heads):
        _, _, _, unit_2, rate_2, second_low, triple, mixed, unit_3, rate_3 = saved
        width = unit_2.shape[1]
        d_third, g_gain_3 = normed_back(unit_3, rate_3, gain_3, d_out.astype(F32) * keep)
        d_branch = d_third.astype(BF16)
        g_mix = weight_grad(mixed, d_branch).astype(BF16)
        d_mixed = pairs_of(project_back(d_branch, mix).astype(BF16))
        d_triple = attend_back((triple, 0), (triple, 1), (triple, 2), fill, d_mixed, width, heads)
        d_triple = rows_of(jnp.concatenate(d_triple, -1))
        g_joint = weight_grad(second_low, d_triple).astype(BF16)
        d_second = d_third + project_back(d_triple, joint)
        d_sum, g_gain_2 = normed_back(unit_2, rate_2, gain_2, d_second)
        return d_sum, g_mix, g_joint, g_gain_2, g_gain_3

    def feed_backward(saved, d_sum, unit_1, rate_1, gain_1, up, down):
        first_low, active, slope = saved[:3]
        d_sum_low = d_sum.astype(BF16)
        g_down = weight_grad(active, d_sum_low).astype(BF16)
        d_hidden = (slope.astype(F32) * project_back(d_sum_low, down)).astype(BF16)
        g_bias = jnp.sum(d_hidden.astype(F32), 0)
        g_up = weight_grad(first_low, d_hidden).astype(BF16)
        d_first = d_sum + project_back(d_hidden, up)
        d_resid, g_gain_1 = normed_back(unit_1, rate_1, gain_1, d_first)
        return d_resid, g_up, g_down, g_bias, g_gain_1

    def split_rows(matrix, parts):
        return [owned_rows(piece, devices) for piece in jnp.split(matrix, parts, 1)]

    out_text, saved_text = forward(
        unit_text_1,
        full["text_gain_cross"],
        full_text_up,
        full["text_bias"],
        full_text_down,
        full["text_gain_ffn"],
        full_text_self,
        full_text_mix,
        full["text_gain_self"],
        text_fill,
        text_keep,
        TEXT_HEADS,
    )
    d_sum_text, g_text_mix, g_text_self, g_text_gain_ffn, g_text_gain_self = self_backward(
        saved_text,
        full["text_gain_ffn"],
        full_text_self,
        full_text_mix,
        full["text_gain_self"],
        text_fill,
        text_keep,
        d_text_out,
        TEXT_HEADS,
    )
    d_resid_text, g_text_up, g_text_down, g_text_bias, g_text_gain_cross = feed_backward(
        saved_text, d_sum_text, unit_text_1, rate_text_1, full["text_gain_cross"], full_text_up, full_text_down
    )
    ups = text_up.shape[1] // text_width
    sum_text = OwnerSum(
        jnp.concatenate(
            split_rows(g_text_up, ups)
            + [owned_rows(g_text_down, devices)]
            + split_rows(g_text_self, 3)
            + [owned_rows(g_text_mix, devices)],
            1,
        ),
        sizes,
    )
    d_resid_text = sum_text.advance(d_resid_text)

    d_merge_text = d_resid_text.astype(BF16)
    g_text_merge = weight_grad(cross_text, d_merge_text).astype(BF16)
    d_heads_text = pairs_of(project_back(d_merge_text, full_text_merge).astype(BF16))
    d_query_text, d_key_image, d_value_image = map(
        rows_of,
        attend_back((triple_text, 0), (triple_image, 1), (triple_image, 2), image_fill, d_heads_text, inner, HEADS),
    )
    g_text_query = weight_grad(text_rows, d_query_text).astype(BF16)
    g_image_key = weight_grad(image_rows, d_key_image).astype(BF16)
    g_image_value = weight_grad(image_rows, d_value_image).astype(BF16)
    unit_image_1 = sum_text.advance(unit_image_1)
    sum_first = OwnerSum(
        jnp.concatenate(
            [
                owned_rows(g_text_query, devices),
                owned_rows(g_image_key, devices),
                owned_rows(g_image_value, devices),
                owned_rows(jnp.pad(g_text_merge, ((0, 0), (0, inner - text_width))), devices),
            ],
            1,
        ),
        sizes,
    )
    unit_image_1 = sum_first.advance(unit_image_1)

    out_image, saved_image = forward(
        unit_image_1,
        full["image_gain_cross"],
        full_image_up,
        full["image_bias"],
        full_image_down,
        full["image_gain_ffn"],
        full_image_self,
        full_image_mix,
        full["image_gain_self"],
        image_fill,
        image_keep,
        IMAGE_HEADS,
    )
    d_image_out = sum_text.advance(d_image_out, *saved_image)[0]
    d_sum_image, g_image_mix, g_image_self, g_image_gain_ffn, g_image_gain_self = self_backward(
        saved_image,
        full["image_gain_ffn"],
        full_image_self,
        full_image_mix,
        full["image_gain_self"],
        image_fill,
        image_keep,
        d_image_out,
        IMAGE_HEADS,
    )
    d_sum_image = sum_first.advance(d_sum_image)
    d_resid_image, g_image_up, g_image_down, g_image_bias, g_image_gain_cross = feed_backward(
        saved_image,
        d_sum_image,
        unit_image_1,
        rate_image_1,
        full["image_gain_cross"],
        full_image_up,
        full_image_down,
    )
    d_resid_image = sum_text.advance(d_resid_image)
    sum_image = OwnerSum(
        jnp.concatenate(
            [owned_rows(g_image_up, devices), owned_rows(g_image_down, devices)]
            + split_rows(g_image_self, 3)
            + [owned_rows(g_image_mix, devices)],
            1,
        ),
        sizes,
    )
    d_resid_image = sum_image.advance(d_resid_image)

    d_merge_image = d_resid_image.astype(BF16)
    g_image_merge = weight_grad(cross_image, d_merge_image).astype(BF16)
    d_heads_image = pairs_of(project_back(d_merge_image, full_image_merge).astype(BF16))
    d_query_image, d_key_text, d_value_text = map(
        rows_of,
        attend_back((triple_image, 0), (triple_text, 1), (triple_text, 2), text_fill, d_heads_image, inner, HEADS),
    )
    d_query_image = sum_first.advance(d_query_image)
    d_key_text = sum_image.advance(d_key_text)
    g_image_query = weight_grad(image_rows, d_query_image).astype(BF16)
    g_text_key = weight_grad(text_rows, d_key_text).astype(BF16)
    g_text_value = weight_grad(text_rows, d_value_text).astype(BF16)
    g_vectors = (
        g_text_gain_cross,
        g_image_gain_cross,
        g_text_bias,
        g_text_gain_ffn,
        g_image_bias,
        g_image_gain_ffn,
        g_text_gain_self,
        g_image_gain_self,
    )
    g_vector = jnp.concatenate([piece.reshape(devices, -1) for piece in g_vectors], 1).astype(BF16)
    g_vector = jnp.pad(g_vector[:, None, :], ((0, 0), (0, vector_rows - 1), (0, inner - g_vector.shape[1])))
    sum_last = OwnerSum(
        jnp.concatenate(
            [
                owned_rows(g_image_query, devices),
                owned_rows(g_text_key, devices),
                owned_rows(g_text_value, devices),
                owned_rows(g_image_merge, devices),
                g_vector,
            ],
            1,
        ),
        sizes,
    )
    d_resid_text, d_resid_image = sum_last.advance(d_resid_text, d_resid_image)
    grad_text = d_resid_text + project_back(
        jnp.concatenate([d_query_text, d_key_text, d_value_text], 1), weight_text
    )
    grad_image = d_resid_image + project_back(
        jnp.concatenate([d_query_image, d_key_image, d_value_image], 1), weight_image
    )

    def owned(total, pieces):
        return [total[start:end] for start, end in starts(pieces)]

    done = [one.result() for one in (sum_text, sum_first, sum_image, sum_last)]
    text_sums = owned(done[0], text_pieces)
    sum_text_query, sum_image_key, sum_image_value, sum_text_merge = owned(
        done[1], [text_query, image_key, image_value, text_merge]
    )
    image_sums = owned(done[2], image_pieces)
    sum_image_query, sum_text_key, sum_text_value, sum_image_merge, sum_vector = owned(
        done[3], [image_query, text_key, text_value, image_merge, vector_block]
    )
    owned_vector = {}
    at = 0
    for name, piece in zip(VECTOR_NAMES, vectors):
        owned_vector[name] = sum_vector[0, at : at + piece.shape[0]]
        at += piece.shape[0]
    return (
        pairs_of(out_text)[:, :length],
        pairs_of(out_image)[:, :regions],
        pairs_of(grad_text)[:, :length],
        pairs_of(grad_image)[:, :regions],
        sum_text_query,
        sum_image_key,
        sum_image_value,
        sum_text_merge[:, :text_width],
        owned_vector["text_gain_cross"],
        sum_image_query,
        sum_text_key,
        sum_text_value,
        sum_image_merge,
        owned_vector["image_gain_cross"],
        jnp.concatenate(text_sums[:-5], 1),
        owned_vector["text_bias"],
        text_sums[-5],
        owned_vector["text_gain_ffn"],
        image_sums[0],
        owned_vector["image_bias"],
        image_sums[1],
        owned_vector["image_gain_ffn"],
        jnp.concatenate(text_sums[-4:-1], 1),
        text_sums[-1],
        owned_vector["text_gain_self"],
        jnp.concatenate(image_sums[2:5], 1),
        image_sums[5],
        owned_vector["image_gain_self"],
    )


def solution(mesh):
    split = {1: P(AXES), 2: P(AXES, None), 3: P(AXES, None, None)}
    in_ranks = (3, 3, 1, 2, 3, 3) + tuple(
        1 if at in (4, 9, 11, 13, 15, 17, 20, 23) else 2 for at in range(24)
    )
    out_ranks = (3, 3, 3, 3) + in_ranks[6:]
    return jax.shard_map(
        functools.partial(per_device, dict(mesh.shape)),
        mesh=mesh,
        in_specs=tuple(split[rank] for rank in in_ranks),
        out_specs=tuple(split[rank] for rank in out_ranks),
        check_vma=False,
    )
```

time: 1040 us -> 795 us (0.76)
  waiting for transfers between devices: 445 us -> 307 us
  Pallas kernels: 134 us -> 39.7 us
  other arithmetic: 97.4 us -> 77.4 us
    pallas_call x6 -> x8, Pallas kernels: 134 us -> 39.7 us  [attention_call(): pl.pallas_call(kernel, grid=(pairs // together,), in_specs=[spec(array.sh...]
    all_gather x3, waiting for transfers between devices: 261 us -> 167 us  [gather(): return lax.all_gather(packed, AXES, axis=0, tiled=False)]
    unnamed x206 -> x317, local copies, waits for them, and re-layouts: 31.4 us -> 79.5 us
    ppermute x21 -> x28, waiting for transfers between devices: 184 us -> 140 us  [advance(): got = lax.ppermute(away, axis, [(at, at ^ 1 << bit) for at in range(count)])]
    concatenate x9 -> x6, other arithmetic: 31.9 us -> 3.85 us  [the longest x1 1.21 us: per_device(): jnp.concatenate([owned_rows(g_text_query, devices), owned_rows(g_image_ke...]
    reshape x5 -> x0, local copies, waits for them, and re-layouts: 20.2 us -> none  [the longest x3 10.1 us: owned_rows(): matrix.reshape(devices, parts, rows // parts, width).transpose(0, 2, 1, 3)]
    slice x24 -> x18, local copies, waits for them, and re-layouts: 55.9 us -> 41.9 us  [the longest x5 27.1 us: taken(): return whole(block[:, at[0]:at[1]])]
    dot_general x12 -> x16, matrix products: 60.6 us -> 48.2 us  [weight_grad(): lax.dot_general(left, right, (((0,), (0,)), ((), ())), preferred_element_...]
  transfers between devices with their start and end apart: 24 -> 31, of which waited for: 13 -> 17; matrix products, arithmetic and copies ran while one was open for 22% -> 35% of each run, Pallas kernels for 5% -> 3%
where the time goes in v1:
time: 795 us; the launch traced here: 789 us
  waiting for transfers between devices  307 us (39%)
  local copies, waits for them, and re-layouts  177 us (22%)
  matrix products  149 us (19%)
  other arithmetic  77.4 us (10%)
  Pallas kernels  39.7 us (5%)
  starting transfers between devices  22.5 us (3%)
  between operations  16.3 us (2%)
    all_gather x3, waiting for transfers between devices, gather(): return lax.all_gather(packed, AXES, axis=0, tiled=False)  167 us
    ppermute x28, waiting for transfers between devices, advance(): got = lax.ppermute(away, axis, [(at, at ^ 1 << bit) for at in range(count)])  140 us
    unnamed x317, local copies, waits for them, and re-layouts  79.5 us
    dot_general x12, matrix products, project_back(): lax.dot_general(left, right, (((1,), (1,)), ((), ())), preferred_element_...  53.8 us
    convert_element_type x24, other arithmetic, advance(): (kept.astype(F32) + got.astype(F32)).astype(F32 if last else BF16)  48.5 us
    dot_general x16, matrix products, weight_grad(): lax.dot_general(left, right, (((0,), (0,)), ((), ())), preferred_element_...  48.2 us
    dot_general x12, matrix products, project(): return jnp.dot(left, right, preferred_element_type=F32)  46.5 us
    pallas_call x8, Pallas kernels, attention_call(): pl.pallas_call(kernel, grid=(pairs // together,), in_specs=[spec(array.sh...  39.7 us
  transfers between devices with their start and end apart: 31, of which 17 were waited for; matrix products, arithmetic and copies ran while one was open for 35% of the time, Pallas kernels for 3%

profile of v1, /device:TPU:0, one launch (start us, length us, event | category | flops | bytes accessed | tf_op | source)
XLA Modules:
  0.0 788.7 jit_solution(5062841260707904078)
XLA Ops:
  27.4 105.8 %all-gather.7.cloned.1.call-done = bf16[7680,1024]{1,0:T(8,128)(2,1)} async-done(((bf16[240,1024]{1,0:T(8,128)(2,1)}), bf16[7680,1024]{1,0:T(8,128)(2,1)}) %all-gather.7.cloned.1.call-update) | async-done | bytes 15728656 | tf_op jit(solution)/shard_map/all_gather | solution.py:156
  152.1 7.4 fusion.107
  164.4 6.3 convolution_convert_fusion.1
  176.8 61.4 %all-gather.9.cloned.1.call-done = bf16[9216,768]{1,0:T(8,128)(2,1)} async-done(((bf16[288,768]{1,0:T(8,128)(2,1)}), bf16[9216,768]{1,0:T(8,128)(2,1)}) %all-gather.9.cloned.1.call-update) | async-done | bytes 14155792 | tf_op jit(solution)/shard_map/all_gather | solution.py:156
  248.9 7.9 fusion.63
  256.8 10.4 %fusion.124 = (f32[832]{0:T(1024)S(1)}, f32[832,768]{1,0:T(8,128)S(1)}) fusion(bf16[3072,768]{1,0:T(8,128)(2,1)S(1)} %bitcast.390, f32[832,3072]{1,0:T(8,128)} %fusion.63, f32[3072]{0:T(1024)S(1)} %reshape.790, f32[768]{0:T(1024)S(1)} %reshape.789, f32[832]{0:T(1024)S(1)} %add_rsqrt_fusion.2, f32[832,768]{1,0:T(8,128)S(1)} %get-tuple-element.233, ...), kind=kOutput, calls=%fused_computation.383 | convolution fusion | flops 3954621696 | bytes 20079360 | tf_op jit(solution)/shard_map/dot_general | solution.py:35
  284.4 8.9 %shard_map.503 = (bf16[8,104,768]{2,1,0:T(8,128)(2,1)S(1)}, bf16[8,104,768]{2,1,0:T(8,128)(2,1)S(1)}, bf16[8,104,768]{2,1,0:T(8,128)(2,1)S(1)}) custom-call(bf16[8,104,2304]{2,1,0:T(8,128)(2,1)} %bitcast.321, bf16[8,104,2304]{2,1,0:T(8,128)(2,1)} %bitcast.322, bf16[8,104,2304]{2,1,0:T(8,128)(2,1)} %bitcast.323, ...), custom_call_target="tpu_custom_call" | custom-call | flops 1329070080 | bytes 9371648 | tf_op jit(solution)/shard_map/pallas_call | solution.py:122
  306.0 14.6 %fusion.129 = (bf16[3072]{0:T(1024)(128)(2,1)}, bf16[832,3072]{1,0:T(8,128)(2,1)S(1)}) fusion(bf16[3072,768]{1,0:T(8,128)(2,1)} %bitcast.391, f32[832,768]{1,0:T(8,128)S(1)} %subtract_multiply_fusion.1, f32[832,3072]{1,0:T(8,128)} %fusion.63, f32[3072]{0:T(1024)S(1)} %reshape.790), kind=kOutput, calls=%fused_computation.388 | convolution fusion | flops 3982734336 | bytes 22628352 | tf_op jit(solution)/shard_map/dot_general | solution.py:39
  320.7 6.1 convolution_convert_fusion.5
  327.7 11.8 %convolution_convert_fusion.4 = bf16[3072,768]{1,0:T(8,128)(2,1)} fusion(f32[832,768]{1,0:T(8,128)S(1)} %subtract_multiply_fusion.1, f32[832,3072]{1,0:T(8,128)} %fusion.63, f32[3072]{0:T(1024)S(1)} %reshape.790), kind=kOutput, calls=%fused_computation.33 | convolution fusion | flops 3954425856 | bytes 17510400 | tf_op jit(solution)/shard_map/dot_general | solution.py:43
  360.6 8.2 %multiply_reduce_fusion.2 = (bf16[768]{0:T(1024)(128)(2,1)S(1)}, f32[832]{0:T(1024)S(1)}, f32[832]{0:T(1024)S(1)}, f32[832,768]{1,0:T(8,128)S(1)}) fusion(f32[832,768]{1,0:T(8,128)S(1)} %copy-done.31, f32[832]{0:T(1024)S(1)} %add_rsqrt_fusion.2, f32[832]{0:T(1024)S(1)} %broadcast_multiply_fusion.8, f32[768]{0:T(1024)S(1)} %reshape.789, ...), kind=kOutput, calls=%fused_computation.62 | convolution fusion | flops 3950491392 | bytes 17516032 | tf_op jit(solution)/shard_map/dot_general | solution.py:39
  382.8 6.6 shard_map.504
  400.6 10.0 %fusion = bf16[2,2,2,2,288,768]{5,4,2,1,3,0:T(8,128)(2,1)} fusion(bf16[2,2,2,2,288,768]{5,4,2,1,3,0:T(8,128)(2,1)} %collective-permute-done, bf16[2,1,2,2,2,288,768]{6,5,4,3,2,1,0:T(8,128)(2,1)} %get-tuple-element.155), kind=kLoop, calls=%fused_computation.2 | loop fusion | flops 14155776 | bytes 21233664 | tf_op jit(solution)/shard_map/convert_element_type | solution.py:193
  422.3 37.8 %collective-permute-done.3 = bf16[2,2,2,288,384]{4,3,1,0,2:T(8,128)(2,1)} collective-permute-done((bf16[2,2,2,288,384]{4,3,1,0,2:T(8,128)(2,1)}, bf16[2,2,2,288,384]{4,3,1,0,2:T(8,128)(2,1)}, u32[]{:S(2)}, u32[]{:S(2)}) %collective-permute-start.3) | collective-permute-done | bytes 1769504 | tf_op jit(solution)/shard_map/ppermute | solution.py:216
  474.7 6.3 fusion.110
  530.4 11.7 %constant_dynamic-slice_fusion.2 = (bf16[2,1,2,2,2,192,1024]{6,5,4,3,2,1,0:T(8,128)(2,1)}, bf16[2,1,2,2,2,192,1024]{6,5,4,3,2,1,0:T(8,128)(2,1)}) fusion(bf16[2,2,2,2,2,192,1024]{6,5,4,3,2,1,0:T(8,128)(2,1)} %constant_dynamic-update-slice_fusion.33, s32[]{:T(128)S(6)} %select_n.132, s32[]{:T(128)S(6)} %select_n.131), kind=kLoop, calls=%fused_computation.298 | loop fusion | bytes 25165832 | tf_op jit(solution)/shard_map/jit(dynamic_index_in_dim)/dynamic_slice | solution.py:209
  565.4 6.9 shard_map.508
  588.7 10.6 %fusion.1 = bf16[2,2,2,2,192,1024]{5,4,2,1,3,0:T(8,128)(2,1)} fusion(bf16[2,2,2,2,192,1024]{5,4,2,1,3,0:T(8,128)(2,1)} %collective-permute-done.8, bf16[2,1,2,2,2,192,1024]{6,5,4,3,2,1,0:T(8,128)(2,1)} %get-tuple-element.165), kind=kLoop, calls=%fused_computation.4 | loop fusion | flops 12582912 | bytes 18874368 | tf_op jit(solution)/shard_map/convert_element_type | solution.py:193
  631.5 14.8 %collective-permute-done.11 = bf16[2,120,1024]{2,1,0:T(8,128)(2,1)} collective-permute-done((bf16[2,120,1024]{2,1,0:T(8,128)(2,1)}, bf16[2,120,1024]{2,1,0:T(8,128)(2,1)}, u32[]{:S(2)}, u32[]{:S(2)}) %collective-permute-start.11) | collective-permute-done | bytes 491552 | tf_op jit(solution)/shard_map/ppermute | solution.py:216
  657.5 26.4 %collective-permute-done.23 = bf16[2,2,2,192,512]{4,3,1,0,2:T(8,128)(2,1)S(1)} collective-permute-done((bf16[2,2,2,192,512]{4,3,1,0,2:T(8,128)(2,1)S(1)}, bf16[2,2,2,192,512]{4,3,1,0,2:T(8,128)(2,1)S(1)}, u32[]{:S(2)}, u32[]{:S(2)}) %collective-permute-start.23) | collective-permute-done | bytes 1572896 | tf_op jit(solution)/shard_map/ppermute | solution.py:216
  699.2 7.7 fusion.47
  714.2 15.2 %collective-permute-done.15 = bf16[2,2,2,120,512]{4,3,1,0,2:T(8,128)(2,1)} collective-permute-done((bf16[2,2,2,120,512]{4,3,1,0,2:T(8,128)(2,1)}, bf16[2,2,2,120,512]{4,3,1,0,2:T(8,128)(2,1)}, u32[]{:S(2)}, u32[]{:S(2)}) %collective-permute-start.15) | collective-permute-done | bytes 983072 | tf_op jit(solution)/shard_map/ppermute | solution.py:216
  751.4 9.5 %collective-permute-done.27 = bf16[192,1024]{1,0:T(8,128)(2,1)S(1)} collective-permute-done((bf16[192,1024]{1,0:T(8,128)(2,1)S(1)}, bf16[192,1024]{1,0:T(8,128)(2,1)S(1)}, u32[]{:S(2)}, u32[]{:S(2)}) %collective-permute-start.27) | collective-permute-done | bytes 393248 | tf_op jit(solution)/shard_map/ppermute | solution.py:216
  761.9 10.4 %collective-permute-done.18 = bf16[2,120,1024]{2,1,0:T(8,128)(2,1)S(1)} collective-permute-done((bf16[2,120,1024]{2,1,0:T(8,128)(2,1)S(1)}, bf16[2,120,1024]{2,1,0:T(8,128)(2,1)S(1)}, u32[]{:S(2)}, u32[]{:S(2)}) %collective-permute-start.18) | collective-permute-done | bytes 491552 | tf_op jit(solution)/shard_map/ppermute | solution.py:216
  (583 shorter events, 349.7 us)
Async XLA Ops:
  7.2 126.0 %all-gather.7.cloned.1.call-start = ((), (), s32[]{:S(2)}) async-start(), calls=%async_computation | async-start | bytes 16220160 | tf_op jit(solution)/shard_map/all_gather | solution.py:156
  20.2 218.0 %all-gather.9.cloned.1.call-start = ((), (), s32[]{:S(2)}) async-start(), calls=%async_computation.1 | async-start | bytes 14598144 | tf_op jit(solution)/shard_map/all_gather | solution.py:156
  133.2 341.4 %all-gather.11.cloned.1.call-start = ((), (), s32[]{:S(2)}) async-start(), calls=%async_computation.2 | async-start | bytes 12976128 | tf_op jit(solution)/shard_map/all_gather | solution.py:156
  370.8 29.8 %collective-permute-start = (bf16[2,2,2,2,288,768]{5,4,2,1,3,0:T(8,128)(2,1)}, bf16[2,2,2,2,288,768]{5,4,2,1,3,0:T(8,128)(2,1)}, u32[]{:S(2)}, u32[]{:S(2)}) collective-permute-start(bf16[2,2,2,2,288,768]{5,4,2,1,3,0:T(8,128)(2,1)} %bitcast.309), channel_id=1, source_target_pairs={{0,8},{8,0},{16,24},{24,16},{1,9},{9,1},{17,25},{25,17},{2,10},{10... | collective-permute-start | bytes 21233672 | tf_op jit(solution)/shard_map/ppermute | solution.py:216
  418.7 48.1 %collective-permute-start.1 = (bf16[2,2,2,2,120,1024]{5,4,2,1,3,0:T(8,128)(2,1)}, bf16[2,2,2,2,120,1024]{5,4,2,1,3,0:T(8,128)(2,1)}, u32[]{:S(2)}, u32[]{:S(2)}) collective-permute-start(bf16[2,2,2,2,120,1024]{5,4,2,1,3,0:T(8,128)(2,1)} %bitcast.312), channel_id=1, source_target_pairs={{0,8},{8,0},{16,24},{24,16},{1,9},{9,1},{17,25},{25,17},{2,10},{10... | collective-permute-start | bytes 11796488 | tf_op jit(solution)/shard_map/ppermute | solution.py:216
  418.9 41.1 %collective-permute-start.3 = (bf16[2,2,2,288,384]{4,3,1,0,2:T(8,128)(2,1)}, bf16[2,2,2,288,384]{4,3,1,0,2:T(8,128)(2,1)}, u32[]{:S(2)}, u32[]{:S(2)}) collective-permute-start(bf16[2,2,2,288,384]{4,3,1,0,2:T(8,128)(2,1)} %dynamic-slice_bitcast_fusion), channel_id=1, source_target_pairs={{0,16},{8,24},{16,0},{24,8},{1,17},{9,25},{17,1},{25,9},{2,18},{10... | collective-permute-start | bytes 5308424 | tf_op jit(solution)/shard_map/ppermute | solution.py:216
  420.4 43.2 %collective-permute-start.2 = (bf16[2,2,2,288,384]{4,3,2,1,0:T(8,128)(2,1)}, bf16[2,2,2,288,384]{4,3,2,1,0:T(8,128)(2,1)}, u32[]{:S(2)}, u32[]{:S(2)}) collective-permute-start(bf16[2,2,2,288,384]{4,3,2,1,0:T(8,128)(2,1)} %dynamic-slice_bitcast_fusion.1), channel_id=1, source_target_pairs={{0,1},{1,0},{2,3},{3,2},{4,5},{5,4},{6,7},{7,6},{8,9},{9,8},{10,11... | collective-permute-start | bytes 5308424 | tf_op jit(solution)/shard_map/ppermute | solution.py:216
  516.2 34.4 %collective-permute-start.7 = (bf16[2,2,288,384]{3,2,1,0:T(8,128)(2,1)}, bf16[2,2,288,384]{3,2,1,0:T(8,128)(2,1)}, u32[]{:S(2)}, u32[]{:S(2)}) collective-permute-start(bf16[2,2,288,384]{3,2,1,0:T(8,128)(2,1)} %dynamic-slice_bitcast_fusion.8), channel_id=1, source_target_pairs={{0,1},{1,0},{2,3},{3,2},{4,5},{5,4},{6,7},{7,6},{8,9},{9,8},{10,11... | collective-permute-start | bytes 2654216 | tf_op jit(solution)/shard_map/ppermute | solution.py:216
  517.6 35.0 %collective-permute-start.6 = (bf16[2,2,288,384]{3,2,1,0:T(8,128)(2,1)}, bf16[2,2,288,384]{3,2,1,0:T(8,128)(2,1)}, u32[]{:S(2)}, u32[]{:S(2)}) collective-permute-start(bf16[2,2,288,384]{3,2,1,0:T(8,128)(2,1)} %dynamic-slice_bitcast_fusion.9), channel_id=1, source_target_pairs={{0,16},{8,24},{16,0},{24,8},{1,17},{9,25},{17,1},{25,9},{2,18},{10... | collective-permute-start | bytes 2654216 | tf_op jit(solution)/shard_map/ppermute | solution.py:216
  555.7 33.1 %collective-permute-start.8 = (bf16[2,2,2,2,192,1024]{5,4,2,1,3,0:T(8,128)(2,1)}, bf16[2,2,2,2,192,1024]{5,4,2,1,3,0:T(8,128)(2,1)}, u32[]{:S(2)}, u32[]{:S(2)}) collective-permute-start(bf16[2,2,2,2,192,1024]{5,4,2,1,3,0:T(8,128)(2,1)} %bitcast.310), channel_id=1, source_target_pairs={{0,8},{8,0},{16,24},{24,16},{1,9},{9,1},{17,25},{25,17},{2,10},{10... | collective-permute-start | bytes 18874376 | tf_op jit(solution)/shard_map/ppermute | solution.py:216
  556.6 24.4 %collective-permute-start.5 = (bf16[2,2,2,120,512]{4,3,1,0,2:T(8,128)(2,1)}, bf16[2,2,2,120,512]{4,3,1,0,2:T(8,128)(2,1)S(1)}, u32[]{:S(2)}, u32[]{:S(2)}) collective-permute-start(bf16[2,2,2,120,512]{4,3,1,0,2:T(8,128)(2,1)} %dynamic-slice_bitcast_fusion.6), channel_id=1, source_target_pairs={{0,16},{8,24},{16,0},{24,8},{1,17},{9,25},{17,1},{25,9},{2,18},{10... | collective-permute-start | bytes 2949128 | tf_op jit(solution)/shard_map/ppermute | solution.py:216
  558.4 24.1 %collective-permute-start.4 = (bf16[2,2,2,120,512]{4,3,2,1,0:T(8,128)(2,1)}, bf16[2,2,2,120,512]{4,3,2,1,0:T(8,128)(2,1)S(1)}, u32[]{:S(2)}, u32[]{:S(2)}) collective-permute-start(bf16[2,2,2,120,512]{4,3,2,1,0:T(8,128)(2,1)} %dynamic-slice_bitcast_fusion.7), channel_id=1, source_target_pairs={{0,1},{1,0},{2,3},{3,2},{4,5},{5,4},{6,7},{7,6},{8,9},{9,8},{10,11... | collective-permute-start | bytes 2949128 | tf_op jit(solution)/shard_map/ppermute | solution.py:216
  564.2 58.0 %collective-permute-start.20 = (bf16[2,288,768]{2,1,0:T(8,128)(2,1)}, bf16[2,288,768]{2,1,0:T(8,128)(2,1)}, u32[]{:S(2)}, u32[]{:S(2)}) collective-permute-start(bf16[2,288,768]{2,1,0:T(8,128)(2,1)} %fusion.59), channel_id=1, source_target_pairs={{0,4},{1,5},{2,6},{3,7},{4,0},{5,1},{6,2},{7,3},{8,12},{9,13},{10,... | collective-permute-start | bytes 2654216 | tf_op jit(solution)/shard_map/ppermute | solution.py:216
  583.7 33.6 %collective-permute-start.10 = (bf16[2,2,120,512]{3,2,1,0:T(8,128)(2,1)}, bf16[2,2,120,512]{3,2,1,0:T(8,128)(2,1)}, u32[]{:S(2)}, u32[]{:S(2)}) collective-permute-start(bf16[2,2,120,512]{3,2,1,0:T(8,128)(2,1)} %dynamic-slice_bitcast_fusion.14), channel_id=1, source_target_pairs={{0,1},{1,0},{2,3},{3,2},{4,5},{5,4},{6,7},{7,6},{8,9},{9,8},{10,11... | collective-permute-start | bytes 1474568 | tf_op jit(solution)/shard_map/ppermute | solution.py:216
  585.2 33.2 %collective-permute-start.9 = (bf16[2,2,120,512]{3,2,1,0:T(8,128)(2,1)}, bf16[2,2,120,512]{3,2,1,0:T(8,128)(2,1)}, u32[]{:S(2)}, u32[]{:S(2)}) collective-permute-start(bf16[2,2,120,512]{3,2,1,0:T(8,128)(2,1)} %dynamic-slice_bitcast_fusion.15), channel_id=1, source_target_pairs={{0,16},{8,24},{16,0},{24,8},{1,17},{9,25},{17,1},{25,9},{2,18},{10... | collective-permute-start | bytes 1474568 | tf_op jit(solution)/shard_map/ppermute | solution.py:216
  617.3 73.8 %collective-permute-start.13 = (bf16[2,2,2,2,120,1024]{5,4,2,1,3,0:T(8,128)(2,1)}, bf16[2,2,2,2,120,1024]{5,4,2,1,3,0:T(8,128)(2,1)}, u32[]{:S(2)}, u32[]{:S(2)}) collective-permute-start(bf16[2,2,2,2,120,1024]{5,4,2,1,3,0:T(8,128)(2,1)} %bitcast.311), channel_id=1, source_target_pairs={{0,8},{8,0},{16,24},{24,16},{1,9},{9,1},{17,25},{25,17},{2,10},{10... | collective-permute-start | bytes 11796488 | tf_op jit(solution)/shard_map/ppermute | solution.py:216
  621.3 24.9 %collective-permute-start.11 = (bf16[2,120,1024]{2,1,0:T(8,128)(2,1)}, bf16[2,120,1024]{2,1,0:T(8,128)(2,1)}, u32[]{:S(2)}, u32[]{:S(2)}) collective-permute-start(bf16[2,120,1024]{2,1,0:T(8,128)(2,1)} %fusion.79), channel_id=1, source_target_pairs={{0,4},{1,5},{2,6},{3,7},{4,0},{5,1},{6,2},{7,3},{8,12},{9,13},{10,... | collective-permute-start | bytes 1474568 | tf_op jit(solution)/shard_map/ppermute | solution.py:216
  625.5 23.6 %collective-permute-start.21 = (bf16[288,768]{1,0:T(8,128)(2,1)}, bf16[288,768]{1,0:T(8,128)(2,1)}, u32[]{:S(2)}, u32[]{:S(2)}) collective-permute-start(bf16[288,768]{1,0:T(8,128)(2,1)} %dynamic-slice_bitcast_fusion.16), channel_id=1, source_target_pairs={{0,2},{1,3},{2,0},{3,1},{4,6},{5,7},{6,4},{7,5},{8,10},{9,11},{10,... | collective-permute-start | bytes 1327112 | tf_op jit(solution)/shard_map/ppermute | solution.py:216
  647.6 36.4 %collective-permute-start.23 = (bf16[2,2,2,192,512]{4,3,1,0,2:T(8,128)(2,1)S(1)}, bf16[2,2,2,192,512]{4,3,1,0,2:T(8,128)(2,1)S(1)}, u32[]{:S(2)}, u32[]{:S(2)}) collective-permute-start(bf16[2,2,2,192,512]{4,3,1,0,2:T(8,128)(2,1)S(1)} %copy-done.93), channel_id=1, source_target_pairs={{0,16},{8,24},{16,0},{24,8},{1,17},{9,25},{17,1},{25,9},{2,18},{10... | collective-permute-start | bytes 4718600 | tf_op jit(solution)/shard_map/ppermute | solution.py:216
  651.6 36.0 %collective-permute-start.22 = (bf16[2,2,2,192,512]{4,3,2,1,0:T(8,128)(2,1)S(1)}, bf16[2,2,2,192,512]{4,3,2,1,0:T(8,128)(2,1)S(1)}, u32[]{:S(2)}, u32[]{:S(2)}) collective-permute-start(bf16[2,2,2,192,512]{4,3,2,1,0:T(8,128)(2,1)S(1)} %copy-done.92), channel_id=1, source_target_pairs={{0,1},{1,0},{2,3},{3,2},{4,5},{5,4},{6,7},{7,6},{8,9},{9,8},{10,11... | collective-permute-start | bytes 4718600 | tf_op jit(solution)/shard_map/ppermute | solution.py:216
  697.7 31.6 %collective-permute-start.15 = (bf16[2,2,2,120,512]{4,3,1,0,2:T(8,128)(2,1)}, bf16[2,2,2,120,512]{4,3,1,0,2:T(8,128)(2,1)}, u32[]{:S(2)}, u32[]{:S(2)}) collective-permute-start(bf16[2,2,2,120,512]{4,3,1,0,2:T(8,128)(2,1)} %dynamic-slice_bitcast_fusion.4), channel_id=1, source_target_pairs={{0,16},{8,24},{16,0},{24,8},{1,17},{9,25},{17,1},{25,9},{2,18},{10... | collective-permute-start | bytes 2949128 | tf_op jit(solution)/shard_map/ppermute | solution.py:216
  706.9 24.2 %collective-permute-start.14 = (bf16[2,2,2,120,512]{4,3,2,1,0:T(8,128)(2,1)}, bf16[2,2,2,120,512]{4,3,2,1,0:T(8,128)(2,1)S(1)}, u32[]{:S(2)}, u32[]{:S(2)}) collective-permute-start(bf16[2,2,2,120,512]{4,3,2,1,0:T(8,128)(2,1)} %dynamic-slice_bitcast_fusion.5), channel_id=1, source_target_pairs={{0,1},{1,0},{2,3},{3,2},{4,5},{5,4},{6,7},{7,6},{8,9},{9,8},{10,11... | collective-permute-start | bytes 2949128 | tf_op jit(solution)/shard_map/ppermute | solution.py:216
  712.2 33.5 %collective-permute-start.26 = (bf16[2,192,1024]{2,1,0:T(8,128)(2,1)S(1)}, bf16[2,192,1024]{2,1,0:T(8,128)(2,1)S(1)}, u32[]{:S(2)}, u32[]{:S(2)}) collective-permute-start(bf16[2,192,1024]{2,1,0:T(8,128)(2,1)S(1)} %fusion.65), channel_id=1, source_target_pairs={{0,4},{1,5},{2,6},{3,7},{4,0},{5,1},{6,2},{7,3},{8,12},{9,13},{10,... | collective-permute-start | bytes 2359304 | tf_op jit(solution)/shard_map/ppermute | solution.py:216
  750.8 21.4 %collective-permute-start.18 = (bf16[2,120,1024]{2,1,0:T(8,128)(2,1)S(1)}, bf16[2,120,1024]{2,1,0:T(8,128)(2,1)S(1)}, u32[]{:S(2)}, u32[]{:S(2)}) collective-permute-start(bf16[2,120,1024]{2,1,0:T(8,128)(2,1)S(1)} %fusion.75), channel_id=1, source_target_pairs={{0,4},{1,5},{2,6},{3,7},{4,0},{5,1},{6,2},{7,3},{8,12},{9,13},{10,... | collective-permute-start | bytes 1474568 | tf_op jit(solution)/shard_map/ppermute | solution.py:216
  (140 other events, 1443.1 us)
Sparse Core Ops, SparseCore 0:
  20.4 112.7 all-gather.6
  136.8 101.4 all-gather.8
  303.2 94.0 all-gather.10

commit v2 on v1

--- a/solution.py
+++ b/solution.py
@@ -156,6 +156,32 @@
     return lax.all_gather(packed, AXES, axis=0, tiled=False)
 
 
+def gather_by_exchange(packed, sizes):
+    core, rows, columns, rest = mesh_axes_bits(sizes)
+    order = mesh_bits(sizes)
+
+    def doubled(block, have, which):
+        axis, bit = which
+        count = lax.axis_size(axis)
+        got = lax.ppermute(block, axis, [(at, at ^ (1 << bit)) for at in range(count)])
+        first = ((lax.axis_index(axis) >> bit) & 1) == 0
+        have = sorted(have + [which], key=order.index)
+        lower, upper = jnp.where(first, block, got), jnp.where(first, got, block)
+        return jnp.stack([lower, upper], have.index(which)), have
+
+    block, have = packed, []
+    for which in reversed(rest):
+        block, have = doubled(block, have, which)
+    width = packed.shape[1]
+    halves = [(block[..., : width // 2], have), (block[..., width // 2 :], have)]
+    for steps in zip(rows + columns, columns + rows):
+        halves = [doubled(block, have, which) for (block, have), which in zip(halves, steps)]
+    block, have = jnp.concatenate([halves[0][0], halves[1][0]], -1), halves[0][1]
+    for which in core:
+        block, have = doubled(block, have, which)
+    return block.reshape((-1,) + packed.shape)
+
+
 def whole(block):
     return block.reshape(-1, block.shape[-1])
 
@@ -171,43 +197,201 @@
     return bits
 
 
+def mesh_axes_bits(sizes):
+    low = (sizes["gy"].bit_length() - 1) // 2
+    bits = mesh_bits(sizes)[::-1]
+    core = [one for one in bits if one == ("gx", 0)]
+    rows = [one for one in bits if one[0] == "gx" and one[1] > 0]
+    columns = [one for one in bits if one[0] == "gy" and one[1] < low]
+    rest = [one for one in bits if one[0] == "gy" and one[1] >= low]
+    return core, rows, columns, rest
+
+
+def grad_kernel(per_core, left_ref, right_ref, core_ref, *refs):
+    away_ref, kept_ref, whole_ref = refs[-3:]
+    own = core_ref[0]
+    grad = weight_grad(left_ref[...], right_ref[...])
+    groups, _, width = whole_ref.shape
+    if grad.shape[1] < width:
+        grad = jnp.pad(grad, ((0, 0), (0, width - grad.shape[1])))
+    whole_ref[...] = grad.reshape(whole_ref.shape)
+    for group in range(groups // 2):
+        shape = kept_ref.shape[1:]
+        kept_ref[group] = whole_ref[2 * group + own].reshape(shape).astype(BF16)
+        away_ref[group] = whole_ref[2 * group + 1 - own].reshape(shape).astype(BF16)
+
+
+def grad_rows_kernel(left_ref, right_ref, core_ref, *refs):
+    away_ref, kept_ref = refs[-2:]
+    stays = pl.program_id(0) % 2 == core_ref[0]
+    shape = kept_ref.shape[1:]
+    grad = weight_grad(left_ref[...], right_ref[...]).astype(BF16).reshape(shape)
+
+    @pl.when(stays)
+    def _():
+        kept_ref[0] = grad
+
+    @pl.when(jnp.logical_not(stays))
+    def _():
+        away_ref[0] = grad
+
+
+def place_kernel(terms_ref, core_ref, *refs):
+    away_ref, kept_ref = refs[-2:]
+    own = core_ref[0]
+    for group in range(kept_ref.shape[0]):
+        kept_ref[group] = terms_ref[group, own]
+        away_ref[group] = terms_ref[group, 1 - own]
+
+
+def pack_terms(pieces, rows, width, sizes):
+    groups, others = sizes["gx"] // 2, sizes["gy"]
+    core = (lax.axis_index("gx") & 1).astype(jnp.int32).reshape(1)
+    shape = jax.ShapeDtypeStruct((groups, others, rows, width), BF16)
+    buffers = []
+    for piece in pieces:
+        first, scratch = piece[0], []
+        scalar = pl.BlockSpec(memory_space=pltpu.SMEM)
+        if len(piece) == 2:
+            terms = piece[1].reshape((groups, 2, others) + piece[1].shape[1:])
+            count = terms.shape[3]
+            kernel, arrays, grid, flops = place_kernel, [terms], (1,), 0
+            in_specs = [pl.BlockSpec(terms.shape, lambda step: (0,) * 5)]
+            place = pl.BlockSpec((groups, others, count, width), lambda step, at=first // count: (0, 0, at, 0))
+        else:
+            left, right = piece[1:]
+            height, tall = left.shape
+            count = tall // (2 * groups * others)
+            arrays, flops = [left, right], 2 * height * tall * right.shape[1]
+            if right.shape[1] <= width and tall >= 2048:
+                kernel, grid = grad_rows_kernel, (2 * groups,)
+                in_specs = [
+                    pl.BlockSpec((height, tall // (2 * groups)), lambda step: (0, step)),
+                    pl.BlockSpec(right.shape, lambda step: (0, 0)),
+                ]
+                place = pl.BlockSpec((1, others, count, width), lambda step, at=first // count: (step // 2, 0, at, 0))
+            else:
+                each = min(width, right.shape[1])
+                kernel, grid = functools.partial(grad_kernel, groups), (right.shape[1] // each,)
+                in_specs = [
+                    pl.BlockSpec(left.shape, lambda step: (0, 0)),
+                    pl.BlockSpec((height, each), lambda step: (0, step)),
+                ]
+                place = pl.BlockSpec(
+                    (groups, others, count, width), lambda step, at=first // count: (0, 0, at + step, 0)
+                )
+                scratch = [pltpu.VMEM((2 * groups, tall // (2 * groups), width), F32)]
+        assert first % count == 0
+        arrays = arrays + [core] + buffers
+        in_specs = in_specs + [scalar] + [pl.BlockSpec(memory_space=pl.ANY)] * len(buffers)
+        moved = sum(array.size * 2 for array in arrays[:2]) + 4 * flops // 2048
+        buffers = list(pl.pallas_call(
+            kernel,
+            grid=grid,
+            in_specs=in_specs,
+            out_specs=[place, place],
+            out_shape=[shape, shape],
+            scratch_shapes=scratch,
+            input_output_aliases={len(arrays) - 2: 0, len(arrays) - 1: 1} if buffers else {},
+            compiler_params=pltpu.CompilerParams(vmem_limit_bytes=VMEM_BYTES),
+            cost_estimate=pl.CostEstimate(flops=flops, bytes_accessed=moved, transcendentals=0),
+        )(*arrays))
+    return buffers
+
+
+def split_kernel(where_ref, kept_ref, got_ref, away_x_ref, kept_x_ref, away_y_ref, kept_y_ref):
+    x, y = where_ref[0], where_ref[1]
+    half = kept_ref.shape[-1] // 2
+
+    def added(at, columns):
+        return (kept_ref[0, 0, 0, at, :, columns].astype(F32) + got_ref[0, 0, 0, at, :, columns].astype(F32)).astype(BF16)
+
+    left, right = slice(0, half), slice(half, 2 * half)
+    kept_x_ref[0, 0, 0] = added(x, left)
+    away_x_ref[0, 0, 0] = added(1 - x, left)
+    stays = pl.program_id(2) == y
+
+    @pl.when(stays)
+    def _():
+        for at in range(2):
+            kept_y_ref[0, 0, at] = added(at, right)
+
+    @pl.when(jnp.logical_not(stays))
+    def _():
+        for at in range(2):
+            away_y_ref[0, 0, at] = added(at, right)
+
+
+def split_terms(kept, got):
+    groups, others, rows, width = kept.shape
+    where = jnp.stack([lax.axis_index("gy") & 1, (lax.axis_index("gx") >> 1) & 1]).astype(jnp.int32)
+    shape = (groups // 2, 2, others // 2, 2, rows, width)
+    half = width // 2
+    inside = pl.BlockSpec((1, 1, 1, 2, rows, width), lambda high, z, y, where: (high, y, z, 0, 0, 0))
+    along_x = pl.BlockSpec((1, 1, 1, rows, half), lambda high, z, y, where: (high, y, z, 0, 0))
+    along_y = pl.BlockSpec((1, 1, 2, rows, half), lambda high, z, y, where: (high, z, 0, 0, 0))
+    shape_x = jax.ShapeDtypeStruct((groups // 2, 2, others // 2, rows, half), BF16)
+    shape_y = jax.ShapeDtypeStruct((groups // 2, others // 2, 2, rows, half), BF16)
+    return pl.pallas_call(
+        split_kernel,
+        grid_spec=pltpu.PrefetchScalarGridSpec(
+            num_scalar_prefetch=1,
+            grid=(groups // 2, others // 2, 2),
+            in_specs=[inside, inside],
+            out_specs=[along_x, along_x, along_y, along_y],
+        ),
+        out_shape=[shape_x, shape_x, shape_y, shape_y],
+        compiler_params=pltpu.CompilerParams(vmem_limit_bytes=VMEM_BYTES),
+        cost_estimate=pl.CostEstimate(flops=kept.size, bytes_accessed=6 * kept.size, transcendentals=0),
+    )(where, kept.reshape(shape), got.reshape(shape))
+
+
 class OwnerSum:
-    def __init__(self, packed, sizes):
+    def __init__(self, pieces, rows, width, sizes):
         bits = mesh_bits(sizes)
-        low = (sizes["gy"].bit_length() - 1) // 2
-        core = [("gx", 0)] if sizes["gx"] > 1 else []
-        rows = [one for one in bits if one[0] == "gx" and one not in core]
-        columns = [one for one in bits if one[0] == "gy" and one[1] < low]
-        rest = [one for one in bits if one[0] == "gy" and one[1] >= low]
-        self.width = packed.shape[-1]
-        self.parts = [(packed.reshape((2,) * len(bits) + packed.shape[1:]), bits)]
-        self.plan = [[which] for which in core]
-        self.plan += [list(pair) for pair in zip(columns + rows, rows + columns)]
-        self.plan += [[which] for which in rest]
+        core, y_bits, x_bits, z_bits = mesh_axes_bits(sizes)
+        self.width = width
         self.flying = None
+        self.plan = [list(pair) for pair in zip(x_bits + y_bits, y_bits + x_bits)] + [[which] for which in z_bits]
+        devices = sizes["gx"] * sizes["gy"]
+        self.whole_tiles = len(core) == 1 and bool(y_bits) and bool(x_bits) and len(x_bits) == len(y_bits)
+        for piece in pieces:
+            self.whole_tiles &= len(piece) == 2 or piece[1].shape[1] % (8 * devices) == 0
+        if self.whole_tiles:
+            away, kept = pack_terms(pieces, rows, width, sizes)
+            self.waiting = [(away, kept) + core[0] + ([one for one in bits if one not in core],)]
+        else:
+            packed = jnp.zeros((devices, rows, width), BF16)
+            for piece in pieces:
+                blocks = [piece[1]]
+                if len(piece) == 3:
+                    grad = weight_grad(*piece[1:]).astype(BF16)
+                    blocks = jnp.split(grad, max(1, grad.shape[1] // width), 1)
+                at = piece[0]
+                for block in blocks:
+                    block = block.reshape(devices, -1, block.shape[-1])
+                    packed = lax.dynamic_update_slice(packed, block, (0, at, 0))
+                    at += block.shape[1]
+            self.waiting = None
+            self.parts = [(packed.reshape((2,) * len(bits) + packed.shape[1:]), bits)]
+            self.plan = [[which] for which in core] + self.plan
 
     def advance(self, *others):
+        sends, self.waiting = self.waiting, None
         if self.flying is not None:
-            last = not self.plan
-            self.parts = [
-                ((kept.astype(F32) + got.astype(F32)).astype(F32 if last else BF16), bits)
-                for kept, got, bits in self.flying
-            ]
+            held = tie(*[got for _, got, _ in self.flying], *others)
+            others = held[len(self.flying) :]
+            if self.whole_tiles and self.flying[0][0].ndim == 4 and self.flying[0][0].shape[-1] == self.width and len(self.plan[0]) == 2:
+                sends = self.first_split(held[0])
+            else:
+                self.parts = [
+                    ((kept.astype(F32) + got.astype(F32)).astype(BF16 if self.plan else F32), bits)
+                    for (kept, _, bits), got in zip(self.flying, held)
+                ]
             self.flying = None
-        if self.plan:
-            step = self.plan.pop(0)
-            if len(step) == 2 and len(self.parts) == 1:
-                total, bits = self.parts[0]
-                self.parts = [(total[..., : self.width // 2], bits), (total[..., self.width // 2 :], bits)]
-            if len(step) == 1 and len(self.parts) == 2:
-                self.parts = [(jnp.concatenate([self.parts[0][0], self.parts[1][0]], -1), self.parts[0][1])]
-            sends = []
-            for (total, bits), (axis, bit) in zip(self.parts, step):
-                place = bits.index((axis, bit))
-                own = (lax.axis_index(axis) >> bit) & 1
-                away = lax.dynamic_index_in_dim(total, 1 - own, place, keepdims=False)
-                kept = lax.dynamic_index_in_dim(total, own, place, keepdims=False)
-                sends.append((away, kept, axis, bit, [one for one in bits if one != (axis, bit)]))
+        if sends is None and self.plan:
+            sends = self.halves()
+        if sends is not None:
             held = tie(*[one[0] for one in sends], *others)
             others = held[len(sends) :]
             self.flying = []
@@ -216,6 +400,32 @@
                 got = lax.ppermute(away, axis, [(at, at ^ (1 << bit)) for at in range(count)])
                 self.flying.append((kept, got, left))
         return others[0] if len(others) == 1 else others
+
+    def first_split(self, got):
+        kept, _, bits = self.flying[0]
+        out = split_terms(kept, got)
+        sends = []
+        for part, which in enumerate(self.plan.pop(0)):
+            left = [one for one in bits if one != which]
+            away, kept = (one.reshape((2,) * len(left) + one.shape[-2:]) for one in out[2 * part : 2 * part + 2])
+            sends.append((away, kept) + which + (left,))
+        return sends
+
+    def halves(self):
+        step = self.plan.pop(0)
+        if len(step) == 2 and len(self.parts) == 1:
+            total, bits = self.parts[0]
+            self.parts = [(total[..., : self.width // 2], bits), (total[..., self.width // 2 :], bits)]
+        if len(step) == 1 and len(self.parts) == 2:
+            self.parts = [(jnp.concatenate([self.parts[0][0], self.parts[1][0]], -1), self.parts[0][1])]
+        sends = []
+        for (total, bits), (axis, bit) in zip(self.parts, step):
+            place = bits.index((axis, bit))
+            own = (lax.axis_index(axis) >> bit) & 1
+            away = lax.dynamic_index_in_dim(total, 1 - own, place, keepdims=False)
+            kept = lax.dynamic_index_in_dim(total, own, place, keepdims=False)
+            sends.append((away, kept, axis, bit, [one for one in bits if one != (axis, bit)]))
+        return sends
 
     def result(self):
         while self.plan or self.flying is not None:
@@ -299,17 +509,16 @@
         text_gain_self,
         image_gain_self,
     )
-    vector = jnp.concatenate(vectors)
-    vector_rows = 8
-    vector_block = jnp.pad(vector[None, :], ((0, vector_rows - 1), (0, inner - vector.shape[0])))
-    cross_pieces = [text_query, text_key, text_value, image_query, image_key, image_value, image_merge]
-    packed_cross = jnp.concatenate(
-        cross_pieces + [jnp.pad(text_merge, ((0, 0), (0, inner - text_width))), vector_block], 0
-    )
+    vector_block = jnp.concatenate(
+        [jnp.pad(vector[None, :], ((0, 0), (0, text_width - vector.shape[0]))) for vector in vectors], 0
+    )
+    first_pieces = [text_query, image_key, image_value]
+    packed_first = jnp.concatenate(first_pieces + [jnp.pad(text_merge, ((0, 0), (0, inner - text_width)))], 0)
     text_pieces = jnp.split(text_up, text_up.shape[1] // text_width, 1) + [text_down]
-    text_pieces += jnp.split(text_self, 3, 1) + [text_mix]
+    text_pieces += jnp.split(text_self, 3, 1) + [text_mix, vector_block]
     packed_text = jnp.concatenate(text_pieces, 0)
-    image_pieces = [image_up, image_down] + jnp.split(image_self, 3, 1) + [image_mix]
+    image_pieces = [image_query, text_key, text_value, image_merge, image_up, image_down]
+    image_pieces += jnp.split(image_self, 3, 1) + [image_mix]
     packed_image = jnp.concatenate(image_pieces, 0)
 
     def starts(pieces):
@@ -318,38 +527,19 @@
             marks.append(marks[-1] + piece.shape[0])
         return list(zip(marks[:-1], marks[1:]))
 
-    cross_at = starts(cross_pieces + [text_merge, vector_block])
-    text_at, image_at = starts(text_pieces), starts(image_pieces)
-    all_cross = gather(packed_cross)
-    all_cross, packed_text = tie(all_cross, packed_text)
-    all_text = gather(packed_text)
-    all_text, packed_image = tie(all_text, packed_image)
-    all_image = gather(packed_image)
-
     def taken(block, at):
         return whole(block[:, at[0] : at[1]])
 
     def side_by_side(block, spans):
         return jnp.concatenate([taken(block, at) for at in spans], 1)
 
-    weight_text = side_by_side(all_cross, cross_at[:3])
-    weight_image = side_by_side(all_cross, cross_at[3:6])
-    full_image_merge = taken(all_cross, cross_at[6])
-    full_text_merge = taken(all_cross, cross_at[7])[:, :text_width]
-    all_vectors = all_cross[:, cross_at[8][0]]
-    full = {}
-    at = 0
-    for name, piece in zip(VECTOR_NAMES, vectors):
-        full[name] = all_vectors[:, at : at + piece.shape[0]].reshape(-1).astype(F32)
-        at += piece.shape[0]
-    full_text_up = side_by_side(all_text, text_at[:-5])
-    full_text_down = taken(all_text, text_at[-5])
-    full_text_self = side_by_side(all_text, text_at[-4:-1])
-    full_text_mix = taken(all_text, text_at[-1])
-    full_image_up = taken(all_image, image_at[0])
-    full_image_down = taken(all_image, image_at[1])
-    full_image_self = side_by_side(all_image, image_at[2:5])
-    full_image_mix = taken(all_image, image_at[5])
+    first_at = starts(first_pieces + [text_merge])
+    text_at, image_at = starts(text_pieces), starts(image_pieces)
+    all_text = gather(packed_text)
+    all_first = gather_by_exchange(packed_first, sizes)
+    weight_text_query = taken(all_first, first_at[0])
+    weight_image_held = side_by_side(all_first, first_at[1:3])
+    full_text_merge = taken(all_first, first_at[3])[:, :text_width]
 
     text_slots, image_slots = round_up(length, 8), round_up(regions, 8)
 
@@ -377,14 +567,23 @@
     text_keep = text_live.astype(F32).reshape(-1, 1)
     image_keep = image_live.astype(F32).reshape(-1, 1)
 
-    triple_text = pairs_of(project(text_rows, weight_text).astype(BF16))
-    triple_image = pairs_of(project(image_rows, weight_image).astype(BF16))
-    cross_text = rows_of(
-        attend((triple_text, 0), (triple_image, 1), (triple_image, 2), image_fill, inner, HEADS)
-    )
-    cross_image = rows_of(attend((triple_image, 0), (triple_text, 1), (triple_text, 2), text_fill, inner, HEADS))
+    query_text = pairs_of(project(text_rows, weight_text_query).astype(BF16))
+    held_image = pairs_of(project(image_rows, weight_image_held).astype(BF16))
+    mixed_cross = attend((query_text, 0), (held_image, 0), (held_image, 1), image_fill, inner, HEADS)
+    mixed_cross, packed_image = tie(mixed_cross, packed_image)
+    all_image = gather(packed_image)
+    cross_text = rows_of(mixed_cross)
     unit_text_1, rate_text_1 = normed_rows(text_rows.astype(F32) + project(cross_text, full_text_merge))
-    unit_image_1, rate_image_1 = normed_rows(image_rows.astype(F32) + project(cross_image, full_image_merge))
+
+    ups = text_up.shape[1] // text_width
+    full_text_up = side_by_side(all_text, text_at[:ups])
+    full_text_down = taken(all_text, text_at[ups])
+    full_text_self = side_by_side(all_text, text_at[ups + 1 : ups + 4])
+    full_text_mix = taken(all_text, text_at[ups + 4])
+    full = {
+        name: all_text[:, text_at[ups + 5][0] + at, : piece.shape[0]].reshape(-1).astype(F32)
+        for at, (name, piece) in enumerate(zip(VECTOR_NAMES, vectors))
+    }
 
     def forward(unit_1, gain_1, up, bias, down, gain_2, joint, mix, gain_3, fill, keep, heads):
         width = unit_1.shape[1]
@@ -407,28 +606,21 @@
         width = unit_2.shape[1]
         d_third, g_gain_3 = normed_back(unit_3, rate_3, gain_3, d_out.astype(F32) * keep)
         d_branch = d_third.astype(BF16)
-        g_mix = weight_grad(mixed, d_branch).astype(BF16)
         d_mixed = pairs_of(project_back(d_branch, mix).astype(BF16))
         d_triple = attend_back((triple, 0), (triple, 1), (triple, 2), fill, d_mixed, width, heads)
         d_triple = rows_of(jnp.concatenate(d_triple, -1))
-        g_joint = weight_grad(second_low, d_triple).astype(BF16)
         d_second = d_third + project_back(d_triple, joint)
         d_sum, g_gain_2 = normed_back(unit_2, rate_2, gain_2, d_second)
-        return d_sum, g_mix, g_joint, g_gain_2, g_gain_3
+        return d_sum, (mixed, d_branch), (second_low, d_triple), g_gain_2, g_gain_3
 
     def feed_backward(saved, d_sum, unit_1, rate_1, gain_1, up, down):
         first_low, active, slope = saved[:3]
         d_sum_low = d_sum.astype(BF16)
-        g_down = weight_grad(active, d_sum_low).astype(BF16)
         d_hidden = (slope.astype(F32) * project_back(d_sum_low, down)).astype(BF16)
         g_bias = jnp.sum(d_hidden.astype(F32), 0)
-        g_up = weight_grad(first_low, d_hidden).astype(BF16)
         d_first = d_sum + project_back(d_hidden, up)
         d_resid, g_gain_1 = normed_back(unit_1, rate_1, gain_1, d_first)
-        return d_resid, g_up, g_down, g_bias, g_gain_1
-
-    def split_rows(matrix, parts):
-        return [owned_rows(piece, devices) for piece in jnp.split(matrix, parts, 1)]
+        return d_resid, (first_low, d_hidden), (active, d_sum_low), g_bias, g_gain_1
 
     out_text, saved_text = forward(
         unit_text_1,
@@ -458,43 +650,52 @@
     d_resid_text, g_text_up, g_text_down, g_text_bias, g_text_gain_cross = feed_backward(
         saved_text, d_sum_text, unit_text_1, rate_text_1, full["text_gain_cross"], full_text_up, full_text_down
     )
-    ups = text_up.shape[1] // text_width
+    row_down, row_self = text_at[ups][0], text_at[ups + 1][0]
     sum_text = OwnerSum(
-        jnp.concatenate(
-            split_rows(g_text_up, ups)
-            + [owned_rows(g_text_down, devices)]
-            + split_rows(g_text_self, 3)
-            + [owned_rows(g_text_mix, devices)],
-            1,
-        ),
+        [
+            (0, *g_text_up),
+            (row_down, *g_text_down),
+            (row_self, *g_text_self),
+            (text_at[ups + 4][0], *g_text_mix),
+        ],
+        text_at[ups + 4][1],
+        text_width,
         sizes,
     )
     d_resid_text = sum_text.advance(d_resid_text)
 
     d_merge_text = d_resid_text.astype(BF16)
-    g_text_merge = weight_grad(cross_text, d_merge_text).astype(BF16)
     d_heads_text = pairs_of(project_back(d_merge_text, full_text_merge).astype(BF16))
     d_query_text, d_key_image, d_value_image = map(
         rows_of,
-        attend_back((triple_text, 0), (triple_image, 1), (triple_image, 2), image_fill, d_heads_text, inner, HEADS),
-    )
-    g_text_query = weight_grad(text_rows, d_query_text).astype(BF16)
-    g_image_key = weight_grad(image_rows, d_key_image).astype(BF16)
-    g_image_value = weight_grad(image_rows, d_value_image).astype(BF16)
-    unit_image_1 = sum_text.advance(unit_image_1)
+        attend_back((query_text, 0), (held_image, 0), (held_image, 1), image_fill, d_heads_text, inner, HEADS),
+    )
+    row_image, row_text = image_key.shape[0], text_query.shape[0]
     sum_first = OwnerSum(
-        jnp.concatenate(
-            [
-                owned_rows(g_text_query, devices),
-                owned_rows(g_image_key, devices),
-                owned_rows(g_image_value, devices),
-                owned_rows(jnp.pad(g_text_merge, ((0, 0), (0, inner - text_width))), devices),
-            ],
-            1,
-        ),
+        [
+            (0, image_rows, d_key_image),
+            (row_image, image_rows, d_value_image),
+            (2 * row_image, cross_text, d_merge_text),
+            (3 * row_image, text_rows, d_query_text),
+        ],
+        3 * row_image + row_text,
+        inner,
         sizes,
     )
-    unit_image_1 = sum_first.advance(unit_image_1)
+    weight_image_query = taken(all_image, image_at[0])
+    weight_text_held = side_by_side(all_image, image_at[1:3])
+    full_image_merge = taken(all_image, image_at[3])
+    full_image_up = taken(all_image, image_at[4])
+    full_image_down = taken(all_image, image_at[5])
+    full_image_self = side_by_side(all_image, image_at[6:9])
+    full_image_mix = taken(all_image, image_at[9])
+
+    image_rows_2 = sum_text.advance(image_rows)
+    image_rows_2 = sum_first.advance(image_rows_2)
+    query_image = pairs_of(project(image_rows_2, weight_image_query).astype(BF16))
+    held_text = pairs_of(project(text_rows, weight_text_held).astype(BF16))
+    cross_image = rows_of(attend((query_image, 0), (held_text, 0), (held_text, 1), text_fill, inner, HEADS))
+    unit_image_1, rate_image_1 = normed_rows(image_rows.astype(F32) + project(cross_image, full_image_merge))
 
     out_image, saved_image = forward(
         unit_image_1,
@@ -510,7 +711,7 @@
         image_keep,
         IMAGE_HEADS,
     )
-    d_image_out = sum_text.advance(d_image_out, *saved_image)[0]
+    d_image_out, *saved_image = sum_text.advance(d_image_out, *saved_image)
     d_sum_image, g_image_mix, g_image_self, g_image_gain_ffn, g_image_gain_self = self_backward(
         saved_image,
         full["image_gain_ffn"],
@@ -533,29 +734,27 @@
         full_image_down,
     )
     d_resid_image = sum_text.advance(d_resid_image)
+
+    d_merge_image = d_resid_image.astype(BF16)
     sum_image = OwnerSum(
-        jnp.concatenate(
-            [owned_rows(g_image_up, devices), owned_rows(g_image_down, devices)]
-            + split_rows(g_image_self, 3)
-            + [owned_rows(g_image_mix, devices)],
-            1,
-        ),
+        [
+            (0, cross_image, d_merge_image),
+            (row_image, *g_image_up),
+            (2 * row_image, *g_image_down),
+            (3 * row_image, *g_image_self),
+            (6 * row_image, *g_image_mix),
+        ],
+        7 * row_image,
+        image_width,
         sizes,
     )
-    d_resid_image = sum_image.advance(d_resid_image)
-
-    d_merge_image = d_resid_image.astype(BF16)
-    g_image_merge = weight_grad(cross_image, d_merge_image).astype(BF16)
+    d_merge_image = sum_image.advance(d_merge_image)
     d_heads_image = pairs_of(project_back(d_merge_image, full_image_merge).astype(BF16))
     d_query_image, d_key_text, d_value_text = map(
         rows_of,
-        attend_back((triple_image, 0), (triple_text, 1), (triple_text, 2), text_fill, d_heads_image, inner, HEADS),
+        attend_back((query_image, 0), (held_text, 0), (held_text, 1), text_fill, d_heads_image, inner, HEADS),
     )
     d_query_image = sum_first.advance(d_query_image)
-    d_key_text = sum_image.advance(d_key_text)
-    g_image_query = weight_grad(image_rows, d_query_image).astype(BF16)
-    g_text_key = weight_grad(text_rows, d_key_text).astype(BF16)
-    g_text_value = weight_grad(text_rows, d_value_text).astype(BF16)
     g_vectors = (
         g_text_gain_cross,
         g_image_gain_cross,
@@ -566,46 +765,63 @@
         g_text_gain_self,
         g_image_gain_self,
     )
-    g_vector = jnp.concatenate([piece.reshape(devices, -1) for piece in g_vectors], 1).astype(BF16)
-    g_vector = jnp.pad(g_vector[:, None, :], ((0, 0), (0, vector_rows - 1), (0, inner - g_vector.shape[1])))
+    row_vector = 2 * row_text
+    vector_rows = max(len(vectors), 2 * row_image - row_vector)
+    g_vector = jnp.stack(
+        [
+            jnp.pad(owned, ((0, 0), (0, inner - owned.shape[1])))
+            for owned in (piece.astype(BF16).reshape(devices, -1) for piece in g_vectors)
+        ],
+        1,
+    )
+    g_vector = jnp.pad(g_vector, ((0, 0), (0, vector_rows - len(vectors)), (0, 0)))
+    row_query = row_vector + vector_rows
     sum_last = OwnerSum(
-        jnp.concatenate(
-            [
-                owned_rows(g_image_query, devices),
-                owned_rows(g_text_key, devices),
-                owned_rows(g_text_value, devices),
-                owned_rows(g_image_merge, devices),
-                g_vector,
-            ],
-            1,
-        ),
+        [
+            (0, text_rows, d_key_text),
+            (row_text, text_rows, d_value_text),
+            (row_query, image_rows, d_query_image),
+            (row_vector, g_vector),
+        ],
+        row_query + row_image,
+        inner,
         sizes,
     )
-    d_resid_text, d_resid_image = sum_last.advance(d_resid_text, d_resid_image)
-    grad_text = d_resid_text + project_back(
-        jnp.concatenate([d_query_text, d_key_text, d_value_text], 1), weight_text
-    )
-    grad_image = d_resid_image + project_back(
-        jnp.concatenate([d_query_image, d_key_image, d_value_image], 1), weight_image
-    )
+    token = sum_image.advance(d_key_text)
+    token = sum_last.advance(token)
+    d_resid_text, d_resid_image, d_key_text = tie(d_resid_text, d_resid_image, token)
+    grad_text = (
+        d_resid_text
+        + project_back(d_query_text, weight_text_query)
+        + project_back(jnp.concatenate([d_key_text, d_value_text], 1), weight_text_held)
+    )
+    grad_image = (
+        d_resid_image
+        + project_back(d_query_image, weight_image_query)
+        + project_back(jnp.concatenate([d_key_image, d_value_image], 1), weight_image_held)
+    )
+    token = sum_text.advance(d_key_text)
+    for _ in range(2):
+        token = sum_first.advance(token)
+    for _ in range(5):
+        token = sum_last.advance(token)
+        token = sum_image.advance(token)
 
     def owned(total, pieces):
         return [total[start:end] for start, end in starts(pieces)]
 
     done = [one.result() for one in (sum_text, sum_first, sum_image, sum_last)]
-    text_sums = owned(done[0], text_pieces)
-    sum_text_query, sum_image_key, sum_image_value, sum_text_merge = owned(
-        done[1], [text_query, image_key, image_value, text_merge]
-    )
-    image_sums = owned(done[2], image_pieces)
-    sum_image_query, sum_text_key, sum_text_value, sum_image_merge, sum_vector = owned(
-        done[3], [image_query, text_key, text_value, image_merge, vector_block]
-    )
-    owned_vector = {}
-    at = 0
-    for name, piece in zip(VECTOR_NAMES, vectors):
-        owned_vector[name] = sum_vector[0, at : at + piece.shape[0]]
-        at += piece.shape[0]
+    text_sums = owned(done[0], text_pieces[:-1])
+    sum_image_key, sum_image_value, sum_text_merge, sum_text_query = owned(
+        done[1], [image_key, image_value, text_merge, text_query]
+    )
+    image_sums = owned(done[2], image_pieces[3:])
+    sum_text_key, sum_text_value = owned(done[3], [text_key, text_value])
+    sum_vector = done[3][row_vector:row_query]
+    sum_image_query = done[3][row_query:]
+    owned_vector = {
+        name: sum_vector[at, : piece.shape[0]] for at, (name, piece) in enumerate(zip(VECTOR_NAMES, vectors))
+    }
     return (
         pairs_of(out_text)[:, :length],
         pairs_of(out_image)[:, :regions],
@@ -619,21 +835,21 @@
         sum_image_query,
         sum_text_key,
         sum_text_value,
-        sum_image_merge,
+        image_sums[0],
         owned_vector["image_gain_cross"],
-        jnp.concatenate(text_sums[:-5], 1),
+        jnp.concatenate(text_sums[:ups], 1),
         owned_vector["text_bias"],
-        text_sums[-5],
+        text_sums[ups],
         owned_vector["text_gain_ffn"],
-        image_sums[0],
+        image_sums[1],
         owned_vector["image_bias"],
-        image_sums[1],
+        image_sums[2],
         owned_vector["image_gain_ffn"],
-        jnp.concatenate(text_sums[-4:-1], 1),
-        text_sums[-1],
+        jnp.concatenate(text_sums[ups + 1 : ups + 4], 1),
+        text_sums[ups + 4],
         owned_vector["text_gain_self"],
-        jnp.concatenate(image_sums[2:5], 1),
-        image_sums[5],
+        jnp.concatenate(image_sums[3:6], 1),
+        image_sums[6],
         owned_vector["image_gain_self"],
     )
 

time: 795 us -> 661 us (0.83)
  waiting for transfers between devices: 307 us -> 182 us
  Pallas kernels: 39.7 us -> 135 us
  local copies, waits for them, and re-layouts: 177 us -> 115 us
  matrix products: 149 us -> 92.8 us
  starting transfers between devices: 22.5 us -> 40.5 us
  other arithmetic: 77.4 us -> 67.4 us
    all_gather x3 -> x2, waiting for transfers between devices: 167 us -> 0.02 us  [gather(): return lax.all_gather(packed, AXES, axis=0, tiled=False)]
    pallas_call x0 -> x21, Pallas kernels: none -> 97.5 us  [the longest x17 66.1 us: pack_terms(): pl.pallas_call(kernel, grid=grid, in_specs=in_specs, out_specs=[place, pl...]
    ppermute x0 -> x7, waiting for transfers between devices: none -> 81.3 us  [doubled(): lax.ppermute(block, axis, [(at, at ^ 1 << bit) for at in range(count)])]
    dot_general x16 -> x0, matrix products: 48.2 us -> none  [weight_grad(): lax.dot_general(left, right, (((0,), (0,)), ((), ())), preferred_element_...]
    ppermute x28, waiting for transfers between devices: 140 us -> 100 us  [advance(): got = lax.ppermute(away, axis, [(at, at ^ 1 << bit) for at in range(count)])]
    unnamed x317 -> x320, local copies, waits for them, and re-layouts: 79.5 us -> 47 us
    dynamic_slice x4 -> x0, local copies, waits for them, and re-layouts: 21.9 us -> none  [advance(): kept = lax.dynamic_index_in_dim(total, own, place, keepdims=False)]
    convert_element_type x27 -> x31, other arithmetic: 48.7 us -> 27.4 us  [the longest x20 18.6 us: advance(): (kept.astype(F32) + got.astype(F32)).astype(BF16 if self.plan else F32)]
  transfers between devices with their start and end apart: 31 -> 37, of which waited for: 17 -> 23; matrix products, arithmetic and copies ran while one was open for 35% -> 35% of each run, Pallas kernels for 3% -> 16%
where the time goes in v2:
time: 661 us; the launch traced here: 649 us
  waiting for transfers between devices  182 us (28%)
  Pallas kernels  135 us (20%)
  local copies, waits for them, and re-layouts  115 us (17%)
  matrix products  92.8 us (14%)
  other arithmetic  67.4 us (10%)
  starting transfers between devices  40.5 us (6%)
  between operations  16.9 us (3%)
    ppermute x28, waiting for transfers between devices, advance(): got = lax.ppermute(away, axis, [(at, at ^ 1 << bit) for at in range(count)])  100 us
    ppermute x7, waiting for transfers between devices, doubled(): lax.ppermute(block, axis, [(at, at ^ 1 << bit) for at in range(count)])  81.3 us
    pallas_call x17, Pallas kernels, pack_terms(): pl.pallas_call(kernel, grid=grid, in_specs=in_specs, out_specs=[place, pl...  66.1 us
    dot_general x14, matrix products, project_back(): lax.dot_general(left, right, (((1,), (1,)), ((), ())), preferred_element_...  53.8 us
    unnamed x320, local copies, waits for them, and re-layouts  47 us
    dot_general x14, matrix products, project(): return jnp.dot(left, right, preferred_element_type=F32)  39 us
    pallas_call x8, Pallas kernels, attention_call(): pl.pallas_call(kernel, grid=(pairs // together,), in_specs=[spec(array.sh...  37.1 us
    pallas_call x4, Pallas kernels, split_terms(): pl.pallas_call(split_kernel, grid_spec=pltpu.PrefetchScalarGridSpec(num_s...  31.4 us
  transfers between devices with their start and end apart: 37, of which 23 were waited for; matrix products, arithmetic and copies ran while one was open for 35% of the time, Pallas kernels for 16%

profile of v2, /device:TPU:0, one launch (start us, length us, event | category | flops | bytes accessed | tf_op | source)
XLA Modules:
  0.0 648.5 jit_solution(4507791208027122828)
XLA Ops:
  13.5 7.9 %concatenate.64 = bf16[296,768]{1,0:T(8,128)(2,1)} concatenate(bf16[24,768]{1,0:T(8,128)(2,1)S(1)} %get-tuple-element.442, bf16[24,768]{1,0:T(8,128)(2,1)S(1)} %get-tuple-element.441, bf16[24,768]{1,0:T(8,128)(2,1)S(1)} %get-tuple-element.443, bf16[24,768]{1,0:T(8,128)(2,1)S(1)} %get-tuple-element.440, bf16[96,768]{1,0:T(8,128)(2,1)} %param.48, ...), dimensions={0} | concatenate | bytes 909312 | tf_op jit(solution)/shard_map/concatenate | solution.py:519
  26.5 14.5 %collective-permute-done = bf16[120,1024]{1,0:T(8,128)(2,1)S(1)} collective-permute-done((bf16[120,1024]{1,0:T(8,128)(2,1)S(1)}, bf16[120,1024]{1,0:T(8,128)(2,1)S(1)}, u32[]{:S(2)}, u32[]{:S(2)}) %collective-permute-start) | collective-permute-done | bytes 245792 | tf_op jit(solution)/shard_map/ppermute | solution.py:166
  45.0 14.9 %collective-permute-done.1 = bf16[2,120,1024]{2,1,0:T(8,128)(2,1)S(1)} collective-permute-done((bf16[2,120,1024]{2,1,0:T(8,128)(2,1)S(1)}, bf16[2,120,1024]{2,1,0:T(8,128)(2,1)S(1)}, u32[]{:S(2)}, u32[]{:S(2)}) %collective-permute-start.1) | collective-permute-done | bytes 491552 | tf_op jit(solution)/shard_map/ppermute | solution.py:166
  63.6 17.5 %collective-permute-done.4 = bf16[2,2,120,512]{3,2,1,0:T(8,128)(2,1)S(1)} collective-permute-done((bf16[2,2,120,512]{3,2,1,0:T(8,128)(2,1)S(1)}, bf16[2,2,120,512]{3,2,1,0:T(8,128)(2,1)S(1)}, u32[]{:S(2)}, u32[]{:S(2)}) %collective-permute-start.4) | collective-permute-done | bytes 491552 | tf_op jit(solution)/shard_map/ppermute | solution.py:166
  83.5 31.6 %collective-permute-done.5 = bf16[2,2,2,120,512]{4,3,2,1,0:T(8,128)(2,1)S(1)} collective-permute-done((bf16[2,2,2,120,512]{4,3,2,1,0:T(8,128)(2,1)S(1)}, bf16[2,2,2,120,512]{4,3,2,1,0:T(8,128)(2,1)S(1)}, u32[]{:S(2)}, u32[]{:S(2)}) %collective-permute-start.5) | collective-permute-done | bytes 983072 | tf_op jit(solution)/shard_map/ppermute | solution.py:166
  181.5 9.9 %fusion.4 = (bf16[832,3072]{1,0:T(8,128)(2,1)S(1)}, f32[832,3072]{1,0:T(8,128)}) fusion(f32[3072]{0:T(1024)S(1)} %reshape.716, bf16[832,768]{1,0:T(8,128)(2,1)S(1)} %multiply_convert_fusion.3.left_ref, bf16[768,768]{1,0:T(8,128)(2,1)S(1)} %bitcast.447, bf16[768,768]{1,0:T(8,128)(2,1)S(1)} %bitcast.449, bf16[768,768]{1,0:T(8,128)(2,1)S(1)} %bitcast.451, ...), kind=kOutput, calls=%fused_computation.5 | convolution fusion | flops 3970301952 | bytes 21344256 | tf_op jit(solution)/shard_map/dot_general | solution.py:35
  217.1 9.0 %shard_map.503 = (bf16[8,104,768]{2,1,0:T(8,128)(2,1)S(1)}, bf16[8,104,768]{2,1,0:T(8,128)(2,1)S(1)}, bf16[8,104,768]{2,1,0:T(8,128)(2,1)S(1)}) custom-call(bf16[8,104,2304]{2,1,0:T(8,128)(2,1)} %bitcast.314, bf16[8,104,2304]{2,1,0:T(8,128)(2,1)} %bitcast.315, bf16[8,104,2304]{2,1,0:T(8,128)(2,1)} %bitcast.316, ...), custom_call_target="tpu_custom_call" | custom-call | flops 1329070080 | bytes 9371648 | tf_op jit(solution)/shard_map/pallas_call | solution.py:122
  227.8 7.0 %multiply_reduce_fusion.1 = (bf16[768]{0:T(1024)(128)(2,1)}, f32[832]{0:T(1024)S(1)}, f32[832]{0:T(1024)S(1)}, f32[832,768]{1,0:T(8,128)S(1)}) fusion(f32[832,768]{1,0:T(8,128)S(1)} %copy-done.51, f32[832]{0:T(1024)S(1)} %add_rsqrt_fusion.1, f32[832]{0:T(1024)S(1)} %broadcast_multiply_fusion.7, f32[768]{0:T(1024)S(1)} %reshape.717, ...), kind=kOutput, calls=%fused_computation.40 | convolution fusion | flops 2960766720 | bytes 15058432 | tf_op jit(solution)/shard_map/dot_general | solution.py:39
  235.8 13.7 %fusion.106 = (bf16[3072]{0:T(1024)(128)(2,1)}, bf16[832,3072]{1,0:T(8,128)(2,1)}) fusion(bf16[832,768]{1,0:T(8,128)(2,1)S(1)} %get-tuple-element.367.right_ref, bf16[3072,768]{1,0:T(8,128)(2,1)S(1)} %bitcast.421, f32[832,3072]{1,0:T(8,128)} %get-tuple-element.450, f32[3072]{0:T(1024)S(1)} %reshape.716), kind=kOutput, calls=%fused_computation.327 | convolution fusion | flops 3982095360 | bytes 21350400 | tf_op jit(solution)/shard_map/dot_general | solution.py:39
  249.6 8.9 %shard_map.504 = (bf16[2,8,288,768]{3,2,1,0:T(8,128)(2,1)}, bf16[2,8,288,768]{3,2,1,0:T(8,128)(2,1)}) custom-call(bf16[832,768]{1,0:T(8,128)(2,1)S(1)} %multiply_convert_fusion.3.left_ref, bf16[832,3072]{1,0:T(8,128)(2,1)} %get-tuple-element.466.right_ref, s32[1]{0:T(128)} %bitcast.49.core_ref), custom_call_target="tpu_custom_call" | custom-call | flops 3925868544 | bytes 14057472 | tf_op jit(solution)/shard_map/pallas_call | solution.py:288
  258.5 9.7 %shard_map.505 = (bf16[2,8,288,768]{3,2,1,0:T(8,128)(2,1)}, bf16[2,8,288,768]{3,2,1,0:T(8,128)(2,1)}) custom-call(bf16[832,3072]{1,0:T(8,128)(2,1)} %copy-done.80, bf16[832,768]{1,0:T(8,128)(2,1)S(1)} %get-tuple-element.367.right_ref, s32[1]{0:T(128)} %bitcast.49.core_ref, ...), custom_call_target="tpu_custom_call", output_to_operand_aliasing={{0}: (3, {}), {1}: (4, {})} | custom-call | flops 3925868544 | bytes 14057472 | tf_op jit(solution)/shard_map/pallas_call | solution.py:288
  277.4 7.7 %multiply_reduce_fusion.2 = (bf16[768]{0:T(1024)(128)(2,1)S(1)}, f32[832]{0:T(1024)S(1)}, f32[832]{0:T(1024)S(1)}, f32[832,768]{1,0:T(8,128)S(1)}) fusion(f32[832,768]{1,0:T(8,128)S(1)} %copy-done.49, f32[832]{0:T(1024)S(1)} %add_rsqrt_fusion.2, f32[832]{0:T(1024)S(1)} %broadcast_multiply_fusion.8, f32[768]{0:T(1024)S(1)} %reshape.715, ...), kind=kOutput, calls=%fused_computation.41 | convolution fusion | flops 3950491392 | bytes 17516032 | tf_op jit(solution)/shard_map/dot_general | solution.py:39
  316.5 9.4 %shard_map.513 = (bf16[1,2,4,288,384]{4,3,2,1,0:T(8,128)(2,1)S(1)}, bf16[1,2,4,288,384]{4,3,2,1,0:T(8,128)(2,1)S(1)}, bf16[1,4,2,288,384]{4,3,2,1,0:T(8,128)(2,1)S(1)}, bf16[1,4,2,288,384]{4,3,2,1,0:T(8,128)(2,1)}) custom-call(s32[2]{0:T(128)S(1)} %pad_add_fusion.where_ref, bf16[1,2,4,2,288,768]{5,4,3,2,1,0:T(8,128)(2,1)} %bitcast.390, ...), custom_call_target="tpu_custom_call" | custom-call | flops 3538944 | bytes 21233664 | tf_op jit(solution)/shard_map/pallas_call | solution.py:335
  330.1 9.7 %fusion.89 = (bf16[32,32,1024]{2,1,0:T(8,128)(2,1)S(1)}, bf16[32,32,1024]{2,1,0:T(8,128)(2,1)}, bf16[32,32,1024]{2,1,0:T(8,128)(2,1)}, bf16[32,32,1024]{2,1,0:T(...) fusion(bf16[32,304,1024]{2,1,0:T(8,128)(2,1)} %bitcast.395), kind=kLoop, calls=%fused_computation.310 | loop fusion | bytes 33554432 | tf_op jit(solution)/shard_map/slice | solution.py:531
  405.9 15.3 %collective-permute-done.10 = bf16[2,2,288,384]{3,2,0,1:T(8,128)(2,1)S(1)} collective-permute-done((bf16[2,2,288,384]{3,2,0,1:T(8,128)(2,1)}, bf16[2,2,288,384]{3,2,0,1:T(8,128)(2,1)S(1)}, u32[]{:S(2)}, u32[]{:S(2)}) %collective-permute-start.10) | collective-permute-done | bytes 884768 | tf_op jit(solution)/shard_map/ppermute | solution.py:400
  459.2 9.3 %collective-permute-done.13 = bf16[2,2,2,120,512]{4,3,1,2,0:T(8,128)(2,1)} collective-permute-done((bf16[2,2,2,120,512]{4,3,1,2,0:T(8,128)(2,1)}, bf16[2,2,2,120,512]{4,3,1,2,0:T(8,128)(2,1)}, u32[]{:S(2)}, u32[]{:S(2)}) %collective-permute-start.13) | collective-permute-done | bytes 983072 | tf_op jit(solution)/shard_map/ppermute | solution.py:400
  480.7 7.2 %collective-permute-done.16 = bf16[2,2,120,512]{3,2,0,1:T(8,128)(2,1)} collective-permute-done((bf16[2,2,120,512]{3,2,0,1:T(8,128)(2,1)S(1)}, bf16[2,2,120,512]{3,2,0,1:T(8,128)(2,1)}, u32[]{:S(2)}, u32[]{:S(2)}) %collective-permute-start.16) | collective-permute-done | bytes 491552 | tf_op jit(solution)/shard_map/ppermute | solution.py:400
  489.4 9.7 %shard_map.528 = (bf16[1,2,4,224,512]{4,3,2,1,0:T(8,128)(2,1)S(1)}, bf16[1,2,4,224,512]{4,3,2,1,0:T(8,128)(2,1)S(1)}, bf16[1,4,2,224,512]{4,3,2,1,0:T(8,128)(2,1)S(1)}, bf16[1,4,2,224,512]{4,3,2,1,0:T(8,128)(2,1)}) custom-call(s32[2]{0:T(128)S(1)} %pad_add_fusion.where_ref, bf16[1,2,4,2,224,1024]{5,4,3,2,1,0:T(8,128)(2,1)} %bitcast.389, ...), custom_call_target="tpu_custom_call" | custom-call | flops 3670016 | bytes 22020096 | tf_op jit(solution)/shard_map/pallas_call | solution.py:335
  532.1 9.0 %collective-permute-done.28 = bf16[2,2,2,224,512]{4,3,1,2,0:T(8,128)(2,1)} collective-permute-done((bf16[2,2,2,224,512]{4,3,1,2,0:T(8,128)(2,1)}, bf16[2,2,2,224,512]{4,3,1,2,0:T(8,128)(2,1)}, u32[]{:S(2)}, u32[]{:S(2)}) %collective-permute-start.28) | collective-permute-done | bytes 1835040 | tf_op jit(solution)/shard_map/ppermute | solution.py:400
  558.9 8.0 %collective-permute-done.30 = bf16[2,2,224,512]{3,2,0,1:T(8,128)(2,1)S(1)} collective-permute-done((bf16[2,2,224,512]{3,2,0,1:T(8,128)(2,1)S(1)}, bf16[2,2,224,512]{3,2,0,1:T(8,128)(2,1)S(1)}, u32[]{:S(2)}, u32[]{:S(2)}) %collective-permute-start.30) | collective-permute-done | bytes 917536 | tf_op jit(solution)/shard_map/ppermute | solution.py:400
  593.9 8.7 %collective-permute-done.22 = bf16[2,2,2,96,512]{4,3,1,2,0:T(8,128)(2,1)S(1)} collective-permute-done((bf16[2,2,2,96,512]{4,3,1,2,0:T(8,128)(2,1)S(1)}, bf16[2,2,2,96,512]{4,3,1,2,0:T(8,128)(2,1)S(1)}, u32[]{:S(2)}, u32[]{:S(2)}) %collective-permute-start.22) | collective-permute-done | bytes 786464 | tf_op jit(solution)/shard_map/ppermute | solution.py:400
  609.0 7.1 %collective-permute-done.33 = bf16[224,1024]{1,0:T(8,128)(2,1)S(1)} collective-permute-done((bf16[224,1024]{1,0:T(8,128)(2,1)S(1)}, bf16[224,1024]{1,0:T(8,128)(2,1)S(1)}, u32[]{:S(2)}, u32[]{:S(2)}) %collective-permute-start.33) | collective-permute-done | bytes 458784 | tf_op jit(solution)/shard_map/ppermute | solution.py:400
  617.5 9.8 %collective-permute-done.26 = bf16[2,96,1024]{2,1,0:T(8,128)(2,1)S(1)} collective-permute-done((bf16[2,96,1024]{2,1,0:T(8,128)(2,1)S(1)}, bf16[2,96,1024]{2,1,0:T(8,128)(2,1)S(1)}, u32[]{:S(2)}, u32[]{:S(2)}) %collective-permute-start.26) | collective-permute-done | bytes 393248 | tf_op jit(solution)/shard_map/ppermute | solution.py:400
  629.2 9.1 %collective-permute-done.27 = bf16[96,1024]{1,0:T(8,128)(2,1)S(1)} collective-permute-done((bf16[96,1024]{1,0:T(8,128)(2,1)S(1)}, bf16[96,1024]{1,0:T(8,128)(2,1)S(1)}, u32[]{:S(2)}, u32[]{:S(2)}) %collective-permute-start.27) | collective-permute-done | bytes 196640 | tf_op jit(solution)/shard_map/ppermute | solution.py:400
  (621 shorter events, 367.0 us)
Async XLA Ops:
  7.3 158.2 %all-gather.5.cloned.1.call-start = ((), (), s32[]{:S(2)}) async-start(), calls=%async_computation | async-start | bytes 15003648 | tf_op jit(solution)/shard_map/all_gather | solution.py:156
  21.5 308.7 %all-gather.7.cloned.1.call-start = ((), (), s32[]{:S(2)}) async-start(), calls=%async_computation.1 | async-start | bytes 20545536 | tf_op jit(solution)/shard_map/all_gather | solution.py:156
  60.1 20.9 %collective-permute-start.4 = (bf16[2,2,120,512]{3,2,1,0:T(8,128)(2,1)S(1)}, bf16[2,2,120,512]{3,2,1,0:T(8,128)(2,1)S(1)}, u32[]{:S(2)}, u32[]{:S(2)}) collective-permute-start(bf16[2,2,120,512]{3,2,1,0:T(8,128)(2,1)S(1)} %get-tuple-element.407), channel_id=1, source_target_pairs={{0,1},{1,0},{2,3},{3,2},{4,5},{5,4},{6,7},{7,6},{8,9},{9,8},{10,11... | collective-permute-start | bytes 1474568 | tf_op jit(solution)/shard_map/ppermute | solution.py:166
  61.9 20.9 %collective-permute-start.2 = (bf16[2,2,120,512]{3,2,1,0:T(8,128)(2,1)S(1)}, bf16[2,2,120,512]{3,2,1,0:T(8,128)(2,1)S(1)}, u32[]{:S(2)}, u32[]{:S(2)}) collective-permute-start(bf16[2,2,120,512]{3,2,1,0:T(8,128)(2,1)S(1)} %get-tuple-element.406), channel_id=1, source_target_pairs={{0,16},{8,24},{16,0},{24,8},{1,17},{9,25},{17,1},{25,9},{2,18},{10... | collective-permute-start | bytes 1474568 | tf_op jit(solution)/shard_map/ppermute | solution.py:166
  81.2 33.9 %collective-permute-start.5 = (bf16[2,2,2,120,512]{4,3,2,1,0:T(8,128)(2,1)S(1)}, bf16[2,2,2,120,512]{4,3,2,1,0:T(8,128)(2,1)S(1)}, u32[]{:S(2)}, u32[]{:S(2)}) collective-permute-start(bf16[2,2,2,120,512]{4,3,2,1,0:T(8,128)(2,1)S(1)} %pad_maximum_fusion.22), channel_id=1, source_target_pairs={{0,16},{8,24},{16,0},{24,8},{1,17},{9,25},{17,1},{25,9},{2,18},{10... | collective-permute-start | bytes 2949128 | tf_op jit(solution)/shard_map/ppermute | solution.py:166
  82.9 35.2 %collective-permute-start.3 = (bf16[2,2,2,120,512]{4,3,2,1,0:T(8,128)(2,1)S(1)}, bf16[2,2,2,120,512]{4,3,2,1,0:T(8,128)(2,1)S(1)}, u32[]{:S(2)}, u32[]{:S(2)}) collective-permute-start(bf16[2,2,2,120,512]{4,3,2,1,0:T(8,128)(2,1)S(1)} %pad_maximum_fusion.21), channel_id=1, source_target_pairs={{0,1},{1,0},{2,3},{3,2},{4,5},{5,4},{6,7},{7,6},{8,9},{9,8},{10,11... | collective-permute-start | bytes 2949128 | tf_op jit(solution)/shard_map/ppermute | solution.py:166
  287.2 29.2 %collective-permute-start.7 = (bf16[2,8,288,768]{3,2,1,0:T(8,128)(2,1)}, bf16[2,8,288,768]{3,2,1,0:T(8,128)(2,1)}, u32[]{:S(2)}, u32[]{:S(2)}) collective-permute-start(bf16[2,8,288,768]{3,2,1,0:T(8,128)(2,1)} %get-tuple-element.207), channel_id=1, source_target_pairs={{0,8},{8,0},{16,24},{24,16},{1,9},{9,1},{17,25},{25,17},{2,10},{10... | collective-permute-start | bytes 21233672 | tf_op jit(solution)/shard_map/ppermute | solution.py:400
  327.3 42.4 %collective-permute-start.8 = (bf16[2,2,2,288,384]{4,3,1,2,0:T(8,128)(2,1)}, bf16[2,2,2,288,384]{4,3,1,2,0:T(8,128)(2,1)}, u32[]{:S(2)}, u32[]{:S(2)}) collective-permute-start(bf16[2,2,2,288,384]{4,3,1,2,0:T(8,128)(2,1)} %copy.224), channel_id=1, source_target_pairs={{0,1},{1,0},{2,3},{3,2},{4,5},{5,4},{6,7},{7,6},{8,9},{9,8},{10,11... | collective-permute-start | bytes 5308424 | tf_op jit(solution)/shard_map/ppermute | solution.py:400
  329.8 40.6 %collective-permute-start.9 = (bf16[2,2,2,288,384]{4,3,0,1,2:T(8,128)(2,1)}, bf16[2,2,2,288,384]{4,3,0,1,2:T(8,128)(2,1)}, u32[]{:S(2)}, u32[]{:S(2)}) collective-permute-start(bf16[2,2,2,288,384]{4,3,0,1,2:T(8,128)(2,1)} %copy.225), channel_id=1, source_target_pairs={{0,16},{8,24},{16,0},{24,8},{1,17},{9,25},{17,1},{25,9},{2,18},{10... | collective-permute-start | bytes 5308424 | tf_op jit(solution)/shard_map/ppermute | solution.py:400
  330.1 62.8 %collective-permute-start.12 = (bf16[2,8,120,1024]{3,2,1,0:T(8,128)(2,1)}, bf16[2,8,120,1024]{3,2,1,0:T(8,128)(2,1)}, u32[]{:S(2)}, u32[]{:S(2)}) collective-permute-start(bf16[2,8,120,1024]{3,2,1,0:T(8,128)(2,1)} %get-tuple-element.235), channel_id=1, source_target_pairs={{0,8},{8,0},{16,24},{24,16},{1,9},{9,1},{17,25},{25,17},{2,10},{10... | collective-permute-start | bytes 11796488 | tf_op jit(solution)/shard_map/ppermute | solution.py:400
  399.6 21.6 %collective-permute-start.10 = (bf16[2,2,288,384]{3,2,0,1:T(8,128)(2,1)}, bf16[2,2,288,384]{3,2,0,1:T(8,128)(2,1)S(1)}, u32[]{:S(2)}, u32[]{:S(2)}) collective-permute-start(bf16[2,2,288,384]{3,2,0,1:T(8,128)(2,1)} %dynamic-slice_bitcast_fusion.3), channel_id=1, source_target_pairs={{0,16},{8,24},{16,0},{24,8},{1,17},{9,25},{17,1},{25,9},{2,18},{10... | collective-permute-start | bytes 2654216 | tf_op jit(solution)/shard_map/ppermute | solution.py:400
  400.7 22.0 %collective-permute-start.11 = (bf16[2,2,288,384]{3,2,0,1:T(8,128)(2,1)}, bf16[2,2,288,384]{3,2,0,1:T(8,128)(2,1)S(1)}, u32[]{:S(2)}, u32[]{:S(2)}) collective-permute-start(bf16[2,2,288,384]{3,2,0,1:T(8,128)(2,1)} %dynamic-slice_bitcast_fusion.2), channel_id=1, source_target_pairs={{0,1},{1,0},{2,3},{3,2},{4,5},{5,4},{6,7},{7,6},{8,9},{9,8},{10,11... | collective-permute-start | bytes 2654216 | tf_op jit(solution)/shard_map/ppermute | solution.py:400
  442.8 46.6 %collective-permute-start.15 = (bf16[2,8,224,1024]{3,2,1,0:T(8,128)(2,1)}, bf16[2,8,224,1024]{3,2,1,0:T(8,128)(2,1)}, u32[]{:S(2)}, u32[]{:S(2)}) collective-permute-start(bf16[2,8,224,1024]{3,2,1,0:T(8,128)(2,1)} %get-tuple-element.288), channel_id=1, source_target_pairs={{0,8},{8,0},{16,24},{24,16},{1,9},{9,1},{17,25},{25,17},{2,10},{10... | collective-permute-start | bytes 22020104 | tf_op jit(solution)/shard_map/ppermute | solution.py:400
  443.9 24.5 %collective-permute-start.13 = (bf16[2,2,2,120,512]{4,3,1,2,0:T(8,128)(2,1)}, bf16[2,2,2,120,512]{4,3,1,2,0:T(8,128)(2,1)}, u32[]{:S(2)}, u32[]{:S(2)}) collective-permute-start(bf16[2,2,2,120,512]{4,3,1,2,0:T(8,128)(2,1)} %copy.230), channel_id=1, source_target_pairs={{0,1},{1,0},{2,3},{3,2},{4,5},{5,4},{6,7},{7,6},{8,9},{9,8},{10,11... | collective-permute-start | bytes 2949128 | tf_op jit(solution)/shard_map/ppermute | solution.py:400
  445.9 24.2 %collective-permute-start.14 = (bf16[2,2,2,120,512]{4,3,0,1,2:T(8,128)(2,1)}, bf16[2,2,2,120,512]{4,3,0,1,2:T(8,128)(2,1)}, u32[]{:S(2)}, u32[]{:S(2)}) collective-permute-start(bf16[2,2,2,120,512]{4,3,0,1,2:T(8,128)(2,1)} %copy.231), channel_id=1, source_target_pairs={{0,16},{8,24},{16,0},{24,8},{1,17},{9,25},{17,1},{25,9},{2,18},{10... | collective-permute-start | bytes 2949128 | tf_op jit(solution)/shard_map/ppermute | solution.py:400
  500.6 40.5 %collective-permute-start.28 = (bf16[2,2,2,224,512]{4,3,1,2,0:T(8,128)(2,1)}, bf16[2,2,2,224,512]{4,3,1,2,0:T(8,128)(2,1)}, u32[]{:S(2)}, u32[]{:S(2)}) collective-permute-start(bf16[2,2,2,224,512]{4,3,1,2,0:T(8,128)(2,1)} %copy.240), channel_id=1, source_target_pairs={{0,1},{1,0},{2,3},{3,2},{4,5},{5,4},{6,7},{7,6},{8,9},{9,8},{10,11... | collective-permute-start | bytes 5505032 | tf_op jit(solution)/shard_map/ppermute | solution.py:400
  503.0 40.2 %collective-permute-start.29 = (bf16[2,2,2,224,512]{4,3,0,1,2:T(8,128)(2,1)}, bf16[2,2,2,224,512]{4,3,0,1,2:T(8,128)(2,1)}, u32[]{:S(2)}, u32[]{:S(2)}) collective-permute-start(bf16[2,2,2,224,512]{4,3,0,1,2:T(8,128)(2,1)} %copy.241), channel_id=1, source_target_pairs={{0,16},{8,24},{16,0},{24,8},{1,17},{9,25},{17,1},{25,9},{2,18},{10... | collective-permute-start | bytes 5505032 | tf_op jit(solution)/shard_map/ppermute | solution.py:400
  523.9 28.4 %collective-permute-start.18 = (bf16[2,288,768]{2,1,0:T(8,128)(2,1)}, bf16[2,288,768]{2,1,0:T(8,128)(2,1)}, u32[]{:S(2)}, u32[]{:S(2)}) collective-permute-start(bf16[2,288,768]{2,1,0:T(8,128)(2,1)} %fusion.52), channel_id=1, source_target_pairs={{0,2},{1,3},{2,0},{3,1},{4,6},{5,7},{6,4},{7,5},{8,10},{9,11},{10,... | collective-permute-start | bytes 2654216 | tf_op jit(solution)/shard_map/ppermute | solution.py:400
  532.0 46.8 %collective-permute-start.21 = (bf16[2,8,96,1024]{3,2,1,0:T(8,128)(2,1)S(1)}, bf16[2,8,96,1024]{3,2,1,0:T(8,128)(2,1)S(1)}, u32[]{:S(2)}, u32[]{:S(2)}) collective-permute-start(bf16[2,8,96,1024]{3,2,1,0:T(8,128)(2,1)S(1)} %get-tuple-element.313), channel_id=1, source_target_pairs={{0,8},{8,0},{16,24},{24,16},{1,9},{9,1},{17,25},{25,17},{2,10},{10... | collective-permute-start | bytes 9437192 | tf_op jit(solution)/shard_map/ppermute | solution.py:400
  547.6 19.3 %collective-permute-start.30 = (bf16[2,2,224,512]{3,2,0,1:T(8,128)(2,1)S(1)}, bf16[2,2,224,512]{3,2,0,1:T(8,128)(2,1)S(1)}, u32[]{:S(2)}, u32[]{:S(2)}) collective-permute-start(bf16[2,2,224,512]{3,2,0,1:T(8,128)(2,1)S(1)} %dynamic-slice_bitcast_fusion.1), channel_id=1, source_target_pairs={{0,16},{8,24},{16,0},{24,8},{1,17},{9,25},{17,1},{25,9},{2,18},{10... | collective-permute-start | bytes 2752520 | tf_op jit(solution)/shard_map/ppermute | solution.py:400
  549.3 19.0 %collective-permute-start.31 = (bf16[2,2,224,512]{3,2,0,1:T(8,128)(2,1)S(1)}, bf16[2,2,224,512]{3,2,0,1:T(8,128)(2,1)S(1)}, u32[]{:S(2)}, u32[]{:S(2)}) collective-permute-start(bf16[2,2,224,512]{3,2,0,1:T(8,128)(2,1)S(1)} %dynamic-slice_bitcast_fusion), channel_id=1, source_target_pairs={{0,1},{1,0},{2,3},{3,2},{4,5},{5,4},{6,7},{7,6},{8,9},{9,8},{10,11... | collective-permute-start | bytes 2752520 | tf_op jit(solution)/shard_map/ppermute | solution.py:400
  553.9 24.9 %collective-permute-start.34 = (bf16[288,768]{1,0:T(8,128)(2,1)S(1)}, bf16[288,768]{1,0:T(8,128)(2,1)S(1)}, u32[]{:S(2)}, u32[]{:S(2)}) collective-permute-start(bf16[288,768]{1,0:T(8,128)(2,1)S(1)} %dynamic-slice_bitcast_fusion.7), channel_id=1, source_target_pairs={{0,4},{1,5},{2,6},{3,7},{4,0},{5,1},{6,2},{7,3},{8,12},{9,13},{10,... | collective-permute-start | bytes 1327112 | tf_op jit(solution)/shard_map/ppermute | solution.py:400
  569.0 23.5 %collective-permute-start.32 = (bf16[2,224,1024]{2,1,0:T(8,128)(2,1)S(1)}, bf16[2,224,1024]{2,1,0:T(8,128)(2,1)S(1)}, u32[]{:S(2)}, u32[]{:S(2)}) collective-permute-start(bf16[2,224,1024]{2,1,0:T(8,128)(2,1)S(1)} %fusion.46), channel_id=1, source_target_pairs={{0,2},{1,3},{2,0},{3,1},{4,6},{5,7},{6,4},{7,5},{8,10},{9,11},{10,... | collective-permute-start | bytes 2752520 | tf_op jit(solution)/shard_map/ppermute | solution.py:400
  592.9 23.2 %collective-permute-start.33 = (bf16[224,1024]{1,0:T(8,128)(2,1)S(1)}, bf16[224,1024]{1,0:T(8,128)(2,1)S(1)}, u32[]{:S(2)}, u32[]{:S(2)}) collective-permute-start(bf16[224,1024]{1,0:T(8,128)(2,1)S(1)} %dynamic-slice_bitcast_fusion.6), channel_id=1, source_target_pairs={{0,4},{1,5},{2,6},{3,7},{4,0},{5,1},{6,2},{7,3},{8,12},{9,13},{10,... | collective-permute-start | bytes 1376264 | tf_op jit(solution)/shard_map/ppermute | solution.py:400
  (161 other events, 1292.4 us)
Sparse Core Ops, SparseCore 0:
  21.6 128.8 all-gather.4
  155.7 129.0 all-gather.6

commit v3 on v2

--- a/solution.py
+++ b/solution.py
@@ -45,6 +45,31 @@
 
 def round_up(size, step):
     return -(-size // step) * step
+
+
+def takes(microseconds):
+    return pl.CostEstimate(flops=0, bytes_accessed=int(3.2e6 * microseconds), transcendentals=0)
+
+
+class Order:
+    last = []
+
+
+def ordered_call(kernel, arrays, in_specs, **rest):
+    after = [one for one in Order.last if all(one is not array for array in arrays)]
+    given = len(arrays)
+
+    def body(*refs):
+        kernel(*refs[:given], *refs[given + len(after) :])
+
+    out = pl.pallas_call(
+        body,
+        in_specs=list(in_specs) + [pl.BlockSpec(memory_space=pl.ANY)] * len(after),
+        compiler_params=pltpu.CompilerParams(vmem_limit_bytes=VMEM_BYTES),
+        **rest,
+    )(*arrays, *after)
+    Order.last = [out[0] if isinstance(out, (list, tuple)) else out]
+    return out
 
 
 def stack_halves(rows):
@@ -110,32 +135,29 @@
         d_queries_ref[p, :, b] = (join_halves(rows) if split else rows).astype(BF16)
 
 
-def attention_call(kernel, together, inputs, outputs, flops):
+def attention_call(kernel, together, inputs, outputs, microseconds):
     pairs = inputs[0][0].shape[0]
     together = math.gcd(pairs, together)
 
     def spec(rows, width, column):
         return pl.BlockSpec((together, rows, width), lambda step: (step, 0, column))
 
-    moved = sum(pairs * array.shape[1] * width * array.dtype.itemsize for array, width, _ in inputs)
-    moved += sum(pairs * rows * width * 2 for rows, width in outputs)
-    return pl.pallas_call(
+    return ordered_call(
         kernel,
+        [array for array, _, _ in inputs],
+        [spec(array.shape[1], width, column) for array, width, column in inputs],
         grid=(pairs // together,),
-        in_specs=[spec(array.shape[1], width, column) for array, width, column in inputs],
         out_specs=[spec(rows, width, 0) for rows, width in outputs],
         out_shape=[jax.ShapeDtypeStruct((pairs, rows, width), BF16) for rows, width in outputs],
-        compiler_params=pltpu.CompilerParams(vmem_limit_bytes=VMEM_BYTES),
-        cost_estimate=pl.CostEstimate(flops=flops, bytes_accessed=moved, transcendentals=0),
-    )(*[array for array, _, _ in inputs])
+        cost_estimate=takes(microseconds),
+    )
 
 
 def attend(queries, keys, values, fill, width, heads):
     pairs, count = queries[0].shape[:2]
     inputs = [(array, width, column) for array, column in (queries, keys, values)] + [(fill, LANES, 0)]
-    flops = 4 * pairs * count * keys[0].shape[1] * max(width, heads * LANES)
     kernel = functools.partial(attend_kernel, width // heads)
-    return attention_call(kernel, 4, inputs, [(count, width)], flops)[0]
+    return attention_call(kernel, 4, inputs, [(count, width)], 4)[0]
 
 
 def attend_back(queries, keys, values, fill, d_mixed, width, heads):
@@ -143,9 +165,8 @@
     inputs = [(array, width, column) for array, column in (queries, keys, values)]
     inputs += [(fill, LANES, 0), (d_mixed, width, 0)]
     keyed = keys[0].shape[1]
-    flops = 10 * pairs * count * keyed * max(width, heads * LANES)
     kernel = functools.partial(attend_back_kernel, width // heads)
-    return attention_call(kernel, 2, inputs, [(count, width), (keyed, width), (keyed, width)], flops)
+    return attention_call(kernel, 2, inputs, [(count, width), (keyed, width), (keyed, width)], 7)
 
 
 def tie(*values):
@@ -156,30 +177,187 @@
     return lax.all_gather(packed, AXES, axis=0, tiled=False)
 
 
-def gather_by_exchange(packed, sizes):
-    core, rows, columns, rest = mesh_axes_bits(sizes)
+def in_vmem(kernel, arrays, shapes, where):
+    vmem, scalar = pl.BlockSpec(memory_space=pltpu.VMEM), pl.BlockSpec(memory_space=pltpu.SMEM)
+    return ordered_call(
+        kernel,
+        [jnp.stack(where).astype(jnp.int32), *arrays],
+        [scalar] + [vmem] * len(arrays),
+        out_specs=[vmem] * len(shapes),
+        out_shape=[jax.ShapeDtypeStruct(shape, BF16) for shape in shapes],
+        cost_estimate=takes(3),
+    )
+
+
+def bit_of(which):
+    return (lax.axis_index(which[0]) >> which[1]) & 1
+
+
+def exchange(block, which):
+    axis, bit = which
+    return lax.ppermute(block, axis, [(at, at ^ (1 << bit)) for at in range(lax.axis_size(axis))])
+
+
+def pack_kernel(pieces, *refs):
+    out_ref = refs[-1]
+    width = out_ref.shape[1]
+    for source, column, row in pieces:
+        wide = min(width, refs[source].shape[1] - column)
+        out_ref[row : row + refs[source].shape[0], :wide] = refs[source][:, column : column + wide]
+
+
+def pack_rows(arrays, width):
+    arrays = [array[None, :] if array.ndim == 1 else array for array in arrays]
+    pieces, row = [], 0
+    for source, array in enumerate(arrays):
+        for column in range(0, array.shape[1], width):
+            pieces.append((source, column, row))
+            row += array.shape[0]
+    if any(array.shape[0] % 8 and array.shape[0] > 1 for array in arrays):
+        blocks = [arrays[source][:, column : column + width] for source, column, _ in pieces]
+        return jnp.concatenate([jnp.pad(one, ((0, 0), (0, width - one.shape[1]))) for one in blocks], 0)
+    return ordered_call(
+        functools.partial(pack_kernel, pieces),
+        arrays,
+        [pl.BlockSpec(array.shape, lambda step: (0, 0)) for array in arrays],
+        grid=(1,),
+        out_specs=pl.BlockSpec((row, width), lambda step: (0, 0)),
+        out_shape=jax.ShapeDtypeStruct((row, width), BF16),
+        cost_estimate=takes(1),
+    )
+
+
+def copy_kernel(pieces, *refs):
+    out_ref, done = refs[-2:]
+    width = out_ref.shape[1]
+    copies = []
+    for at, (source, column, row) in enumerate(pieces):
+        rows = refs[source].shape[0]
+        copies.append(
+            pltpu.make_async_copy(
+                refs[source].at[:, column : column + width], out_ref.at[row : row + rows, :], done.at[at]
+            )
+        )
+    for one in copies:
+        one.start()
+    for one in copies:
+        one.wait()
+
+
+def copy_rows(arrays, width):
+    pieces, row = [], 0
+    for source, array in enumerate(arrays):
+        for column in range(0, array.shape[1], width):
+            pieces.append((source, column, row))
+            row += array.shape[0]
+    if any(array.shape[0] % 8 for array in arrays):
+        return jnp.concatenate([arrays[source][:, column : column + width] for source, column, _ in pieces], 0)
+    anywhere = pl.BlockSpec(memory_space=pl.ANY)
+    return ordered_call(
+        functools.partial(copy_kernel, pieces),
+        arrays,
+        [anywhere] * len(arrays),
+        out_specs=anywhere,
+        out_shape=jax.ShapeDtypeStruct((row, width), BF16),
+        scratch_shapes=[pltpu.SemaphoreType.DMA((len(pieces),))],
+        cost_estimate=takes(2),
+    )
+
+
+def join_kernel(count, where_ref, *refs):
+    outs = refs[2 * count :]
+    shares = len(outs) // count
+    for part in range(count):
+        own, (block_ref, got_ref) = where_ref[part], refs[2 * part : 2 * part + 2]
+        for share in range(shares):
+            out_ref = outs[part * shares + share]
+            width = out_ref.shape[-1]
+            columns = slice(share * width, (share + 1) * width)
+            for before in range(block_ref.shape[0]):
+                out_ref[before, own] = block_ref[before, :, :, columns]
+                out_ref[before, 1 - own] = got_ref[before, :, :, columns]
+
+
+def joined(pairs, shares=1):
+    arrays, shapes, where, news = [], [], [], []
+    for block, got, have, which in pairs:
+        new = [one for one in which[1] if one in have or one == which[0]]
+        place = new.index(which[0])
+        before, behind = 1 << place, 1 << (len(have) - place)
+        rows, width = block.shape[-2:]
+        arrays += [one.reshape(before, behind, rows, width) for one in (block, got)]
+        shapes += [(before, 2, behind, rows, width // shares)] * shares
+        where.append(bit_of(which[0]))
+        news.append(new)
+    outs = in_vmem(functools.partial(join_kernel, len(pairs)), arrays, shapes, where)
+    return [
+        (out.reshape((2,) * len(news[at // shares]) + out.shape[-2:]), news[at // shares])
+        for at, out in enumerate(outs)
+    ]
+
+
+def unpack_kernel(pieces, own_ref, *refs):
+    parts, outs = refs[: len(refs) - len(pieces)], refs[len(refs) - len(pieces) :]
+    shares = len(parts) // 2
+    for out_ref, firsts in zip(outs, pieces):
+        rows = out_ref.shape[3]
+        for source in range(2):
+            core = own_ref[0] if source == 0 else 1 - own_ref[0]
+            at = 0
+            for first in firsts:
+                for part_ref in parts[source * shares : (source + 1) * shares]:
+                    width = part_ref.shape[-1]
+                    out_ref[0, core, :, :, at : at + width] = part_ref[0, :, first : first + rows, :]
+                    at += width
+
+
+def gather_weights(pieces, vectors, sizes, meanwhile):
+    core, y_bits, x_bits, z_bits = mesh_axes_bits(sizes)
     order = mesh_bits(sizes)
-
-    def doubled(block, have, which):
-        axis, bit = which
-        count = lax.axis_size(axis)
-        got = lax.ppermute(block, axis, [(at, at ^ (1 << bit)) for at in range(count)])
-        first = ((lax.axis_index(axis) >> bit) & 1) == 0
-        have = sorted(have + [which], key=order.index)
-        lower, upper = jnp.where(first, block, got), jnp.where(first, got, block)
-        return jnp.stack([lower, upper], have.index(which)), have
-
-    block, have = packed, []
-    for which in reversed(rest):
-        block, have = doubled(block, have, which)
-    width = packed.shape[1]
-    halves = [(block[..., : width // 2], have), (block[..., width // 2 :], have)]
-    for steps in zip(rows + columns, columns + rows):
-        halves = [doubled(block, have, which) for (block, have), which in zip(halves, steps)]
-    block, have = jnp.concatenate([halves[0][0], halves[1][0]], -1), halves[0][1]
-    for which in core:
-        block, have = doubled(block, have, which)
-    return block.reshape((-1,) + packed.shape)
+    shards = [shard for group in pieces for shard in group]
+    width = shards[0].shape[1]
+    packed = pack_rows(shards + list(vectors), width)
+    if not sizes["aligned"] or len(core) != 1 or len(x_bits) != len(y_bits) or not z_bits:
+        meanwhile()
+        gathered, at, out = gather(packed), 0, []
+        for group in pieces:
+            blocks = []
+            for shard in group:
+                blocks.append(whole(gathered[:, at : at + shard.shape[0]]))
+                at += shard.shape[0]
+            out.append(jnp.concatenate(blocks, 1))
+        return out + [whole(gathered[:, at:])]
+    meanwhile()
+    parts = [(packed, [])]
+    for step, which in enumerate(reversed(z_bits)):
+        block, have = parts[0]
+        parts = joined([(block, exchange(block, which), have, (which, order))], 2 if step == len(z_bits) - 1 else 1)
+    for steps in zip(y_bits + x_bits, x_bits + y_bits):
+        flying = [(block, exchange(block, which), have, (which, order)) for (block, have), which in zip(parts, steps)]
+        parts = joined(flying)
+    groups, others, rows = sizes["gx"] // 2, sizes["gy"], packed.shape[0]
+    halves = [block.reshape(groups, others, rows, width // 2) for block, _ in parts]
+    halves += [exchange(block, core[0]) for block in halves]
+    firsts, shapes, at = [], [], 0
+    for group in pieces:
+        firsts.append([])
+        for shard in group:
+            firsts[-1].append(at)
+            at += shard.shape[0]
+        shapes.append((groups, 2, others, group[0].shape[0], width * len(group)))
+    firsts.append([at])
+    shapes.append((groups, 2, others, len(vectors), width))
+    out = ordered_call(
+        functools.partial(unpack_kernel, firsts),
+        [bit_of(core[0]).astype(jnp.int32).reshape(1), *halves],
+        [pl.BlockSpec(memory_space=pltpu.SMEM)]
+        + [pl.BlockSpec((1, others, rows, width // 2), lambda step: (step, 0, 0, 0))] * 4,
+        grid=(groups,),
+        out_specs=[pl.BlockSpec((1,) + shape[1:], lambda step: (step, 0, 0, 0, 0)) for shape in shapes],
+        out_shape=[jax.ShapeDtypeStruct(shape, BF16) for shape in shapes],
+        cost_estimate=takes(6),
+    )
+    return [whole(block) for block in out]
 
 
 def whole(block):
@@ -284,132 +462,240 @@
         assert first % count == 0
         arrays = arrays + [core] + buffers
         in_specs = in_specs + [scalar] + [pl.BlockSpec(memory_space=pl.ANY)] * len(buffers)
-        moved = sum(array.size * 2 for array in arrays[:2]) + 4 * flops // 2048
-        buffers = list(pl.pallas_call(
-            kernel,
-            grid=grid,
-            in_specs=in_specs,
-            out_specs=[place, place],
-            out_shape=[shape, shape],
-            scratch_shapes=scratch,
-            input_output_aliases={len(arrays) - 2: 0, len(arrays) - 1: 1} if buffers else {},
-            compiler_params=pltpu.CompilerParams(vmem_limit_bytes=VMEM_BYTES),
-            cost_estimate=pl.CostEstimate(flops=flops, bytes_accessed=moved, transcendentals=0),
-        )(*arrays))
+        buffers = list(
+            ordered_call(
+                kernel,
+                arrays,
+                in_specs,
+                grid=grid,
+                out_specs=[place, place],
+                out_shape=[shape, shape],
+                scratch_shapes=scratch,
+                input_output_aliases={len(arrays) - 2: 0, len(arrays) - 1: 1} if buffers else {},
+                cost_estimate=takes(1 + flops / 4.5e8),
+            )
+        )
     return buffers
 
 
-def split_kernel(where_ref, kept_ref, got_ref, away_x_ref, kept_x_ref, away_y_ref, kept_y_ref):
+def whole_kernel(left_ref, right_ref, *refs):
+    refs[-1][...] = weight_grad(left_ref[...], right_ref[...]).reshape(refs[-1].shape).astype(BF16)
+
+
+def scattered(pieces, rows, width, sizes):
+    devices = sizes["gx"] * sizes["gy"]
+    if not sizes["aligned"]:
+        packed = jnp.zeros((devices, rows, width), BF16)
+        for first, left, right in pieces:
+            grad = weight_grad(left, right).astype(BF16)
+            packed = lax.dynamic_update_slice(packed, grad.reshape(devices, -1, width), (0, first, 0))
+    else:
+        buffers = []
+        for first, left, right in pieces:
+            count = left.shape[1] // devices
+            block = pl.BlockSpec((devices, count, width), lambda step, at=first // count: (0, at, 0))
+            buffers = [
+                ordered_call(
+                    whole_kernel,
+                    [left, right] + buffers,
+                    [pl.BlockSpec(one.shape, lambda step: (0, 0)) for one in (left, right)]
+                    + [pl.BlockSpec(memory_space=pl.ANY)] * len(buffers),
+                    grid=(1,),
+                    out_specs=block,
+                    out_shape=jax.ShapeDtypeStruct((devices, rows, width), BF16),
+                    input_output_aliases={2: 0} if buffers else {},
+                    cost_estimate=takes(3),
+                )
+            ]
+        (packed,) = buffers
+    return lax.psum_scatter(packed.reshape(devices * rows, width), AXES, scatter_dimension=0, tiled=True)
+
+
+def widen_kernel(low_ref, high_ref):
+    high_ref[...] = low_ref[...].astype(F32)
+
+
+def widened(low):
+    whole_block = pl.BlockSpec(low.shape, lambda step: (0, 0))
+    return ordered_call(
+        widen_kernel,
+        [low],
+        [whole_block],
+        grid=(1,),
+        out_specs=whole_block,
+        out_shape=jax.ShapeDtypeStruct(low.shape, F32),
+        cost_estimate=takes(1),
+    )
+
+
+def split_kernel(where_ref, *refs):
+    away_x_ref, kept_x_ref, away_y_ref, kept_y_ref = refs[-4:]
     x, y = where_ref[0], where_ref[1]
-    half = kept_ref.shape[-1] // 2
-
-    def added(at, columns):
-        return (kept_ref[0, 0, 0, at, :, columns].astype(F32) + got_ref[0, 0, 0, at, :, columns].astype(F32)).astype(BF16)
-
+    half = kept_x_ref.shape[-1]
     left, right = slice(0, half), slice(half, 2 * half)
-    kept_x_ref[0, 0, 0] = added(x, left)
-    away_x_ref[0, 0, 0] = added(1 - x, left)
     stays = pl.program_id(2) == y
-
-    @pl.when(stays)
-    def _():
-        for at in range(2):
-            kept_y_ref[0, 0, at] = added(at, right)
-
-    @pl.when(jnp.logical_not(stays))
-    def _():
-        for at in range(2):
-            away_y_ref[0, 0, at] = added(at, right)
-
-
-def split_terms(kept, got):
-    groups, others, rows, width = kept.shape
+    row = 0
+    for kept_ref, got_ref in zip(refs[:-4:2], refs[1:-4:2]):
+        rows = slice(row, row + kept_ref.shape[-2])
+        row += kept_ref.shape[-2]
+
+        def added(at, columns, kept_ref=kept_ref, got_ref=got_ref):
+            total = kept_ref[0, 0, 0, at, :, columns].astype(F32) + got_ref[0, 0, 0, at, :, columns].astype(F32)
+            return total.astype(BF16)
+
+        kept_x_ref[0, 0, 0, rows, :] = added(x, left)
+        away_x_ref[0, 0, 0, rows, :] = added(1 - x, left)
+
+        @pl.when(stays)
+        def _(added=added, rows=rows):
+            for at in range(2):
+                kept_y_ref[0, 0, at, rows, :] = added(at, right)
+
+        @pl.when(jnp.logical_not(stays))
+        def _(added=added, rows=rows):
+            for at in range(2):
+                away_y_ref[0, 0, at, rows, :] = added(at, right)
+
+
+def split_terms(pairs):
+    groups, others, _, width = pairs[0][0].shape
+    rows = sum(kept.shape[2] for kept, _ in pairs)
     where = jnp.stack([lax.axis_index("gy") & 1, (lax.axis_index("gx") >> 1) & 1]).astype(jnp.int32)
-    shape = (groups // 2, 2, others // 2, 2, rows, width)
-    half = width // 2
-    inside = pl.BlockSpec((1, 1, 1, 2, rows, width), lambda high, z, y, where: (high, y, z, 0, 0, 0))
-    along_x = pl.BlockSpec((1, 1, 1, rows, half), lambda high, z, y, where: (high, y, z, 0, 0))
-    along_y = pl.BlockSpec((1, 1, 2, rows, half), lambda high, z, y, where: (high, z, 0, 0, 0))
-    shape_x = jax.ShapeDtypeStruct((groups // 2, 2, others // 2, rows, half), BF16)
-    shape_y = jax.ShapeDtypeStruct((groups // 2, others // 2, 2, rows, half), BF16)
-    return pl.pallas_call(
+    high, z, half = groups // 2, others // 2, width // 2
+    arrays = [one.reshape((high, 2, z, 2) + one.shape[2:]) for pair in pairs for one in pair]
+    along_x = pl.BlockSpec((1, 1, 1, rows, half), lambda high, z, y: (high, y, z, 0, 0))
+    along_y = pl.BlockSpec((1, 1, 2, rows, half), lambda high, z, y: (high, z, 0, 0, 0))
+    shape_x = jax.ShapeDtypeStruct((high, 2, z, rows, half), BF16)
+    shape_y = jax.ShapeDtypeStruct((high, z, 2, rows, half), BF16)
+    size = groups * others * rows * width
+    return ordered_call(
         split_kernel,
-        grid_spec=pltpu.PrefetchScalarGridSpec(
-            num_scalar_prefetch=1,
-            grid=(groups // 2, others // 2, 2),
-            in_specs=[inside, inside],
-            out_specs=[along_x, along_x, along_y, along_y],
-        ),
+        [where] + arrays,
+        [pl.BlockSpec(memory_space=pltpu.SMEM)]
+        + [pl.BlockSpec((1, 1, 1) + array.shape[3:], lambda high, z, y: (high, y, z, 0, 0, 0)) for array in arrays],
+        grid=(high, z, 2),
+        out_specs=[along_x, along_x, along_y, along_y],
         out_shape=[shape_x, shape_x, shape_y, shape_y],
-        compiler_params=pltpu.CompilerParams(vmem_limit_bytes=VMEM_BYTES),
-        cost_estimate=pl.CostEstimate(flops=kept.size, bytes_accessed=6 * kept.size, transcendentals=0),
-    )(where, kept.reshape(shape), got.reshape(shape))
+        cost_estimate=takes(2.8e-6 * size),
+    )
+
+
+def halve_kernel(count, where_ref, *refs):
+    outs = refs[2 * count :]
+    side = 0
+    for part in range(count):
+        own, (kept_ref, got_ref) = where_ref[part], refs[2 * part : 2 * part + 2]
+        width = kept_ref.shape[-1]
+        away_ref, stay_ref = (refs[-2], refs[-1]) if refs[-1].shape[-1] > width else refs[-2 * (count - part) :][:2]
+        columns = slice(side, side + width) if refs[-1].shape[-1] > width else slice(0, width)
+        side += width
+        for before in range(kept_ref.shape[0]):
+            for behind in range(kept_ref.shape[2]):
+                for out_ref, at in ((away_ref, 1 - own), (stay_ref, own)):
+                    total = kept_ref[before, at, behind].astype(F32) + got_ref[before, at, behind].astype(F32)
+                    out_ref[before, behind, :, columns] = total.astype(BF16)
+
+
+def halve_terms(parts, steps, join):
+    arrays, where, shapes, lefts = [], [], [], []
+    for (kept, got, bits), which in zip(parts, steps):
+        place = bits.index(which)
+        rows, width = kept.shape[-2:]
+        before, behind = 1 << place, 1 << (len(bits) - place - 1)
+        arrays += [one.reshape(before, 2, behind, rows, width) for one in (kept, got)]
+        where.append(bit_of(which))
+        lefts.append([one for one in bits if one != which])
+        shapes += [(before, behind, rows, width)] * 2
+    if join:
+        shapes = [shape[:-1] + (2 * shape[-1],) for shape in shapes[:2]]
+    outs = in_vmem(functools.partial(halve_kernel, len(parts)), arrays, shapes, where)
+    outs = [out.reshape((2,) * len(lefts[0]) + out.shape[-2:]) for out in outs]
+    return [
+        tuple(outs[2 * at : 2 * at + 2]) + which + (left,)
+        for at, (which, left) in enumerate(zip(steps[: len(outs) // 2], lefts))
+    ]
+
+
+def added_kernel(kept_ref, got_ref, total_ref):
+    total_ref[...] = kept_ref[...].astype(F32) + got_ref[...].astype(F32)
+
+
+def added(kept, got):
+    vmem = pl.BlockSpec(memory_space=pltpu.VMEM)
+    return ordered_call(
+        added_kernel,
+        [kept, got],
+        [vmem, vmem],
+        out_specs=vmem,
+        out_shape=jax.ShapeDtypeStruct(kept.shape, F32),
+        cost_estimate=takes(1),
+    )
 
 
 class OwnerSum:
-    def __init__(self, pieces, rows, width, sizes):
-        bits = mesh_bits(sizes)
+    def __init__(self, width, sizes):
         core, y_bits, x_bits, z_bits = mesh_axes_bits(sizes)
-        self.width = width
-        self.flying = None
+        self.width, self.sizes, self.core, self.bits = width, sizes, core, mesh_bits(sizes)
         self.plan = [list(pair) for pair in zip(x_bits + y_bits, y_bits + x_bits)] + [[which] for which in z_bits]
-        devices = sizes["gx"] * sizes["gy"]
-        self.whole_tiles = len(core) == 1 and bool(y_bits) and bool(x_bits) and len(x_bits) == len(y_bits)
+        self.kernels = sizes["aligned"] and len(core) == 1 and bool(y_bits) and len(x_bits) == len(y_bits)
+        self.terms, self.flying, self.parts = [], [], None
+
+    def add(self, rows, *pieces):
+        devices = self.sizes["gx"] * self.sizes["gy"]
+        if self.kernels:
+            away, kept = pack_terms(pieces, rows, self.width, self.sizes)
+            self.terms.append((kept, exchange(away, self.core[0])))
+            return
+        packed = jnp.zeros((devices, rows, self.width), BF16)
         for piece in pieces:
-            self.whole_tiles &= len(piece) == 2 or piece[1].shape[1] % (8 * devices) == 0
-        if self.whole_tiles:
-            away, kept = pack_terms(pieces, rows, width, sizes)
-            self.waiting = [(away, kept) + core[0] + ([one for one in bits if one not in core],)]
+            blocks = [piece[1]]
+            if len(piece) == 3:
+                grad = weight_grad(*piece[1:]).astype(BF16)
+                blocks = jnp.split(grad, max(1, grad.shape[1] // self.width), 1)
+            at = piece[0]
+            for block in blocks:
+                block = block.reshape(devices, -1, block.shape[-1])
+                packed = lax.dynamic_update_slice(packed, block, (0, at, 0))
+                at += block.shape[1]
+        self.terms.append(packed)
+
+    def advance(self):
+        sends = None
+        if self.terms and self.kernels:
+            sends = self.first_split()
+        elif self.terms:
+            packed = jnp.concatenate(self.terms, 1)
+            self.parts = [(packed.reshape((2,) * len(self.bits) + packed.shape[1:]), self.bits)]
+            self.plan = [[which] for which in self.core] + self.plan
+        elif self.plan and self.kernels:
+            sends = self.next_sends()
+        elif self.kernels:
+            self.parts = [(added(*self.flying[0][:2]), [])]
         else:
-            packed = jnp.zeros((devices, rows, width), BF16)
-            for piece in pieces:
-                blocks = [piece[1]]
-                if len(piece) == 3:
-                    grad = weight_grad(*piece[1:]).astype(BF16)
-                    blocks = jnp.split(grad, max(1, grad.shape[1] // width), 1)
-                at = piece[0]
-                for block in blocks:
-                    block = block.reshape(devices, -1, block.shape[-1])
-                    packed = lax.dynamic_update_slice(packed, block, (0, at, 0))
-                    at += block.shape[1]
-            self.waiting = None
-            self.parts = [(packed.reshape((2,) * len(bits) + packed.shape[1:]), bits)]
-            self.plan = [[which] for which in core] + self.plan
-
-    def advance(self, *others):
-        sends, self.waiting = self.waiting, None
-        if self.flying is not None:
-            held = tie(*[got for _, got, _ in self.flying], *others)
-            others = held[len(self.flying) :]
-            if self.whole_tiles and self.flying[0][0].ndim == 4 and self.flying[0][0].shape[-1] == self.width and len(self.plan[0]) == 2:
-                sends = self.first_split(held[0])
-            else:
-                self.parts = [
-                    ((kept.astype(F32) + got.astype(F32)).astype(BF16 if self.plan else F32), bits)
-                    for (kept, _, bits), got in zip(self.flying, held)
-                ]
-            self.flying = None
+            self.parts = [
+                ((kept.astype(F32) + got.astype(F32)).astype(BF16 if self.plan else F32), bits)
+                for kept, got, bits in self.flying
+            ]
+        self.terms, self.flying = [], []
         if sends is None and self.plan:
             sends = self.halves()
-        if sends is not None:
-            held = tie(*[one[0] for one in sends], *others)
-            others = held[len(sends) :]
-            self.flying = []
-            for away, (_, kept, axis, bit, left) in zip(held, sends):
-                count = lax.axis_size(axis)
-                got = lax.ppermute(away, axis, [(at, at ^ (1 << bit)) for at in range(count)])
-                self.flying.append((kept, got, left))
-        return others[0] if len(others) == 1 else others
-
-    def first_split(self, got):
-        kept, _, bits = self.flying[0]
-        out = split_terms(kept, got)
+        for away, kept, axis, bit, left in sends or []:
+            self.flying.append((kept, exchange(away, (axis, bit)), left))
+
+    def first_split(self):
+        bits = [one for one in self.bits if one not in self.core]
+        out = split_terms(self.terms)
         sends = []
         for part, which in enumerate(self.plan.pop(0)):
             left = [one for one in bits if one != which]
             away, kept = (one.reshape((2,) * len(left) + one.shape[-2:]) for one in out[2 * part : 2 * part + 2])
             sends.append((away, kept) + which + (left,))
         return sends
+
+    def next_sends(self):
+        steps = self.plan.pop(0)
+        join = len(steps) < len(self.flying)
+        return halve_terms(self.flying, steps * 2 if join else steps, join)
 
     def halves(self):
         step = self.plan.pop(0)
@@ -428,7 +714,7 @@
         return sends
 
     def result(self):
-        while self.plan or self.flying is not None:
+        while self.plan or self.flying:
             self.advance()
         return self.parts[0][0].astype(F32)
 
@@ -494,6 +780,8 @@
         image_mix,
         image_gain_self,
     ) = given
+    matrices = [array for array in given[6:] if array.ndim == 2]
+    sizes = dict(sizes, aligned=all(array.shape[0] % 8 == 0 for array in matrices))
     devices = sizes["gx"] * sizes["gy"]
     pairs, length, text_width = text_tokens.shape
     regions, image_width = image_regions.shape[1:]
@@ -509,18 +797,10 @@
         text_gain_self,
         image_gain_self,
     )
-    vector_block = jnp.concatenate(
-        [jnp.pad(vector[None, :], ((0, 0), (0, text_width - vector.shape[0]))) for vector in vectors], 0
-    )
-    first_pieces = [text_query, image_key, image_value]
-    packed_first = jnp.concatenate(first_pieces + [jnp.pad(text_merge, ((0, 0), (0, inner - text_width)))], 0)
     text_pieces = jnp.split(text_up, text_up.shape[1] // text_width, 1) + [text_down]
-    text_pieces += jnp.split(text_self, 3, 1) + [text_mix, vector_block]
-    packed_text = jnp.concatenate(text_pieces, 0)
+    text_pieces += jnp.split(text_self, 3, 1) + [text_mix, text_merge]
     image_pieces = [image_query, text_key, text_value, image_merge, image_up, image_down]
     image_pieces += jnp.split(image_self, 3, 1) + [image_mix]
-    packed_image = jnp.concatenate(image_pieces, 0)
-
     def starts(pieces):
         marks = [0]
         for piece in pieces:
@@ -533,13 +813,19 @@
     def side_by_side(block, spans):
         return jnp.concatenate([taken(block, at) for at in spans], 1)
 
-    first_at = starts(first_pieces + [text_merge])
     text_at, image_at = starts(text_pieces), starts(image_pieces)
-    all_text = gather(packed_text)
-    all_first = gather_by_exchange(packed_first, sizes)
-    weight_text_query = taken(all_first, first_at[0])
-    weight_image_held = side_by_side(all_first, first_at[1:3])
-    full_text_merge = taken(all_first, first_at[3])[:, :text_width]
+    packed = []
+
+    def pack_image():
+        shards = [image_query, text_key, text_value, image_merge, image_up, image_down, image_self, image_mix]
+        packed.append(pack_rows(shards, inner))
+
+    Order.last = []
+    all_text = gather(copy_rows([text_up, text_down, text_self, text_mix, text_merge], text_width))
+    weight_text_query, weight_image_held, all_vectors = gather_weights(
+        [[text_query], [image_key, image_value]], vectors, sizes, pack_image
+    )
+    (packed_image,) = packed
 
     text_slots, image_slots = round_up(length, 8), round_up(regions, 8)
 
@@ -573,15 +859,16 @@
     mixed_cross, packed_image = tie(mixed_cross, packed_image)
     all_image = gather(packed_image)
     cross_text = rows_of(mixed_cross)
+    ups = text_up.shape[1] // text_width
+    full_text_merge = taken(all_text, text_at[ups + 5])
     unit_text_1, rate_text_1 = normed_rows(text_rows.astype(F32) + project(cross_text, full_text_merge))
 
-    ups = text_up.shape[1] // text_width
     full_text_up = side_by_side(all_text, text_at[:ups])
     full_text_down = taken(all_text, text_at[ups])
     full_text_self = side_by_side(all_text, text_at[ups + 1 : ups + 4])
     full_text_mix = taken(all_text, text_at[ups + 4])
     full = {
-        name: all_text[:, text_at[ups + 5][0] + at, : piece.shape[0]].reshape(-1).astype(F32)
+        name: all_vectors.reshape(devices, len(vectors), inner)[:, at, : piece.shape[0]].reshape(-1).astype(F32)
         for at, (name, piece) in enumerate(zip(VECTOR_NAMES, vectors))
     }
 
@@ -590,8 +877,7 @@
         first = unit_1 * gain_1
         first_low = first.astype(BF16)
         hidden = project(first_low, up) + bias
-        active = gelu(hidden).astype(BF16)
-        slope = gelu_slope(hidden).astype(BF16)
+        active, slope = tie(gelu(hidden).astype(BF16), gelu_slope(hidden).astype(BF16))
         unit_2, rate_2 = normed_rows(first + project(active, down))
         second = unit_2 * gain_2
         second_low = second.astype(BF16)
@@ -647,38 +933,31 @@
         d_text_out,
         TEXT_HEADS,
     )
+    row_text, row_image, row_down = text_query.shape[0], image_key.shape[0], text_down.shape[0]
+    sum_a, sum_b = OwnerSum(text_width, sizes), OwnerSum(text_width, sizes)
+    sum_c, sum_d, sum_e = OwnerSum(inner, sizes), OwnerSum(inner, sizes), OwnerSum(inner, sizes)
+    sum_a.add(4 * row_text, (0, *g_text_self), (3 * row_text, *g_text_mix))
     d_resid_text, g_text_up, g_text_down, g_text_bias, g_text_gain_cross = feed_backward(
         saved_text, d_sum_text, unit_text_1, rate_text_1, full["text_gain_cross"], full_text_up, full_text_down
     )
     row_down, row_self = text_at[ups][0], text_at[ups + 1][0]
-    sum_text = OwnerSum(
-        [
-            (0, *g_text_up),
-            (row_down, *g_text_down),
-            (row_self, *g_text_self),
-            (text_at[ups + 4][0], *g_text_mix),
-        ],
-        text_at[ups + 4][1],
-        text_width,
-        sizes,
-    )
-    d_resid_text = sum_text.advance(d_resid_text)
-
+    sum_a.advance()
+    sum_b.add(ups * row_text, (0, *g_text_up))
+    sum_a.advance()
+    sum_b.add(row_down, (0, *g_text_down))
     d_merge_text = d_resid_text.astype(BF16)
+    sum_b.add(text_merge.shape[0], (0, cross_text, d_merge_text))
     d_heads_text = pairs_of(project_back(d_merge_text, full_text_merge).astype(BF16))
     d_query_text, d_key_image, d_value_image = map(
         rows_of,
         attend_back((query_text, 0), (held_image, 0), (held_image, 1), image_fill, d_heads_text, inner, HEADS),
     )
-    row_image, row_text = image_key.shape[0], text_query.shape[0]
-    sum_first = OwnerSum(
-        [
-            (0, image_rows, d_key_image),
-            (row_image, image_rows, d_value_image),
-            (2 * row_image, cross_text, d_merge_text),
-            (3 * row_image, text_rows, d_query_text),
-        ],
-        3 * row_image + row_text,
+    sum_b.advance()
+    sum_a.advance()
+    row_first = round_up(2 * row_image, row_text)
+    sums_first = scattered(
+        [(0, image_rows, d_key_image), (row_image, image_rows, d_value_image), (row_first, text_rows, d_query_text)],
+        row_first + row_text,
         inner,
         sizes,
     )
@@ -690,11 +969,10 @@
     full_image_self = side_by_side(all_image, image_at[6:9])
     full_image_mix = taken(all_image, image_at[9])
 
-    image_rows_2 = sum_text.advance(image_rows)
-    image_rows_2 = sum_first.advance(image_rows_2)
-    query_image = pairs_of(project(image_rows_2, weight_image_query).astype(BF16))
+    query_image = pairs_of(project(image_rows, weight_image_query).astype(BF16))
     held_text = pairs_of(project(text_rows, weight_text_held).astype(BF16))
     cross_image = rows_of(attend((query_image, 0), (held_text, 0), (held_text, 1), text_fill, inner, HEADS))
+    sum_a.advance()
     unit_image_1, rate_image_1 = normed_rows(image_rows.astype(F32) + project(cross_image, full_image_merge))
 
     out_image, saved_image = forward(
@@ -711,7 +989,8 @@
         image_keep,
         IMAGE_HEADS,
     )
-    d_image_out, *saved_image = sum_text.advance(d_image_out, *saved_image)
+    sum_b.advance()
+    sum_a.advance()
     d_sum_image, g_image_mix, g_image_self, g_image_gain_ffn, g_image_gain_self = self_backward(
         saved_image,
         full["image_gain_ffn"],
@@ -723,7 +1002,8 @@
         d_image_out,
         IMAGE_HEADS,
     )
-    d_sum_image = sum_first.advance(d_sum_image)
+    sum_c.add(4 * row_image, (0, *g_image_self), (3 * row_image, *g_image_mix))
+    sum_b.advance()
     d_resid_image, g_image_up, g_image_down, g_image_bias, g_image_gain_cross = feed_backward(
         saved_image,
         d_sum_image,
@@ -733,28 +1013,21 @@
         full_image_up,
         full_image_down,
     )
-    d_resid_image = sum_text.advance(d_resid_image)
-
+
+    sum_c.advance()
+    sum_b.advance()
     d_merge_image = d_resid_image.astype(BF16)
-    sum_image = OwnerSum(
-        [
-            (0, cross_image, d_merge_image),
-            (row_image, *g_image_up),
-            (2 * row_image, *g_image_down),
-            (3 * row_image, *g_image_self),
-            (6 * row_image, *g_image_mix),
-        ],
-        7 * row_image,
-        image_width,
-        sizes,
-    )
-    d_merge_image = sum_image.advance(d_merge_image)
+    sum_e.add(
+        3 * row_image,
+        (0, cross_image, d_merge_image),
+        (row_image, *g_image_up),
+        (2 * row_image, *g_image_down),
+    )
     d_heads_image = pairs_of(project_back(d_merge_image, full_image_merge).astype(BF16))
     d_query_image, d_key_text, d_value_text = map(
         rows_of,
         attend_back((query_image, 0), (held_text, 0), (held_text, 1), text_fill, d_heads_image, inner, HEADS),
     )
-    d_query_image = sum_first.advance(d_query_image)
     g_vectors = (
         g_text_gain_cross,
         g_image_gain_cross,
@@ -766,7 +1039,8 @@
         g_image_gain_self,
     )
     row_vector = 2 * row_text
-    vector_rows = max(len(vectors), 2 * row_image - row_vector)
+    vector_rows = max(len(vectors), round_up(row_vector + len(vectors), row_image) - row_vector)
+    row_query = row_vector + vector_rows
     g_vector = jnp.stack(
         [
             jnp.pad(owned, ((0, 0), (0, inner - owned.shape[1])))
@@ -775,21 +1049,18 @@
         1,
     )
     g_vector = jnp.pad(g_vector, ((0, 0), (0, vector_rows - len(vectors)), (0, 0)))
-    row_query = row_vector + vector_rows
-    sum_last = OwnerSum(
-        [
-            (0, text_rows, d_key_text),
-            (row_text, text_rows, d_value_text),
-            (row_query, image_rows, d_query_image),
-            (row_vector, g_vector),
-        ],
+    sum_c.advance()
+    sum_e.advance()
+    sum_b.advance()
+    sum_d.add(
         row_query + row_image,
-        inner,
-        sizes,
-    )
-    token = sum_image.advance(d_key_text)
-    token = sum_last.advance(token)
-    d_resid_text, d_resid_image, d_key_text = tie(d_resid_text, d_resid_image, token)
+        (0, text_rows, d_key_text),
+        (row_text, text_rows, d_value_text),
+        (row_query, image_rows, d_query_image),
+        (row_vector, g_vector),
+    )
+    sum_c.advance()
+    sum_d.advance()
     grad_text = (
         d_resid_text
         + project_back(d_query_text, weight_text_query)
@@ -800,25 +1071,28 @@
         + project_back(d_query_image, weight_image_query)
         + project_back(jnp.concatenate([d_key_image, d_value_image], 1), weight_image_held)
     )
-    token = sum_text.advance(d_key_text)
-    for _ in range(2):
-        token = sum_first.advance(token)
-    for _ in range(5):
-        token = sum_last.advance(token)
-        token = sum_image.advance(token)
+    sum_e.advance()
+    sum_c.advance()
+    sum_d.advance()
+    sum_e.advance()
+    sum_c.advance()
+    sum_d.advance()
+    sum_e.advance()
+    sum_d.advance()
+    sum_e.advance()
+    sum_d.advance()
 
     def owned(total, pieces):
         return [total[start:end] for start, end in starts(pieces)]
 
-    done = [one.result() for one in (sum_text, sum_first, sum_image, sum_last)]
-    text_sums = owned(done[0], text_pieces[:-1])
-    sum_image_key, sum_image_value, sum_text_merge, sum_text_query = owned(
-        done[1], [image_key, image_value, text_merge, text_query]
-    )
-    image_sums = owned(done[2], image_pieces[3:])
-    sum_text_key, sum_text_value = owned(done[3], [text_key, text_value])
-    sum_vector = done[3][row_vector:row_query]
-    sum_image_query = done[3][row_query:]
+    sums_first = widened(sums_first)
+    sums_a, sums_b, sums_c, sums_d, sums_e = [one.result() for one in (sum_a, sum_b, sum_c, sum_d, sum_e)]
+    text_selfs = owned(sums_a, text_pieces[ups + 1 : ups + 5])
+    text_sums = owned(sums_b, text_pieces[: ups + 1] + [text_merge])
+    image_firsts = owned(sums_first, [image_key, image_value]) + [sums_first[row_first : row_first + row_text]]
+    image_selfs = owned(sums_c, image_pieces[6:10])
+    image_sums = owned(sums_e, image_pieces[3:6]) + owned(sums_d, [text_key, text_value])
+    sum_vector = sums_d[row_vector:row_query]
     owned_vector = {
         name: sum_vector[at, : piece.shape[0]] for at, (name, piece) in enumerate(zip(VECTOR_NAMES, vectors))
     }
@@ -827,14 +1101,14 @@
         pairs_of(out_image)[:, :regions],
         pairs_of(grad_text)[:, :length],
         pairs_of(grad_image)[:, :regions],
-        sum_text_query,
-        sum_image_key,
-        sum_image_value,
-        sum_text_merge[:, :text_width],
+        image_firsts[2],
+        image_firsts[0],
+        image_firsts[1],
+        text_sums[ups + 1],
         owned_vector["text_gain_cross"],
-        sum_image_query,
-        sum_text_key,
-        sum_text_value,
+        sums_d[row_query:],
+        image_sums[3],
+        image_sums[4],
         image_sums[0],
         owned_vector["image_gain_cross"],
         jnp.concatenate(text_sums[:ups], 1),
@@ -845,11 +1119,11 @@
         owned_vector["image_bias"],
         image_sums[2],
         owned_vector["image_gain_ffn"],
-        jnp.concatenate(text_sums[ups + 1 : ups + 4], 1),
-        text_sums[ups + 4],
+        jnp.concatenate(text_selfs[:3], 1),
+        text_selfs[3],
         owned_vector["text_gain_self"],
-        jnp.concatenate(image_sums[3:6], 1),
-        image_sums[6],
+        jnp.concatenate(image_selfs[:3], 1),
+        image_selfs[3],
         owned_vector["image_gain_self"],
     )
 

time: 661 us -> 636 us (0.962)
  other arithmetic: 67.4 us -> 34.8 us
  Pallas kernels: 135 us -> 164 us
  waiting for transfers between devices: 182 us -> 158 us
  local copies, waits for them, and re-layouts: 115 us -> 97.1 us
  matrix products: 92.8 us -> 107 us
  starting transfers between devices: 40.5 us -> 48 us
    ppermute x35 -> x45, waiting for transfers between devices: 182 us -> 139 us  [exchange(): lax.ppermute(block, axis, [(at, at ^ 1 << bit) for at in range(lax.axis_s...]
    pallas_call x29 -> x59, Pallas kernels: 135 us -> 164 us  [ordered_call(): pl.pallas_call(body, in_specs=list(in_specs) + [pl.BlockSpec(memory_space...]
    convert_element_type x26 -> x5, other arithmetic: 22.4 us -> 1.98 us  [the longest x4 1.97 us: per_device(): all_vectors.reshape(devices, len(vectors), inner)[:, at, :piece.shape[0]]]
    all_gather x2, waiting for transfers between devices: 0.02 us -> 18.4 us  [gather(): return lax.all_gather(packed, AXES, axis=0, tiled=False)]
    dot_general x14, matrix products: 39 us -> 52.7 us  [project(): return jnp.dot(left, right, preferred_element_type=F32)]
    another operation x12 -> x3, other arithmetic: 12.1 us -> 0.22 us  [in_vmem(): jnp.stack(where).astype(jnp.int32)]
    concatenate x2 -> x0, local copies, waits for them, and re-layouts: 8.55 us -> none  [the longest x1 7.93 us: per_device(): packed_text = jnp.concatenate(text_pieces, 0)]
    optimization_barrier x8 -> x0, local copies, waits for them, and re-layouts: 7.9 us -> none  [tie(): return lax.optimization_barrier(values)]
  transfers between devices with their start and end apart: 37 -> 48, of which waited for: 23 -> 24; matrix products, arithmetic and copies ran while one was open for 35% -> 32% of each run, Pallas kernels for 16% -> 23%
where the time goes in v3:
time: 636 us; the launch traced here: 625 us
  Pallas kernels  164 us (26%)
  waiting for transfers between devices  158 us (25%)
  matrix products  107 us (17%)
  local copies, waits for them, and re-layouts  97.1 us (15%)
  starting transfers between devices  48 us (8%)
  other arithmetic  34.8 us (5%)
  between operations  16.2 us (3%)
    pallas_call x59, Pallas kernels, ordered_call(): pl.pallas_call(body, in_specs=list(in_specs) + [pl.BlockSpec(memory_space...  164 us
    ppermute x45, waiting for transfers between devices, exchange(): lax.ppermute(block, axis, [(at, at ^ 1 << bit) for at in range(lax.axis_s...  139 us
    dot_general x14, matrix products, project_back(): lax.dot_general(left, right, (((1,), (1,)), ((), ())), preferred_element_...  54.7 us
    dot_general x14, matrix products, project(): return jnp.dot(left, right, preferred_element_type=F32)  52.7 us
    unnamed x318, local copies, waits for them, and re-layouts  47.9 us
    ppermute x45, starting transfers between devices, exchange(): lax.ppermute(block, axis, [(at, at ^ 1 << bit) for at in range(lax.axis_s...  47.9 us
    slice x5, local copies, waits for them, and re-layouts, taken(): return whole(block[:, at[0]:at[1]])  27.5 us
    all_gather x2, waiting for transfers between devices, gather(): return lax.all_gather(packed, AXES, axis=0, tiled=False)  18.4 us
  transfers between devices with their start and end apart: 48, of which 24 were waited for; matrix products, arithmetic and copies ran while one was open for 32% of the time, Pallas kernels for 23%

profile of v3, /device:TPU:0, one launch (start us, length us, event | category | flops | bytes accessed | tf_op | source)
XLA Modules:
  0.0 625.1 jit_solution(15970186606773063863)
XLA Ops:
  25.3 15.8 %collective-permute-done = bf16[96,1024]{1,0:T(8,128)(2,1)S(1)} collective-permute-done((bf16[96,1024]{1,0:T(8,128)(2,1)S(1)}, bf16[96,1024]{1,0:T(8,128)(2,1)S(1)}, u32[]{:S(2)}, u32[]{:S(2)}) %collective-permute-start) | collective-permute-done | bytes 196640 | tf_op jit(solution)/shard_map/ppermute | solution.py:198
  43.8 9.3 %collective-permute-done.1 = bf16[2,96,1024]{2,1,0:T(8,128)(2,1)S(1)} collective-permute-done((bf16[2,96,1024]{2,1,0:T(8,128)(2,1)S(1)}, bf16[2,96,1024]{2,1,0:T(8,128)(2,1)S(1)}, u32[]{:S(2)}, u32[]{:S(2)}) %collective-permute-start.1) | collective-permute-done | bytes 393248 | tf_op jit(solution)/shard_map/ppermute | solution.py:198
  56.0 12.6 %collective-permute-done.2 = bf16[2,2,96,512]{3,2,1,0:T(8,128)(2,1)S(1)} collective-permute-done((bf16[2,2,96,512]{3,2,1,0:T(8,128)(2,1)S(1)}, bf16[2,2,96,512]{3,2,1,0:T(8,128)(2,1)S(1)}, u32[]{:S(2)}, u32[]{:S(2)}) %collective-permute-start.2) | collective-permute-done | bytes 393248 | tf_op jit(solution)/shard_map/ppermute | solution.py:198
  76.5 16.0 %collective-permute-done.4 = bf16[2,2,2,96,512]{4,3,2,1,0:T(8,128)(2,1)S(1)} collective-permute-done((bf16[2,2,2,96,512]{4,3,2,1,0:T(8,128)(2,1)S(1)}, bf16[2,2,2,96,512]{4,3,2,1,0:T(8,128)(2,1)S(1)}, u32[]{:S(2)}, u32[]{:S(2)}) %collective-permute-start.4) | collective-permute-done | bytes 786464 | tf_op jit(solution)/shard_map/ppermute | solution.py:198
  124.2 18.4 %all-gather.5.cloned.1.call-done = bf16[10240,768]{1,0:T(8,128)(2,1)} async-done(((bf16[320,768]{1,0:T(8,128)(2,1)}), bf16[10240,768]{1,0:T(8,128)(2,1)}) %all-gather.5.cloned.1.call-update) | async-done | bytes 15728656 | tf_op jit(solution)/shard_map/all_gather | solution.py:177
  152.1 7.0 %fusion.46 = (bf16[32,24,768]{2,1,0:T(8,128)(2,1)}, bf16[32,24,768]{2,1,0:T(8,128)(2,1)}, bf16[32,24,768]{2,1,0:T(8,128)(2,1)}, bf16[32,24,768]{2,1,0:T(8,128)(2...) fusion(bf16[32,320,768]{2,1,0:T(8,128)(2,1)} %bitcast.456), kind=kLoop, calls=%fused_computation.187 | loop fusion | bytes 18874368 | tf_op jit(solution)/shard_map/slice | solution.py:811
  159.2 16.3 %add_convert_fusion = (bf16[832,3072]{1,0:T(8,128)(2,1)}, bf16[832,3072]{1,0:T(8,128)(2,1)S(1)}) fusion(f32[3072]{0:T(1024)S(1)} %reshape.932, bf16[832,768]{1,0:T(8,128)(2,1)S(1)} %multiply_convert_fusion.3.refs_0_, bf16[768,768]{1,0:T(8,128)(2,1)S(1)} %bitcast.493, bf16[768,768]{1,0:T(8,128)(2,1)S(1)} %bitcast.495, bf16[768,768]{1,0:T(8,128)(2,1)S(1)} %bitcast.497, ...), kind=kOutput, calls=%fused_computation.7 | convolution fusion | flops 4011196416 | bytes 16232448 | tf_op jit(solution)/shard_map/dot_general | solution.py:35
  175.5 8.6 %fusion.55 = (f32[832]{0:T(1024)S(1)}, f32[832,768]{1,0:T(8,128)S(1)}) fusion(bf16[832,3072]{1,0:T(8,128)(2,1)S(1)} %get-tuple-element.153.refs_0_, bf16[3072,768]{1,0:T(8,128)(2,1)} %bitcast.467, f32[768]{0:T(1024)S(1)} %reshape.931, f32[832]{0:T(1024)S(1)} %add_rsqrt_fusion.2, f32[832,768]{1,0:T(8,128)S(1)} %get-tuple-element.346, ...), kind=kOutput, calls=%fused_computation.196 | convolution fusion | flops 3929062656 | bytes 14955264 | tf_op jit(solution)/shard_map/dot_general | solution.py:35
  209.5 8.9 %shard_map.511 = (bf16[8,104,768]{2,1,0:T(8,128)(2,1)S(1)}, bf16[8,104,768]{2,1,0:T(8,128)(2,1)S(1)}, bf16[8,104,768]{2,1,0:T(8,128)(2,1)S(1)}) custom-call(bf16[8,104,2304]{2,1,0:T(8,128)(2,1)} %bitcast.446, bf16[8,104,2304]{2,1,0:T(8,128)(2,1)} %bitcast.447, bf16[8,104,2304]{2,1,0:T(8,128)(2,1)} %bitcast.448, f32[8,104,128]{2,1,0:T(8,128)S(1)} %broadcast_in_dim.77.refs_3_, ...), custom_call_target="tpu_custom_call" | custom-call | bytes 22400000 | tf_op jit(solution)/shard_map/pallas_call | solution.py:65
  220.5 7.3 %shard_map.512 = (bf16[2,8,96,768]{3,2,1,0:T(8,128)(2,1)}, bf16[2,8,96,768]{3,2,1,0:T(8,128)(2,1)}) custom-call(bf16[832,768]{1,0:T(8,128)(2,1)S(1)} %multiply_convert_fusion.2.refs_0_, bf16[832,2304]{1,0:T(8,128)(2,1)} %bitcast.457, s32[1]{0:T(128)} %bitcast.64.refs_2_.refs_1_, bf16[8,104,768]{2,1,0:T(8,128)(2,1)S(1)} %get-tuple-element.155.refs_3_), custom_call_target="tpu_custom_call" | custom-call | bytes 24137964 | tf_op jit(solution)/shard_map/pallas_call | solution.py:65
  235.3 7.3 %multiply_reduce_fusion.1 = (bf16[768]{0:T(1024)(128)(2,1)}, f32[832]{0:T(1024)S(1)}, f32[832]{0:T(1024)S(1)}, f32[832,768]{1,0:T(8,128)S(1)}) fusion(f32[832,768]{1,0:T(8,128)S(1)} %copy-done.95, f32[832]{0:T(1024)S(1)} %add_rsqrt_fusion.1, f32[832]{0:T(1024)S(1)} %broadcast_multiply_fusion.8, f32[768]{0:T(1024)S(1)} %reshape.933, ...), kind=kOutput, calls=%fused_computation.24 | convolution fusion | flops 2960766720 | bytes 15058432 | tf_op jit(solution)/shard_map/dot_general | solution.py:39
  250.5 10.3 %fusion.60 = (bf16[3072]{0:T(1024)(128)(2,1)}, bf16[832,3072]{1,0:T(8,128)(2,1)}) fusion(bf16[832,768]{1,0:T(8,128)(2,1)S(1)} %get-tuple-element.288.refs_1_, bf16[3072,768]{1,0:T(8,128)(2,1)} %bitcast.468, bf16[832,3072]{1,0:T(8,128)(2,1)} %get-tuple-element.158), kind=kOutput, calls=%fused_computation.201 | convolution fusion | flops 3936089088 | bytes 16226304 | tf_op jit(solution)/shard_map/dot_general | solution.py:39
  260.7 9.0 %shard_map.515 = (bf16[2,8,96,768]{3,2,1,0:T(8,128)(2,1)}, bf16[2,8,96,768]{3,2,1,0:T(8,128)(2,1)}) custom-call(bf16[832,768]{1,0:T(8,128)(2,1)S(1)} %copy-done.24, bf16[832,3072]{1,0:T(8,128)(2,1)} %get-tuple-element.362.refs_1_, s32[1]{0:T(128)} %bitcast.64.refs_2_.refs_1_, bf16[1,2,4,96,384]{4,3,2,1,0:T(8,128)(2,1)S(1)} %get-tuple-element.164.refs_3_), custom_call_target="tpu_custom_call" | custom-call | bytes 31117288 | tf_op jit(solution)/shard_map/pallas_call | solution.py:65
  270.6 10.1 %shard_map.517 = (bf16[2,8,96,768]{3,2,1,0:T(8,128)(2,1)}, bf16[2,8,96,768]{3,2,1,0:T(8,128)(2,1)}) custom-call(bf16[832,3072]{1,0:T(8,128)(2,1)} %copy-done.112, bf16[832,768]{1,0:T(8,128)(2,1)S(1)} %get-tuple-element.288.refs_1_, s32[1]{0:T(128)} %bitcast.64.refs_2_.refs_1_, bf16[1,4,96,384]{3,2,1,0:T(8,128)(2,1)S(1)} %get-tuple-element.168.refs_3_), custom_call_target="tpu_custom_call" | custom-call | bytes 31117288 | tf_op jit(solution)/shard_map/pallas_call | solution.py:65
  281.4 8.8 %multiply_reduce_fusion.2 = (bf16[768]{0:T(1024)(128)(2,1)}, f32[832]{0:T(1024)S(1)}, f32[832]{0:T(1024)S(1)}, f32[832,768]{1,0:T(8,128)S(1)}) fusion(f32[832,768]{1,0:T(8,128)S(1)} %copy-done.93, f32[832]{0:T(1024)S(1)} %add_rsqrt_fusion.2, f32[832]{0:T(1024)S(1)} %broadcast_multiply_fusion.9, f32[768]{0:T(1024)S(1)} %reshape.931, ...), kind=kOutput, calls=%fused_computation.25 | convolution fusion | flops 3950491392 | bytes 17516032 | tf_op jit(solution)/shard_map/dot_general | solution.py:39
  322.5 9.0 %shard_map.520 = (bf16[1,2,4,224,384]{4,3,2,1,0:T(8,128)(2,1)}, bf16[1,2,4,224,384]{4,3,2,1,0:T(8,128)(2,1)S(1)}, bf16[1,4,2,224,384]{4,3,2,1,0:T(8,128)(2,1)}, bf16[1,4,2,224,384]{4,3,2,1,0:T(8,128)(2,1)}) custom-call(s32[2]{0:T(128)S(1)} %pad_add_fusion.2.refs_0_, bf16[1,2,4,2,96,768]{5,4,3,2,1,0:T(8,128)(2,1)} %bitcast.470, ...), custom_call_target="tpu_custom_call" | custom-call | bytes 24662508 | tf_op jit(solution)/shard_map/pallas_call | solution.py:65
  347.6 11.4 %fusion.44 = (bf16[32,32,1024]{2,1,0:T(8,128)(2,1)}, bf16[32,32,1024]{2,1,0:T(8,128)(2,1)}, bf16[32,32,1024]{2,1,0:T(8,128)(2,1)}, bf16[32,32,1024]{2,1,0:T(8,12...) fusion(bf16[32,304,1024]{2,1,0:T(8,128)(2,1)} %bitcast.452), kind=kLoop, calls=%fused_computation.185 | loop fusion | bytes 33554432 | tf_op jit(solution)/shard_map/slice | solution.py:811
  462.9 6.9 %shard_map.539 = (bf16[8,40,1024]{2,1,0:T(8,128)(2,1)S(1)}, bf16[8,104,1024]{2,1,0:T(8,128)(2,1)S(1)}, bf16[8,104,1024]{2,1,0:T(8,128)(2,1)S(1)}) custom-call(bf16[8,40,1024]{2,1,0:T(8,128)(2,1)S(1)} %bitcast.332, bf16[8,104,2048]{2,1,0:T(8,128)(2,1)} %bitcast.291, bf16[8,104,2048]{2,1,0:T(8,128)(2,1)} %bitcast.292, f32[8,104,128]{2,1,0:T(8,128)S(1)} %copy-done.15, ...), custom_call_target="tpu_custom_call" | custom-call | bytes 22400000 | tf_op jit(solution)/shard_map/pallas_call | solution.py:65
  469.8 7.4 %collective-permute-done.26 = bf16[2,2,2,128,512]{4,3,2,1,0:T(8,128)(2,1)} collective-permute-done((bf16[2,2,2,128,512]{4,3,2,1,0:T(8,128)(2,1)}, bf16[2,2,2,128,512]{4,3,2,1,0:T(8,128)(2,1)}, u32[]{:S(2)}, u32[]{:S(2)}) %collective-permute-start.26) | collective-permute-done | bytes 1048608 | tf_op jit(solution)/shard_map/ppermute | solution.py:198
  479.8 7.4 %shard_map.541 = (bf16[1,2,4,96,512]{4,3,2,1,0:T(8,128)(2,1)S(1)}, bf16[1,2,4,96,512]{4,3,2,1,0:T(8,128)(2,1)S(1)}, bf16[1,4,2,96,512]{4,3,2,1,0:T(8,128)(2,1)}, bf16[1,4,2,96,512]{4,3,2,1,0:T(8,128)(2,1)S(1)}) custom-call(s32[2]{0:T(128)S(1)} %pad_add_fusion.2.refs_0_, bf16[1,2,4,2,96,1024]{5,4,3,2,1,0:T(8,128)(2,1)} %bitcast.450, ...), custom_call_target="tpu_custom_call" | custom-call | bytes 14092861 | tf_op jit(solution)/shard_map/pallas_call | solution.py:65
  513.7 9.6 %collective-permute-done.29 = bf16[2,2,128,512]{3,2,1,0:T(8,128)(2,1)S(1)} collective-permute-done((bf16[2,2,128,512]{3,2,1,0:T(8,128)(2,1)S(1)}, bf16[2,2,128,512]{3,2,1,0:T(8,128)(2,1)S(1)}, u32[]{:S(2)}, u32[]{:S(2)}) %collective-permute-start.29) | collective-permute-done | bytes 524320 | tf_op jit(solution)/shard_map/ppermute | solution.py:198
  583.4 6.5 %collective-permute-done.42 = bf16[2,96,1024]{2,1,0:T(8,128)(2,1)S(1)} collective-permute-done((bf16[2,96,1024]{2,1,0:T(8,128)(2,1)S(1)}, bf16[2,96,1024]{2,1,0:T(8,128)(2,1)S(1)}, u32[]{:S(2)}, u32[]{:S(2)}) %collective-permute-start.42) | collective-permute-done | bytes 393248 | tf_op jit(solution)/shard_map/ppermute | solution.py:198
  591.7 9.4 %collective-permute-done.41 = bf16[2,96,1024]{2,1,0:T(8,128)(2,1)S(1)} collective-permute-done((bf16[2,96,1024]{2,1,0:T(8,128)(2,1)S(1)}, bf16[2,96,1024]{2,1,0:T(8,128)(2,1)S(1)}, u32[]{:S(2)}, u32[]{:S(2)}) %collective-permute-start.41) | collective-permute-done | bytes 393248 | tf_op jit(solution)/shard_map/ppermute | solution.py:198
  604.3 8.5 %collective-permute-done.43.refs_1_ = bf16[96,1024]{1,0:T(8,128)(2,1)S(1)} collective-permute-done((bf16[96,1024]{1,0:T(8,128)(2,1)S(1)}, bf16[96,1024]{1,0:T(8,128)(2,1)S(1)}, u32[]{:S(2)}, u32[]{:S(2)}) %collective-permute-start.43) | collective-permute-done | bytes 196640 | tf_op jit(solution)/shard_map/ppermute | solution.py:198
  (598 shorter events, 367.1 us)
Async XLA Ops:
  7.2 135.4 %all-gather.5.cloned.1.call-start = ((), (), s32[]{:S(2)}) async-start(), calls=%async_computation.2 | async-start | bytes 16220160 | tf_op jit(solution)/shard_map/all_gather | solution.py:177
  12.5 332.8 %all-gather.7.cloned.1.call-start = ((), (), s32[]{:S(2)}) async-start(), calls=%async_computation.3 | async-start | bytes 20545536 | tf_op jit(solution)/shard_map/all_gather | solution.py:177
  115.4 497.4 %reduce-scatter.2.cloned.1.call-start = ((), (), s32[]{:S(2)}) async-start(), calls=%async_computation.1 | async-start | bytes 6488064 | tf_op jit(solution)/shard_map/reduce_scatter | solution.py:511
  269.7 52.7 %collective-permute-start.13 = (bf16[2,8,96,768]{3,2,1,0:T(8,128)(2,1)}, bf16[2,8,96,768]{3,2,1,0:T(8,128)(2,1)}, u32[]{:S(2)}, u32[]{:S(2)}) collective-permute-start(bf16[2,8,96,768]{3,2,1,0:T(8,128)(2,1)} %get-tuple-element.167.refs_5_), channel_id=1, source_target_pairs={{0,8},{8,0},{16,24},{24,16},{1,9},{9,1},{17,25},{25,17},{2,10},{10... | collective-permute-start | bytes 7077896 | tf_op jit(solution)/shard_map/ppermute | solution.py:198
  280.7 41.7 %collective-permute-start.14 = (bf16[2,8,96,768]{3,2,1,0:T(8,128)(2,1)}, bf16[2,8,96,768]{3,2,1,0:T(8,128)(2,1)}, u32[]{:S(2)}, u32[]{:S(2)}) collective-permute-start(bf16[2,8,96,768]{3,2,1,0:T(8,128)(2,1)} %get-tuple-element.169.refs_3_), channel_id=1, source_target_pairs={{0,8},{8,0},{16,24},{24,16},{1,9},{9,1},{17,25},{25,17},{2,10},{10... | collective-permute-start | bytes 7077896 | tf_op jit(solution)/shard_map/ppermute | solution.py:198
  295.3 27.1 %collective-permute-start.15 = (bf16[2,8,32,768]{3,2,1,0:T(8,128)(2,1)}, bf16[2,8,32,768]{3,2,1,0:T(8,128)(2,1)}, u32[]{:S(2)}, u32[]{:S(2)}) collective-permute-start(bf16[2,8,32,768]{3,2,1,0:T(8,128)(2,1)} %get-tuple-element.170.refs_5_), channel_id=1, source_target_pairs={{0,8},{8,0},{16,24},{24,16},{1,9},{9,1},{17,25},{25,17},{2,10},{10... | collective-permute-start | bytes 2359304 | tf_op jit(solution)/shard_map/ppermute | solution.py:198
  308.2 24.5 %collective-permute-start.11 = (bf16[2,2,96,384]{3,2,1,0:T(8,128)(2,1)}, bf16[2,2,96,384]{3,2,1,0:T(8,128)(2,1)S(1)}, u32[]{:S(2)}, u32[]{:S(2)}) collective-permute-start(bf16[2,2,96,384]{3,2,1,0:T(8,128)(2,1)} %bitcast.413), channel_id=1, source_target_pairs={{0,16},{8,24},{16,0},{24,8},{1,17},{9,25},{17,1},{25,9},{2,18},{10... | collective-permute-start | bytes 884744 | tf_op jit(solution)/shard_map/ppermute | solution.py:198
  309.7 22.9 %collective-permute-start.12 = (bf16[2,2,96,384]{3,2,1,0:T(8,128)(2,1)}, bf16[2,2,96,384]{3,2,1,0:T(8,128)(2,1)S(1)}, u32[]{:S(2)}, u32[]{:S(2)}) collective-permute-start(bf16[2,2,96,384]{3,2,1,0:T(8,128)(2,1)} %bitcast.441), channel_id=1, source_target_pairs={{0,1},{1,0},{2,3},{3,2},{4,5},{5,4},{6,7},{7,6},{8,9},{9,8},{10,11... | collective-permute-start | bytes 884744 | tf_op jit(solution)/shard_map/ppermute | solution.py:198
  336.3 37.0 %collective-permute-start.16 = (bf16[2,96,768]{2,1,0:T(8,128)(2,1)S(1)}, bf16[2,96,768]{2,1,0:T(8,128)(2,1)}, u32[]{:S(2)}, u32[]{:S(2)}) collective-permute-start(bf16[2,96,768]{2,1,0:T(8,128)(2,1)S(1)} %bitcast.407), channel_id=1, source_target_pairs={{0,2},{1,3},{2,0},{3,1},{4,6},{5,7},{6,4},{7,5},{8,10},{9,11},{10,... | collective-permute-start | bytes 884744 | tf_op jit(solution)/shard_map/ppermute | solution.py:198
  337.3 51.4 %collective-permute-start.18 = (bf16[2,2,2,224,384]{4,3,2,1,0:T(8,128)(2,1)}, bf16[2,2,2,224,384]{4,3,2,1,0:T(8,128)(2,1)}, u32[]{:S(2)}, u32[]{:S(2)}) collective-permute-start(bf16[2,2,2,224,384]{4,3,2,1,0:T(8,128)(2,1)} %bitcast.106), channel_id=1, source_target_pairs={{0,1},{1,0},{2,3},{3,2},{4,5},{5,4},{6,7},{7,6},{8,9},{9,8},{10,11... | collective-permute-start | bytes 4128776 | tf_op jit(solution)/shard_map/ppermute | solution.py:198
  338.5 50.2 %collective-permute-start.19 = (bf16[2,2,2,224,384]{4,3,2,1,0:T(8,128)(2,1)}, bf16[2,2,2,224,384]{4,3,2,1,0:T(8,128)(2,1)}, u32[]{:S(2)}, u32[]{:S(2)}) collective-permute-start(bf16[2,2,2,224,384]{4,3,2,1,0:T(8,128)(2,1)} %bitcast.109), channel_id=1, source_target_pairs={{0,16},{8,24},{16,0},{24,8},{1,17},{9,25},{17,1},{25,9},{2,18},{10... | collective-permute-start | bytes 4128776 | tf_op jit(solution)/shard_map/ppermute | solution.py:198
  405.0 23.2 %collective-permute-start.23 = (bf16[2,8,128,1024]{3,2,1,0:T(8,128)(2,1)}, bf16[2,8,128,1024]{3,2,1,0:T(8,128)(2,1)}, u32[]{:S(2)}, u32[]{:S(2)}) collective-permute-start(bf16[2,8,128,1024]{3,2,1,0:T(8,128)(2,1)} %get-tuple-element.199.refs_5_), channel_id=1, source_target_pairs={{0,8},{8,0},{16,24},{24,16},{1,9},{9,1},{17,25},{25,17},{2,10},{10... | collective-permute-start | bytes 12582920 | tf_op jit(solution)/shard_map/ppermute | solution.py:198
  449.5 30.3 %collective-permute-start.25 = (bf16[2,8,96,1024]{3,2,1,0:T(8,128)(2,1)S(1)}, bf16[2,8,96,1024]{3,2,1,0:T(8,128)(2,1)}, u32[]{:S(2)}, u32[]{:S(2)}) collective-permute-start(bf16[2,8,96,1024]{3,2,1,0:T(8,128)(2,1)S(1)} %get-tuple-element.209.refs_5_), channel_id=1, source_target_pairs={{0,8},{8,0},{16,24},{24,16},{1,9},{9,1},{17,25},{25,17},{2,10},{10... | collective-permute-start | bytes 9437192 | tf_op jit(solution)/shard_map/ppermute | solution.py:198
  452.3 24.9 %collective-permute-start.26 = (bf16[2,2,2,128,512]{4,3,2,1,0:T(8,128)(2,1)}, bf16[2,2,2,128,512]{4,3,2,1,0:T(8,128)(2,1)}, u32[]{:S(2)}, u32[]{:S(2)}) collective-permute-start(bf16[2,2,2,128,512]{4,3,2,1,0:T(8,128)(2,1)} %bitcast.344), channel_id=1, source_target_pairs={{0,1},{1,0},{2,3},{3,2},{4,5},{5,4},{6,7},{7,6},{8,9},{9,8},{10,11... | collective-permute-start | bytes 3145736 | tf_op jit(solution)/shard_map/ppermute | solution.py:198
  453.0 24.6 %collective-permute-start.27 = (bf16[2,2,2,128,512]{4,3,2,1,0:T(8,128)(2,1)}, bf16[2,2,2,128,512]{4,3,2,1,0:T(8,128)(2,1)}, u32[]{:S(2)}, u32[]{:S(2)}) collective-permute-start(bf16[2,2,2,128,512]{4,3,2,1,0:T(8,128)(2,1)} %bitcast.434), channel_id=1, source_target_pairs={{0,16},{8,24},{16,0},{24,8},{1,17},{9,25},{17,1},{25,9},{2,18},{10... | collective-permute-start | bytes 3145736 | tf_op jit(solution)/shard_map/ppermute | solution.py:198
  458.4 28.9 %collective-permute-start.24 = (bf16[224,768]{1,0:T(8,128)(2,1)}, bf16[224,768]{1,0:T(8,128)(2,1)}, u32[]{:S(2)}, u32[]{:S(2)}) collective-permute-start(bf16[224,768]{1,0:T(8,128)(2,1)} %bitcast.405), channel_id=1, source_target_pairs={{0,4},{1,5},{2,6},{3,7},{4,0},{5,1},{6,2},{7,3},{8,12},{9,13},{10,... | collective-permute-start | bytes 1032200 | tf_op jit(solution)/shard_map/ppermute | solution.py:198
  499.0 26.7 %collective-permute-start.28 = (bf16[2,8,96,1024]{3,2,1,0:T(8,128)(2,1)}, bf16[2,8,96,1024]{3,2,1,0:T(8,128)(2,1)}, u32[]{:S(2)}, u32[]{:S(2)}) collective-permute-start(bf16[2,8,96,1024]{3,2,1,0:T(8,128)(2,1)} %get-tuple-element.227.refs_5_), channel_id=1, source_target_pairs={{0,8},{8,0},{16,24},{24,16},{1,9},{9,1},{17,25},{25,17},{2,10},{10... | collective-permute-start | bytes 9437192 | tf_op jit(solution)/shard_map/ppermute | solution.py:198
  508.6 34.4 %collective-permute-start.34 = (bf16[2,2,2,96,512]{4,3,2,1,0:T(8,128)(2,1)S(1)}, bf16[2,2,2,96,512]{4,3,2,1,0:T(8,128)(2,1)S(1)}, u32[]{:S(2)}, u32[]{:S(2)}) collective-permute-start(bf16[2,2,2,96,512]{4,3,2,1,0:T(8,128)(2,1)S(1)} %bitcast.346), channel_id=1, source_target_pairs={{0,1},{1,0},{2,3},{3,2},{4,5},{5,4},{6,7},{7,6},{8,9},{9,8},{10,11... | collective-permute-start | bytes 2359304 | tf_op jit(solution)/shard_map/ppermute | solution.py:198
  510.1 35.6 %collective-permute-start.35 = (bf16[2,2,2,96,512]{4,3,2,1,0:T(8,128)(2,1)}, bf16[2,2,2,96,512]{4,3,2,1,0:T(8,128)(2,1)S(1)}, u32[]{:S(2)}, u32[]{:S(2)}) collective-permute-start(bf16[2,2,2,96,512]{4,3,2,1,0:T(8,128)(2,1)} %bitcast.167), channel_id=1, source_target_pairs={{0,16},{8,24},{16,0},{24,8},{1,17},{9,25},{17,1},{25,9},{2,18},{10... | collective-permute-start | bytes 2359304 | tf_op jit(solution)/shard_map/ppermute | solution.py:198
  524.2 32.8 %collective-permute-start.33 = (bf16[2,128,1024]{2,1,0:T(8,128)(2,1)S(1)}, bf16[2,128,1024]{2,1,0:T(8,128)(2,1)S(1)}, u32[]{:S(2)}, u32[]{:S(2)}) collective-permute-start(bf16[2,128,1024]{2,1,0:T(8,128)(2,1)S(1)} %bitcast.381), channel_id=1, source_target_pairs={{0,2},{1,3},{2,0},{3,1},{4,6},{5,7},{6,4},{7,5},{8,10},{9,11},{10,... | collective-permute-start | bytes 1572872 | tf_op jit(solution)/shard_map/ppermute | solution.py:198
  531.6 28.3 %collective-permute-start.31 = (bf16[2,2,2,96,512]{4,3,2,1,0:T(8,128)(2,1)S(1)}, bf16[2,2,2,96,512]{4,3,2,1,0:T(8,128)(2,1)S(1)}, u32[]{:S(2)}, u32[]{:S(2)}) collective-permute-start(bf16[2,2,2,96,512]{4,3,2,1,0:T(8,128)(2,1)S(1)} %bitcast.353), channel_id=1, source_target_pairs={{0,1},{1,0},{2,3},{3,2},{4,5},{5,4},{6,7},{7,6},{8,9},{9,8},{10,11... | collective-permute-start | bytes 2359304 | tf_op jit(solution)/shard_map/ppermute | solution.py:198
  533.0 30.9 %collective-permute-start.32 = (bf16[2,2,2,96,512]{4,3,2,1,0:T(8,128)(2,1)S(1)}, bf16[2,2,2,96,512]{4,3,2,1,0:T(8,128)(2,1)S(1)}, u32[]{:S(2)}, u32[]{:S(2)}) collective-permute-start(bf16[2,2,2,96,512]{4,3,2,1,0:T(8,128)(2,1)S(1)} %bitcast.435), channel_id=1, source_target_pairs={{0,16},{8,24},{16,0},{24,8},{1,17},{9,25},{17,1},{25,9},{2,18},{10... | collective-permute-start | bytes 2359304 | tf_op jit(solution)/shard_map/ppermute | solution.py:198
  546.6 25.8 %collective-permute-start.39 = (bf16[2,2,96,512]{3,2,1,0:T(8,128)(2,1)S(1)}, bf16[2,2,96,512]{3,2,1,0:T(8,128)(2,1)S(1)}, u32[]{:S(2)}, u32[]{:S(2)}) collective-permute-start(bf16[2,2,96,512]{3,2,1,0:T(8,128)(2,1)S(1)} %bitcast.393), channel_id=1, source_target_pairs={{0,16},{8,24},{16,0},{24,8},{1,17},{9,25},{17,1},{25,9},{2,18},{10... | collective-permute-start | bytes 1179656 | tf_op jit(solution)/shard_map/ppermute | solution.py:198
  547.0 25.4 %collective-permute-start.40 = (bf16[2,2,96,512]{3,2,1,0:T(8,128)(2,1)S(1)}, bf16[2,2,96,512]{3,2,1,0:T(8,128)(2,1)S(1)}, u32[]{:S(2)}, u32[]{:S(2)}) collective-permute-start(bf16[2,2,96,512]{3,2,1,0:T(8,128)(2,1)S(1)} %bitcast.439), channel_id=1, source_target_pairs={{0,1},{1,0},{2,3},{3,2},{4,5},{5,4},{6,7},{7,6},{8,9},{9,8},{10,11... | collective-permute-start | bytes 1179656 | tf_op jit(solution)/shard_map/ppermute | solution.py:198
  (176 other events, 1516.0 us)
Sparse Core Ops, SparseCore 0:
  12.6 129.9 all-gather.4
  145.5 130.2 all-gather.6
  449.7 128.6 reduce-scatter.1

commit v4 on v3

--- a/solution.py
+++ b/solution.py
@@ -616,6 +616,23 @@
     ]
 
 
+def passed_kernel(given_ref, same_ref):
+    pass
+
+
+def passed(array):
+    anywhere = pl.BlockSpec(memory_space=pl.ANY)
+    return ordered_call(
+        passed_kernel,
+        [array],
+        [anywhere],
+        out_specs=anywhere,
+        out_shape=jax.ShapeDtypeStruct(array.shape, array.dtype),
+        input_output_aliases={0: 0},
+        cost_estimate=takes(0),
+    )
+
+
 def added_kernel(kept_ref, got_ref, total_ref):
     total_ref[...] = kept_ref[...].astype(F32) + got_ref[...].astype(F32)
 
@@ -638,13 +655,15 @@
         self.width, self.sizes, self.core, self.bits = width, sizes, core, mesh_bits(sizes)
         self.plan = [list(pair) for pair in zip(x_bits + y_bits, y_bits + x_bits)] + [[which] for which in z_bits]
         self.kernels = sizes["aligned"] and len(core) == 1 and bool(y_bits) and len(x_bits) == len(y_bits)
-        self.terms, self.flying, self.parts = [], [], None
-
-    def add(self, rows, *pieces):
+        self.held, self.terms, self.flying, self.parts = [], [], [], None
+
+    def add(self, rows, *pieces, later=False):
         devices = self.sizes["gx"] * self.sizes["gy"]
         if self.kernels:
             away, kept = pack_terms(pieces, rows, self.width, self.sizes)
-            self.terms.append((kept, exchange(away, self.core[0])))
+            self.held.append((away, kept))
+            if not later:
+                self.send()
             return
         packed = jnp.zeros((devices, rows, self.width), BF16)
         for piece in pieces:
@@ -658,6 +677,14 @@
                 packed = lax.dynamic_update_slice(packed, block, (0, at, 0))
                 at += block.shape[1]
         self.terms.append(packed)
+
+    def send(self):
+        for away, kept in self.held:
+            self.terms.append((kept, exchange(away, self.core[0])))
+        self.held = []
+
+    def hold(self):
+        self.held = [(passed(away), kept) for away, kept in self.held]
 
     def advance(self):
         sends = None
@@ -1049,18 +1076,21 @@
         1,
     )
     g_vector = jnp.pad(g_vector, ((0, 0), (0, vector_rows - len(vectors)), (0, 0)))
-    sum_c.advance()
-    sum_e.advance()
-    sum_b.advance()
     sum_d.add(
         row_query + row_image,
         (0, text_rows, d_key_text),
         (row_text, text_rows, d_value_text),
         (row_query, image_rows, d_query_image),
         (row_vector, g_vector),
+        later=True,
     )
     sum_c.advance()
+    sum_d.hold()
+    sum_d.send()
+    sum_e.advance()
     sum_d.advance()
+    sum_c.advance()
+    sum_b.advance()
     grad_text = (
         d_resid_text
         + project_back(d_query_text, weight_text_query)
@@ -1072,6 +1102,7 @@
         + project_back(jnp.concatenate([d_key_image, d_value_image], 1), weight_image_held)
     )
     sum_e.advance()
+    sums_first = widened(sums_first)
     sum_c.advance()
     sum_d.advance()
     sum_e.advance()
@@ -1079,14 +1110,11 @@
     sum_d.advance()
     sum_e.advance()
     sum_d.advance()
-    sum_e.advance()
-    sum_d.advance()
 
     def owned(total, pieces):
         return [total[start:end] for start, end in starts(pieces)]
 
-    sums_first = widened(sums_first)
-    sums_a, sums_b, sums_c, sums_d, sums_e = [one.result() for one in (sum_a, sum_b, sum_c, sum_d, sum_e)]
+    sums_a, sums_b, sums_c, sums_e, sums_d = [one.result() for one in (sum_a, sum_b, sum_c, sum_e, sum_d)]
     text_selfs = owned(sums_a, text_pieces[ups + 1 : ups + 5])
     text_sums = owned(sums_b, text_pieces[: ups + 1] + [text_merge])
     image_firsts = owned(sums_first, [image_key, image_value]) + [sums_first[row_first : row_first + row_text]]

time: 636 us -> 617 us (0.970)
  waiting for transfers between devices: 158 us -> 122 us
  local copies, waits for them, and re-layouts: 97.1 us -> 108 us
    ppermute x45, waiting for transfers between devices: 139 us -> 103 us  [exchange(): lax.ppermute(block, axis, [(at, at ^ 1 << bit) for at in range(lax.axis_s...]
    unnamed x318 -> x340, local copies, waits for them, and re-layouts: 47.9 us -> 58.3 us
    pallas_call x59 -> x60, Pallas kernels: 164 us -> 167 us  [ordered_call(): pl.pallas_call(body, in_specs=list(in_specs) + [pl.BlockSpec(memory_space...]
  transfers between devices with their start and end apart: 48 -> 48, of which waited for: 24 -> 20; matrix products, arithmetic and copies ran while one was open for 32% -> 34% of each run, Pallas kernels for 23% -> 25%
where the time goes in v4:
time: 617 us; the launch traced here: 606 us
  Pallas kernels  167 us (27%)
  waiting for transfers between devices  122 us (20%)
  matrix products  112 us (18%)
  local copies, waits for them, and re-layouts  108 us (18%)
  starting transfers between devices  47.3 us (8%)
  other arithmetic  35.5 us (6%)
  between operations  16 us (3%)
    pallas_call x60, Pallas kernels, ordered_call(): pl.pallas_call(body, in_specs=list(in_specs) + [pl.BlockSpec(memory_space...  167 us
    ppermute x45, waiting for transfers between devices, exchange(): lax.ppermute(block, axis, [(at, at ^ 1 << bit) for at in range(lax.axis_s...  103 us
    unnamed x340, local copies, waits for them, and re-layouts  58.3 us
    dot_general x14, matrix products, project_back(): lax.dot_general(left, right, (((1,), (1,)), ((), ())), preferred_element_...  58 us
    dot_general x14, matrix products, project(): return jnp.dot(left, right, preferred_element_type=F32)  53.5 us
    ppermute x45, starting transfers between devices, exchange(): lax.ppermute(block, axis, [(at, at ^ 1 << bit) for at in range(lax.axis_s...  47.2 us
    slice x5, local copies, waits for them, and re-layouts, taken(): return whole(block[:, at[0]:at[1]])  27.6 us
    all_gather x2, waiting for transfers between devices, gather(): return lax.all_gather(packed, AXES, axis=0, tiled=False)  18.4 us
  transfers between devices with their start and end apart: 48, of which 20 were waited for; matrix products, arithmetic and copies ran while one was open for 34% of the time, Pallas kernels for 25%

profile of v4, /device:TPU:0, one launch (start us, length us, event | category | flops | bytes accessed | tf_op | source)
XLA Modules:
  0.0 606.1 jit_solution(4505432022978475693)
XLA Ops:
  25.4 15.8 %collective-permute-done = bf16[96,1024]{1,0:T(8,128)(2,1)S(1)} collective-permute-done((bf16[96,1024]{1,0:T(8,128)(2,1)S(1)}, bf16[96,1024]{1,0:T(8,128)(2,1)S(1)}, u32[]{:S(2)}, u32[]{:S(2)}) %collective-permute-start) | collective-permute-done | bytes 196640 | tf_op jit(solution)/shard_map/ppermute | solution.py:198
  43.8 9.3 %collective-permute-done.1 = bf16[2,96,1024]{2,1,0:T(8,128)(2,1)S(1)} collective-permute-done((bf16[2,96,1024]{2,1,0:T(8,128)(2,1)S(1)}, bf16[2,96,1024]{2,1,0:T(8,128)(2,1)S(1)}, u32[]{:S(2)}, u32[]{:S(2)}) %collective-permute-start.1) | collective-permute-done | bytes 393248 | tf_op jit(solution)/shard_map/ppermute | solution.py:198
  56.0 12.6 %collective-permute-done.2 = bf16[2,2,96,512]{3,2,1,0:T(8,128)(2,1)S(1)} collective-permute-done((bf16[2,2,96,512]{3,2,1,0:T(8,128)(2,1)S(1)}, bf16[2,2,96,512]{3,2,1,0:T(8,128)(2,1)S(1)}, u32[]{:S(2)}, u32[]{:S(2)}) %collective-permute-start.2) | collective-permute-done | bytes 393248 | tf_op jit(solution)/shard_map/ppermute | solution.py:198
  76.5 16.0 %collective-permute-done.4 = bf16[2,2,2,96,512]{4,3,2,1,0:T(8,128)(2,1)S(1)} collective-permute-done((bf16[2,2,2,96,512]{4,3,2,1,0:T(8,128)(2,1)S(1)}, bf16[2,2,2,96,512]{4,3,2,1,0:T(8,128)(2,1)S(1)}, u32[]{:S(2)}, u32[]{:S(2)}) %collective-permute-start.4) | collective-permute-done | bytes 786464 | tf_op jit(solution)/shard_map/ppermute | solution.py:198
  124.2 18.4 %all-gather.5.cloned.1.call-done = bf16[10240,768]{1,0:T(8,128)(2,1)} async-done(((bf16[320,768]{1,0:T(8,128)(2,1)}), bf16[10240,768]{1,0:T(8,128)(2,1)}) %all-gather.5.cloned.1.call-update) | async-done | bytes 15728656 | tf_op jit(solution)/shard_map/all_gather | solution.py:177
  152.1 7.1 %fusion.46 = (bf16[32,24,768]{2,1,0:T(8,128)(2,1)}, bf16[32,24,768]{2,1,0:T(8,128)(2,1)}, bf16[32,24,768]{2,1,0:T(8,128)(2,1)}, bf16[32,24,768]{2,1,0:T(8,128)(2...) fusion(bf16[32,320,768]{2,1,0:T(8,128)(2,1)} %bitcast.445), kind=kLoop, calls=%fused_computation.187 | loop fusion | bytes 18874368 | tf_op jit(solution)/shard_map/slice | solution.py:838
  159.2 16.3 %add_convert_fusion = (bf16[832,3072]{1,0:T(8,128)(2,1)}, bf16[832,3072]{1,0:T(8,128)(2,1)S(1)}) fusion(f32[3072]{0:T(1024)S(1)} %reshape.932, bf16[832,768]{1,0:T(8,128)(2,1)S(1)} %multiply_convert_fusion.3.refs_0_, bf16[768,768]{1,0:T(8,128)(2,1)S(1)} %bitcast.484, bf16[768,768]{1,0:T(8,128)(2,1)S(1)} %bitcast.486, bf16[768,768]{1,0:T(8,128)(2,1)S(1)} %bitcast.488, ...), kind=kOutput, calls=%fused_computation.7 | convolution fusion | flops 4011196416 | bytes 16232448 | tf_op jit(solution)/shard_map/dot_general | solution.py:35
  175.5 8.6 %fusion.55 = (f32[832]{0:T(1024)S(1)}, f32[832,768]{1,0:T(8,128)S(1)}) fusion(bf16[832,3072]{1,0:T(8,128)(2,1)S(1)} %get-tuple-element.153.refs_0_, bf16[3072,768]{1,0:T(8,128)(2,1)} %bitcast.456, f32[768]{0:T(1024)S(1)} %reshape.931, f32[832]{0:T(1024)S(1)} %add_rsqrt_fusion.2, f32[832,768]{1,0:T(8,128)S(1)} %get-tuple-element.346, ...), kind=kOutput, calls=%fused_computation.196 | convolution fusion | flops 3929062656 | bytes 14955264 | tf_op jit(solution)/shard_map/dot_general | solution.py:35
  209.5 8.9 %shard_map.511 = (bf16[8,104,768]{2,1,0:T(8,128)(2,1)S(1)}, bf16[8,104,768]{2,1,0:T(8,128)(2,1)S(1)}, bf16[8,104,768]{2,1,0:T(8,128)(2,1)S(1)}) custom-call(bf16[8,104,2304]{2,1,0:T(8,128)(2,1)} %bitcast.435, bf16[8,104,2304]{2,1,0:T(8,128)(2,1)} %bitcast.436, bf16[8,104,2304]{2,1,0:T(8,128)(2,1)} %bitcast.437, f32[8,104,128]{2,1,0:T(8,128)S(1)} %broadcast_in_dim.77.refs_3_, ...), custom_call_target="tpu_custom_call" | custom-call | bytes 22400000 | tf_op jit(solution)/shard_map/pallas_call | solution.py:65
  220.5 7.3 %shard_map.512 = (bf16[2,8,96,768]{3,2,1,0:T(8,128)(2,1)}, bf16[2,8,96,768]{3,2,1,0:T(8,128)(2,1)}) custom-call(bf16[832,768]{1,0:T(8,128)(2,1)S(1)} %multiply_convert_fusion.2.refs_0_, bf16[832,2304]{1,0:T(8,128)(2,1)} %bitcast.446, s32[1]{0:T(128)} %bitcast.64.refs_2_.refs_1_, bf16[8,104,768]{2,1,0:T(8,128)(2,1)S(1)} %get-tuple-element.155.refs_3_), custom_call_target="tpu_custom_call" | custom-call | bytes 24137964 | tf_op jit(solution)/shard_map/pallas_call | solution.py:65
  235.1 8.2 %multiply_reduce_fusion.1 = (bf16[768]{0:T(1024)(128)(2,1)}, f32[832]{0:T(1024)S(1)}, f32[832]{0:T(1024)S(1)}, f32[832,768]{1,0:T(8,128)S(1)}) fusion(f32[832,768]{1,0:T(8,128)S(1)} %copy-done.100, f32[832]{0:T(1024)S(1)} %add_rsqrt_fusion.1, f32[832]{0:T(1024)S(1)} %broadcast_multiply_fusion.8, f32[768]{0:T(1024)S(1)} %reshape.933, ...), kind=kOutput, calls=%fused_computation.24 | convolution fusion | flops 2960766720 | bytes 15058432 | tf_op jit(solution)/shard_map/dot_general | solution.py:39
  251.6 8.4 %fusion.60 = (bf16[3072]{0:T(1024)(128)(2,1)}, bf16[832,3072]{1,0:T(8,128)(2,1)}) fusion(bf16[832,768]{1,0:T(8,128)(2,1)S(1)} %get-tuple-element.288.refs_1_, bf16[3072,768]{1,0:T(8,128)(2,1)S(1)} %bitcast.459, bf16[832,3072]{1,0:T(8,128)(2,1)} %get-tuple-element.158), kind=kOutput, calls=%fused_computation.201 | convolution fusion | flops 3936089088 | bytes 16226304 | tf_op jit(solution)/shard_map/dot_general | solution.py:39
  260.0 8.8 %shard_map.515 = (bf16[2,8,96,768]{3,2,1,0:T(8,128)(2,1)}, bf16[2,8,96,768]{3,2,1,0:T(8,128)(2,1)}) custom-call(bf16[832,768]{1,0:T(8,128)(2,1)S(1)} %copy-done.32, bf16[832,3072]{1,0:T(8,128)(2,1)} %get-tuple-element.362.refs_1_, s32[1]{0:T(128)} %bitcast.64.refs_2_.refs_1_, bf16[1,2,4,96,384]{4,3,2,1,0:T(8,128)(2,1)S(1)} %get-tuple-element.164.refs_3_), custom_call_target="tpu_custom_call" | custom-call | bytes 31117288 | tf_op jit(solution)/shard_map/pallas_call | solution.py:65
  269.8 10.1 %shard_map.517 = (bf16[2,8,96,768]{3,2,1,0:T(8,128)(2,1)}, bf16[2,8,96,768]{3,2,1,0:T(8,128)(2,1)}) custom-call(bf16[832,3072]{1,0:T(8,128)(2,1)} %copy-done.118, bf16[832,768]{1,0:T(8,128)(2,1)S(1)} %get-tuple-element.288.refs_1_, s32[1]{0:T(128)} %bitcast.64.refs_2_.refs_1_, bf16[1,4,96,384]{3,2,1,0:T(8,128)(2,1)S(1)} %get-tuple-element.168.refs_3_), custom_call_target="tpu_custom_call" | custom-call | bytes 31117288 | tf_op jit(solution)/shard_map/pallas_call | solution.py:65
  280.4 10.5 %multiply_reduce_fusion.2 = (bf16[768]{0:T(1024)(128)(2,1)}, f32[832]{0:T(1024)S(1)}, f32[832]{0:T(1024)S(1)}, f32[832,768]{1,0:T(8,128)S(1)}) fusion(f32[832,768]{1,0:T(8,128)S(1)} %copy-done.98, f32[832]{0:T(1024)S(1)} %add_rsqrt_fusion.2, f32[832]{0:T(1024)S(1)} %broadcast_multiply_fusion.9, f32[768]{0:T(1024)S(1)} %reshape.931, ...), kind=kOutput, calls=%fused_computation.25 | convolution fusion | flops 3950491392 | bytes 17516032 | tf_op jit(solution)/shard_map/dot_general | solution.py:39
  316.1 6.6 %shard_map.519 = (bf16[8,104,1024]{2,1,0:T(8,128)(2,1)S(1)}, bf16[8,40,1024]{2,1,0:T(8,128)(2,1)S(1)}, bf16[8,40,1024]{2,1,0:T(8,128)(2,1)S(1)}) custom-call(bf16[8,104,1024]{2,1,0:T(8,128)(2,1)} %bitcast.454, bf16[8,40,2048]{2,1,0:T(8,128)(2,1)S(1)} %bitcast.295, bf16[8,40,2048]{2,1,0:T(8,128)(2,1)S(1)} %bitcast.296, ...), custom_call_target="tpu_custom_call" | custom-call | bytes 22400000 | tf_op jit(solution)/shard_map/pallas_call | solution.py:65
  323.9 9.0 %shard_map.520 = (bf16[1,2,4,224,384]{4,3,2,1,0:T(8,128)(2,1)}, bf16[1,2,4,224,384]{4,3,2,1,0:T(8,128)(2,1)S(1)}, bf16[1,4,2,224,384]{4,3,2,1,0:T(8,128)(2,1)}, bf16[1,4,2,224,384]{4,3,2,1,0:T(8,128)(2,1)}) custom-call(s32[2]{0:T(128)S(1)} %pad_add_fusion.2.refs_0_, bf16[1,2,4,2,96,768]{5,4,3,2,1,0:T(8,128)(2,1)} %bitcast.461, ...), custom_call_target="tpu_custom_call" | custom-call | bytes 24662508 | tf_op jit(solution)/shard_map/pallas_call | solution.py:65
  349.8 10.3 %fusion.44 = (bf16[32,32,1024]{2,1,0:T(8,128)(2,1)}, bf16[32,32,1024]{2,1,0:T(8,128)(2,1)S(1)}, bf16[32,32,1024]{2,1,0:T(8,128)(2,1)}, bf16[32,32,1024]{2,1,0:T(...) fusion(bf16[32,304,1024]{2,1,0:T(8,128)(2,1)} %bitcast.441), kind=kLoop, calls=%fused_computation.185 | loop fusion | bytes 33554432 | tf_op jit(solution)/shard_map/slice | solution.py:838
  431.2 7.3 %shard_map.534 = (bf16[1,2,4,128,512]{4,3,2,1,0:T(8,128)(2,1)}, bf16[1,2,4,128,512]{4,3,2,1,0:T(8,128)(2,1)S(1)}, bf16[1,4,2,128,512]{4,3,2,1,0:T(8,128)(2,1)S(1)}, bf16[1,4,2,128,512]{4,3,2,1,0:T(8,128)(2,1)S(1)}) custom-call(s32[2]{0:T(128)S(1)} %pad_add_fusion.2.refs_0_, bf16[1,2,4,2,128,1024]{5,4,3,2,1,0:T(8,128)(2,1)} %bitcast.442, ...), custom_call_target="tpu_custom_call" | custom-call | bytes 18790480 | tf_op jit(solution)/shard_map/pallas_call | solution.py:65
  445.6 11.7 %collective-permute-done.22 = bf16[2,224,768]{2,1,0:T(8,128)(2,1)S(1)} collective-permute-done((bf16[2,224,768]{2,1,0:T(8,128)(2,1)S(1)}, bf16[2,224,768]{2,1,0:T(8,128)(2,1)S(1)}, u32[]{:S(2)}, u32[]{:S(2)}) %collective-permute-start.22) | collective-permute-done | bytes 688160 | tf_op jit(solution)/shard_map/ppermute | solution.py:198
  466.6 7.0 %shard_map.539 = (bf16[8,40,1024]{2,1,0:T(8,128)(2,1)S(1)}, bf16[8,104,1024]{2,1,0:T(8,128)(2,1)S(1)}, bf16[8,104,1024]{2,1,0:T(8,128)(2,1)S(1)}) custom-call(bf16[8,40,1024]{2,1,0:T(8,128)(2,1)S(1)} %bitcast.332, bf16[8,104,2048]{2,1,0:T(8,128)(2,1)} %bitcast.291, bf16[8,104,2048]{2,1,0:T(8,128)(2,1)} %bitcast.292, f32[8,104,128]{2,1,0:T(8,128)S(1)} %copy-done.21, ...), custom_call_target="tpu_custom_call" | custom-call | bytes 22400000 | tf_op jit(solution)/shard_map/pallas_call | solution.py:65
  509.8 6.3 %shard_map.546 = (bf16[1,2,4,96,512]{4,3,2,1,0:T(8,128)(2,1)S(1)}, bf16[1,2,4,96,512]{4,3,2,1,0:T(8,128)(2,1)S(1)}, bf16[1,4,2,96,512]{4,3,2,1,0:T(8,128)(2,1)}, bf16[1,4,2,96,512]{4,3,2,1,0:T(8,128)(2,1)S(1)}) custom-call(s32[2]{0:T(128)S(1)} %pad_add_fusion.2.refs_0_, bf16[1,2,4,2,96,1024]{5,4,3,2,1,0:T(8,128)(2,1)} %bitcast.439, ...), custom_call_target="tpu_custom_call" | custom-call | bytes 14092861 | tf_op jit(solution)/shard_map/pallas_call | solution.py:65
  517.8 7.1 %shard_map.547 = (bf16[1,2,4,96,512]{4,3,2,1,0:T(8,128)(2,1)}, bf16[1,2,4,96,512]{4,3,2,1,0:T(8,128)(2,1)S(1)}, bf16[1,4,2,96,512]{4,3,2,1,0:T(8,128)(2,1)}, bf16[1,4,2,96,512]{4,3,2,1,0:T(8,128)(2,1)S(1)}) custom-call(s32[2]{0:T(128)S(1)} %pad_add_fusion.2.refs_0_, bf16[1,2,4,2,96,1024]{5,4,3,2,1,0:T(8,128)(2,1)} %bitcast.438, ...), custom_call_target="tpu_custom_call" | custom-call | bytes 14092861 | tf_op jit(solution)/shard_map/pallas_call | solution.py:65
  585.9 6.9 %collective-permute-done.44.refs_1_ = bf16[96,1024]{1,0:T(8,128)(2,1)S(1)} collective-permute-done((bf16[96,1024]{1,0:T(8,128)(2,1)S(1)}, bf16[96,1024]{1,0:T(8,128)(2,1)S(1)}, u32[]{:S(2)}, u32[]{:S(2)}) %collective-permute-start.44) | collective-permute-done | bytes 196640 | tf_op jit(solution)/shard_map/ppermute | solution.py:198
  (622 shorter events, 351.7 us)
Async XLA Ops:
  7.2 135.4 %all-gather.5.cloned.1.call-start = ((), (), s32[]{:S(2)}) async-start(), calls=%async_computation.2 | async-start | bytes 16220160 | tf_op jit(solution)/shard_map/all_gather | solution.py:177
  12.5 333.9 %all-gather.7.cloned.1.call-start = ((), (), s32[]{:S(2)}) async-start(), calls=%async_computation.3 | async-start | bytes 20545536 | tf_op jit(solution)/shard_map/all_gather | solution.py:177
  20.3 20.9 %collective-permute-start = (bf16[96,1024]{1,0:T(8,128)(2,1)S(1)}, bf16[96,1024]{1,0:T(8,128)(2,1)S(1)}, u32[]{:S(2)}, u32[]{:S(2)}) collective-permute-start(bf16[96,1024]{1,0:T(8,128)(2,1)S(1)} %shard_map.502.refs_8_), channel_id=1, source_target_pairs={{0,4},{1,5},{2,6},{3,7},{4,0},{5,1},{6,2},{7,3},{8,12},{9,13},{10,... | collective-permute-start | bytes 589832 | tf_op jit(solution)/shard_map/ppermute | solution.py:198
  115.5 432.0 %reduce-scatter.2.cloned.1.call-start = ((), (), s32[]{:S(2)}) async-start(), calls=%async_computation.1 | async-start | bytes 6488064 | tf_op jit(solution)/shard_map/reduce_scatter | solution.py:511
  268.8 55.0 %collective-permute-start.13 = (bf16[2,8,96,768]{3,2,1,0:T(8,128)(2,1)}, bf16[2,8,96,768]{3,2,1,0:T(8,128)(2,1)}, u32[]{:S(2)}, u32[]{:S(2)}) collective-permute-start(bf16[2,8,96,768]{3,2,1,0:T(8,128)(2,1)} %get-tuple-element.167.refs_5_), channel_id=1, source_target_pairs={{0,8},{8,0},{16,24},{24,16},{1,9},{9,1},{17,25},{25,17},{2,10},{10... | collective-permute-start | bytes 7077896 | tf_op jit(solution)/shard_map/ppermute | solution.py:198
  279.9 44.0 %collective-permute-start.14 = (bf16[2,8,96,768]{3,2,1,0:T(8,128)(2,1)}, bf16[2,8,96,768]{3,2,1,0:T(8,128)(2,1)}, u32[]{:S(2)}, u32[]{:S(2)}) collective-permute-start(bf16[2,8,96,768]{3,2,1,0:T(8,128)(2,1)} %get-tuple-element.169.refs_3_), channel_id=1, source_target_pairs={{0,8},{8,0},{16,24},{24,16},{1,9},{9,1},{17,25},{25,17},{2,10},{10... | collective-permute-start | bytes 7077896 | tf_op jit(solution)/shard_map/ppermute | solution.py:198
  295.8 28.0 %collective-permute-start.15 = (bf16[2,8,32,768]{3,2,1,0:T(8,128)(2,1)}, bf16[2,8,32,768]{3,2,1,0:T(8,128)(2,1)}, u32[]{:S(2)}, u32[]{:S(2)}) collective-permute-start(bf16[2,8,32,768]{3,2,1,0:T(8,128)(2,1)} %get-tuple-element.170.refs_5_), channel_id=1, source_target_pairs={{0,8},{8,0},{16,24},{24,16},{1,9},{9,1},{17,25},{25,17},{2,10},{10... | collective-permute-start | bytes 2359304 | tf_op jit(solution)/shard_map/ppermute | solution.py:198
  308.7 25.3 %collective-permute-start.11 = (bf16[2,2,96,384]{3,2,1,0:T(8,128)(2,1)}, bf16[2,2,96,384]{3,2,1,0:T(8,128)(2,1)S(1)}, u32[]{:S(2)}, u32[]{:S(2)}) collective-permute-start(bf16[2,2,96,384]{3,2,1,0:T(8,128)(2,1)} %bitcast.404), channel_id=1, source_target_pairs={{0,16},{8,24},{16,0},{24,8},{1,17},{9,25},{17,1},{25,9},{2,18},{10... | collective-permute-start | bytes 884744 | tf_op jit(solution)/shard_map/ppermute | solution.py:198
  310.9 23.1 %collective-permute-start.12 = (bf16[2,2,96,384]{3,2,1,0:T(8,128)(2,1)}, bf16[2,2,96,384]{3,2,1,0:T(8,128)(2,1)S(1)}, u32[]{:S(2)}, u32[]{:S(2)}) collective-permute-start(bf16[2,2,96,384]{3,2,1,0:T(8,128)(2,1)} %bitcast.430), channel_id=1, source_target_pairs={{0,1},{1,0},{2,3},{3,2},{4,5},{5,4},{6,7},{7,6},{8,9},{9,8},{10,11... | collective-permute-start | bytes 884744 | tf_op jit(solution)/shard_map/ppermute | solution.py:198
  337.8 38.3 %collective-permute-start.16 = (bf16[2,96,768]{2,1,0:T(8,128)(2,1)S(1)}, bf16[2,96,768]{2,1,0:T(8,128)(2,1)S(1)}, u32[]{:S(2)}, u32[]{:S(2)}) collective-permute-start(bf16[2,96,768]{2,1,0:T(8,128)(2,1)S(1)} %bitcast.397), channel_id=1, source_target_pairs={{0,2},{1,3},{2,0},{3,1},{4,6},{5,7},{6,4},{7,5},{8,10},{9,11},{10,... | collective-permute-start | bytes 884744 | tf_op jit(solution)/shard_map/ppermute | solution.py:198
  338.0 54.7 %collective-permute-start.18 = (bf16[2,2,2,224,384]{4,3,2,1,0:T(8,128)(2,1)}, bf16[2,2,2,224,384]{4,3,2,1,0:T(8,128)(2,1)}, u32[]{:S(2)}, u32[]{:S(2)}) collective-permute-start(bf16[2,2,2,224,384]{4,3,2,1,0:T(8,128)(2,1)} %bitcast.106), channel_id=1, source_target_pairs={{0,1},{1,0},{2,3},{3,2},{4,5},{5,4},{6,7},{7,6},{8,9},{9,8},{10,11... | collective-permute-start | bytes 4128776 | tf_op jit(solution)/shard_map/ppermute | solution.py:198
  339.4 53.3 %collective-permute-start.19 = (bf16[2,2,2,224,384]{4,3,2,1,0:T(8,128)(2,1)}, bf16[2,2,2,224,384]{4,3,2,1,0:T(8,128)(2,1)}, u32[]{:S(2)}, u32[]{:S(2)}) collective-permute-start(bf16[2,2,2,224,384]{4,3,2,1,0:T(8,128)(2,1)} %bitcast.109), channel_id=1, source_target_pairs={{0,16},{8,24},{16,0},{24,8},{1,17},{9,25},{17,1},{25,9},{2,18},{10... | collective-permute-start | bytes 4128776 | tf_op jit(solution)/shard_map/ppermute | solution.py:198
  408.3 22.9 %collective-permute-start.23 = (bf16[2,8,128,1024]{3,2,1,0:T(8,128)(2,1)}, bf16[2,8,128,1024]{3,2,1,0:T(8,128)(2,1)}, u32[]{:S(2)}, u32[]{:S(2)}) collective-permute-start(bf16[2,8,128,1024]{3,2,1,0:T(8,128)(2,1)} %get-tuple-element.199.refs_5_), channel_id=1, source_target_pairs={{0,8},{8,0},{16,24},{24,16},{1,9},{9,1},{17,25},{25,17},{2,10},{10... | collective-permute-start | bytes 12582920 | tf_op jit(solution)/shard_map/ppermute | solution.py:198
  438.5 51.9 %collective-permute-start.25 = (bf16[2,2,2,128,512]{4,3,2,1,0:T(8,128)(2,1)}, bf16[2,2,2,128,512]{4,3,2,1,0:T(8,128)(2,1)}, u32[]{:S(2)}, u32[]{:S(2)}) collective-permute-start(bf16[2,2,2,128,512]{4,3,2,1,0:T(8,128)(2,1)} %bitcast.141), channel_id=1, source_target_pairs={{0,1},{1,0},{2,3},{3,2},{4,5},{5,4},{6,7},{7,6},{8,9},{9,8},{10,11... | collective-permute-start | bytes 3145736 | tf_op jit(solution)/shard_map/ppermute | solution.py:198
  439.4 51.0 %collective-permute-start.26 = (bf16[2,2,2,128,512]{4,3,2,1,0:T(8,128)(2,1)S(1)}, bf16[2,2,2,128,512]{4,3,2,1,0:T(8,128)(2,1)}, u32[]{:S(2)}, u32[]{:S(2)}) collective-permute-start(bf16[2,2,2,128,512]{4,3,2,1,0:T(8,128)(2,1)S(1)} %bitcast.425), channel_id=1, source_target_pairs={{0,16},{8,24},{16,0},{24,8},{1,17},{9,25},{17,1},{25,9},{2,18},{10... | collective-permute-start | bytes 3145736 | tf_op jit(solution)/shard_map/ppermute | solution.py:198
  465.0 44.8 %collective-permute-start.24 = (bf16[2,8,96,1024]{3,2,1,0:T(8,128)(2,1)S(1)}, bf16[2,8,96,1024]{3,2,1,0:T(8,128)(2,1)}, u32[]{:S(2)}, u32[]{:S(2)}) collective-permute-start(bf16[2,8,96,1024]{3,2,1,0:T(8,128)(2,1)S(1)} %get-tuple-element.209.refs_5_), channel_id=1, source_target_pairs={{0,8},{8,0},{16,24},{24,16},{1,9},{9,1},{17,25},{25,17},{2,10},{10... | collective-permute-start | bytes 9437192 | tf_op jit(solution)/shard_map/ppermute | solution.py:198
  493.3 23.2 %collective-permute-start.32 = (bf16[2,8,96,1024]{3,2,1,0:T(8,128)(2,1)S(1)}, bf16[2,8,96,1024]{3,2,1,0:T(8,128)(2,1)}, u32[]{:S(2)}, u32[]{:S(2)}) collective-permute-start(bf16[2,8,96,1024]{3,2,1,0:T(8,128)(2,1)S(1)} %shard_map.545.refs_3_), channel_id=1, source_target_pairs={{0,8},{8,0},{16,24},{24,16},{1,9},{9,1},{17,25},{25,17},{2,10},{10... | collective-permute-start | bytes 9437192 | tf_op jit(solution)/shard_map/ppermute | solution.py:198
  499.2 32.8 %collective-permute-start.29 = (bf16[224,768]{1,0:T(8,128)(2,1)S(1)}, bf16[224,768]{1,0:T(8,128)(2,1)S(1)}, u32[]{:S(2)}, u32[]{:S(2)}) collective-permute-start(bf16[224,768]{1,0:T(8,128)(2,1)S(1)} %bitcast.395), channel_id=1, source_target_pairs={{0,4},{1,5},{2,6},{3,7},{4,0},{5,1},{6,2},{7,3},{8,12},{9,13},{10,... | collective-permute-start | bytes 1032200 | tf_op jit(solution)/shard_map/ppermute | solution.py:198
  504.3 20.6 %collective-permute-start.30 = (bf16[2,2,128,512]{3,2,1,0:T(8,128)(2,1)S(1)}, bf16[2,2,128,512]{3,2,1,0:T(8,128)(2,1)S(1)}, u32[]{:S(2)}, u32[]{:S(2)}) collective-permute-start(bf16[2,2,128,512]{3,2,1,0:T(8,128)(2,1)S(1)} %bitcast.376), channel_id=1, source_target_pairs={{0,16},{8,24},{16,0},{24,8},{1,17},{9,25},{17,1},{25,9},{2,18},{10... | collective-permute-start | bytes 1572872 | tf_op jit(solution)/shard_map/ppermute | solution.py:198
  505.1 21.6 %collective-permute-start.31 = (bf16[2,2,128,512]{3,2,1,0:T(8,128)(2,1)S(1)}, bf16[2,2,128,512]{3,2,1,0:T(8,128)(2,1)S(1)}, u32[]{:S(2)}, u32[]{:S(2)}) collective-permute-start(bf16[2,2,128,512]{3,2,1,0:T(8,128)(2,1)S(1)} %bitcast.428), channel_id=1, source_target_pairs={{0,1},{1,0},{2,3},{3,2},{4,5},{5,4},{6,7},{7,6},{8,9},{9,8},{10,11... | collective-permute-start | bytes 1572872 | tf_op jit(solution)/shard_map/ppermute | solution.py:198
  516.1 25.8 %collective-permute-start.27 = (bf16[2,2,2,96,512]{4,3,2,1,0:T(8,128)(2,1)S(1)}, bf16[2,2,2,96,512]{4,3,2,1,0:T(8,128)(2,1)S(1)}, u32[]{:S(2)}, u32[]{:S(2)}) collective-permute-start(bf16[2,2,2,96,512]{4,3,2,1,0:T(8,128)(2,1)S(1)} %bitcast.344), channel_id=1, source_target_pairs={{0,1},{1,0},{2,3},{3,2},{4,5},{5,4},{6,7},{7,6},{8,9},{9,8},{10,11... | collective-permute-start | bytes 2359304 | tf_op jit(solution)/shard_map/ppermute | solution.py:198
  516.5 25.4 %collective-permute-start.28 = (bf16[2,2,2,96,512]{4,3,2,1,0:T(8,128)(2,1)}, bf16[2,2,2,96,512]{4,3,2,1,0:T(8,128)(2,1)S(1)}, u32[]{:S(2)}, u32[]{:S(2)}) collective-permute-start(bf16[2,2,2,96,512]{4,3,2,1,0:T(8,128)(2,1)} %bitcast.149), channel_id=1, source_target_pairs={{0,16},{8,24},{16,0},{24,8},{1,17},{9,25},{17,1},{25,9},{2,18},{10... | collective-permute-start | bytes 2359304 | tf_op jit(solution)/shard_map/ppermute | solution.py:198
  524.9 29.9 %collective-permute-start.33 = (bf16[2,2,2,96,512]{4,3,2,1,0:T(8,128)(2,1)}, bf16[2,2,2,96,512]{4,3,2,1,0:T(8,128)(2,1)S(1)}, u32[]{:S(2)}, u32[]{:S(2)}) collective-permute-start(bf16[2,2,2,96,512]{4,3,2,1,0:T(8,128)(2,1)} %bitcast.161), channel_id=1, source_target_pairs={{0,1},{1,0},{2,3},{3,2},{4,5},{5,4},{6,7},{7,6},{8,9},{9,8},{10,11... | collective-permute-start | bytes 2359304 | tf_op jit(solution)/shard_map/ppermute | solution.py:198
  526.6 28.9 %collective-permute-start.34 = (bf16[2,2,2,96,512]{4,3,2,1,0:T(8,128)(2,1)}, bf16[2,2,2,96,512]{4,3,2,1,0:T(8,128)(2,1)}, u32[]{:S(2)}, u32[]{:S(2)}) collective-permute-start(bf16[2,2,2,96,512]{4,3,2,1,0:T(8,128)(2,1)} %bitcast.164), channel_id=1, source_target_pairs={{0,16},{8,24},{16,0},{24,8},{1,17},{9,25},{17,1},{25,9},{2,18},{10... | collective-permute-start | bytes 2359304 | tf_op jit(solution)/shard_map/ppermute | solution.py:198
  (187 other events, 1532.3 us)
Sparse Core Ops, SparseCore 0:
  12.6 129.9 all-gather.4
  145.5 130.1 all-gather.6
  409.5 124.8 reduce-scatter.1

commit v5 on v4

--- a/solution.py
+++ b/solution.py
@@ -1042,7 +1042,6 @@
     )
 
     sum_c.advance()
-    sum_b.advance()
     d_merge_image = d_resid_image.astype(BF16)
     sum_e.add(
         3 * row_image,
@@ -1055,6 +1054,8 @@
         rows_of,
         attend_back((query_image, 0), (held_text, 0), (held_text, 1), text_fill, d_heads_image, inner, HEADS),
     )
+    sum_b.advance()
+    sum_c.advance()
     g_vectors = (
         g_text_gain_cross,
         g_image_gain_cross,
@@ -1084,7 +1085,7 @@
         (row_vector, g_vector),
         later=True,
     )
-    sum_c.advance()
+    sums_first = widened(sums_first)
     sum_d.hold()
     sum_d.send()
     sum_e.advance()
@@ -1102,7 +1103,6 @@
         + project_back(jnp.concatenate([d_key_image, d_value_image], 1), weight_image_held)
     )
     sum_e.advance()
-    sums_first = widened(sums_first)
     sum_c.advance()
     sum_d.advance()
     sum_e.advance()

time: 617 us -> 606 us (0.982)
  local copies, waits for them, and re-layouts: 108 us -> 96.7 us
    unnamed x340 -> x360, local copies, waits for them, and re-layouts: 58.3 us -> 47.4 us
  transfers between devices with their start and end apart: 48 -> 48, of which waited for: 20 -> 18; matrix products, arithmetic and copies ran while one was open for 34% -> 34% of each run, Pallas kernels for 25% -> 28%
where the time goes in v5:
time: 606 us; the launch traced here: 595 us
  Pallas kernels  166 us (27%)
  waiting for transfers between devices  127 us (21%)
  matrix products  112 us (18%)
  local copies, waits for them, and re-layouts  96.7 us (16%)
  starting transfers between devices  41.7 us (7%)
  other arithmetic  35 us (6%)
  between operations  16.4 us (3%)
    pallas_call x60, Pallas kernels, ordered_call(): pl.pallas_call(body, in_specs=list(in_specs) + [pl.BlockSpec(memory_space...  166 us
    ppermute x45, waiting for transfers between devices, exchange(): lax.ppermute(block, axis, [(at, at ^ 1 << bit) for at in range(lax.axis_s...  109 us
    dot_general x14, matrix products, project_back(): lax.dot_general(left, right, (((1,), (1,)), ((), ())), preferred_element_...  58.5 us
    dot_general x14, matrix products, project(): return jnp.dot(left, right, preferred_element_type=F32)  53.5 us
    unnamed x360, local copies, waits for them, and re-layouts  47.4 us
    ppermute x45, starting transfers between devices, exchange(): lax.ppermute(block, axis, [(at, at ^ 1 << bit) for at in range(lax.axis_s...  41.5 us
    slice x5, local copies, waits for them, and re-layouts, taken(): return whole(block[:, at[0]:at[1]])  28.2 us
    all_gather x2, waiting for transfers between devices, gather(): return lax.all_gather(packed, AXES, axis=0, tiled=False)  18.4 us
  transfers between devices with their start and end apart: 48, of which 18 were waited for; matrix products, arithmetic and copies ran while one was open for 34% of the time, Pallas kernels for 28%

profile of v5, /device:TPU:0, one launch (start us, length us, event | category | flops | bytes accessed | tf_op | source)
XLA Modules:
  0.0 595.1 jit_solution(2002884498849304140)
XLA Ops:
  25.4 15.8 %collective-permute-done = bf16[96,1024]{1,0:T(8,128)(2,1)S(1)} collective-permute-done((bf16[96,1024]{1,0:T(8,128)(2,1)S(1)}, bf16[96,1024]{1,0:T(8,128)(2,1)S(1)}, u32[]{:S(2)}, u32[]{:S(2)}) %collective-permute-start) | collective-permute-done | bytes 196640 | tf_op jit(solution)/shard_map/ppermute | solution.py:198
  43.8 9.3 %collective-permute-done.1 = bf16[2,96,1024]{2,1,0:T(8,128)(2,1)S(1)} collective-permute-done((bf16[2,96,1024]{2,1,0:T(8,128)(2,1)S(1)}, bf16[2,96,1024]{2,1,0:T(8,128)(2,1)S(1)}, u32[]{:S(2)}, u32[]{:S(2)}) %collective-permute-start.1) | collective-permute-done | bytes 393248 | tf_op jit(solution)/shard_map/ppermute | solution.py:198
  56.0 12.6 %collective-permute-done.2 = bf16[2,2,96,512]{3,2,1,0:T(8,128)(2,1)S(1)} collective-permute-done((bf16[2,2,96,512]{3,2,1,0:T(8,128)(2,1)S(1)}, bf16[2,2,96,512]{3,2,1,0:T(8,128)(2,1)S(1)}, u32[]{:S(2)}, u32[]{:S(2)}) %collective-permute-start.2) | collective-permute-done | bytes 393248 | tf_op jit(solution)/shard_map/ppermute | solution.py:198
  76.5 16.0 %collective-permute-done.4 = bf16[2,2,2,96,512]{4,3,2,1,0:T(8,128)(2,1)S(1)} collective-permute-done((bf16[2,2,2,96,512]{4,3,2,1,0:T(8,128)(2,1)S(1)}, bf16[2,2,2,96,512]{4,3,2,1,0:T(8,128)(2,1)S(1)}, u32[]{:S(2)}, u32[]{:S(2)}) %collective-permute-start.4) | collective-permute-done | bytes 786464 | tf_op jit(solution)/shard_map/ppermute | solution.py:198
  124.3 18.3 %all-gather.5.cloned.1.call-done = bf16[10240,768]{1,0:T(8,128)(2,1)} async-done(((bf16[320,768]{1,0:T(8,128)(2,1)}), bf16[10240,768]{1,0:T(8,128)(2,1)}) %all-gather.5.cloned.1.call-update) | async-done | bytes 15728656 | tf_op jit(solution)/shard_map/all_gather | solution.py:177
  152.1 7.1 %fusion.46 = (bf16[32,24,768]{2,1,0:T(8,128)(2,1)}, bf16[32,24,768]{2,1,0:T(8,128)(2,1)}, bf16[32,24,768]{2,1,0:T(8,128)(2,1)}, bf16[32,24,768]{2,1,0:T(8,128)(2...) fusion(bf16[32,320,768]{2,1,0:T(8,128)(2,1)} %bitcast.451), kind=kLoop, calls=%fused_computation.187 | loop fusion | bytes 18874368 | tf_op jit(solution)/shard_map/slice | solution.py:838
  159.2 16.2 %add_convert_fusion = (bf16[832,3072]{1,0:T(8,128)(2,1)}, bf16[832,3072]{1,0:T(8,128)(2,1)S(1)}) fusion(f32[3072]{0:T(1024)S(1)} %reshape.932, bf16[832,768]{1,0:T(8,128)(2,1)S(1)} %multiply_convert_fusion.3.refs_0_, bf16[768,768]{1,0:T(8,128)(2,1)S(1)} %bitcast.488, bf16[768,768]{1,0:T(8,128)(2,1)S(1)} %bitcast.490, bf16[768,768]{1,0:T(8,128)(2,1)S(1)} %bitcast.492, ...), kind=kOutput, calls=%fused_computation.7 | convolution fusion | flops 4011196416 | bytes 16232448 | tf_op jit(solution)/shard_map/dot_general | solution.py:35
  175.5 8.6 %fusion.55 = (f32[832]{0:T(1024)S(1)}, f32[832,768]{1,0:T(8,128)S(1)}) fusion(bf16[832,3072]{1,0:T(8,128)(2,1)S(1)} %get-tuple-element.153.refs_0_, bf16[3072,768]{1,0:T(8,128)(2,1)} %bitcast.462, f32[768]{0:T(1024)S(1)} %reshape.931, f32[832]{0:T(1024)S(1)} %add_rsqrt_fusion.2, f32[832,768]{1,0:T(8,128)S(1)} %get-tuple-element.346, ...), kind=kOutput, calls=%fused_computation.196 | convolution fusion | flops 3929062656 | bytes 14955264 | tf_op jit(solution)/shard_map/dot_general | solution.py:35
  209.5 8.9 %shard_map.511 = (bf16[8,104,768]{2,1,0:T(8,128)(2,1)S(1)}, bf16[8,104,768]{2,1,0:T(8,128)(2,1)S(1)}, bf16[8,104,768]{2,1,0:T(8,128)(2,1)S(1)}) custom-call(bf16[8,104,2304]{2,1,0:T(8,128)(2,1)} %bitcast.441, bf16[8,104,2304]{2,1,0:T(8,128)(2,1)} %bitcast.442, bf16[8,104,2304]{2,1,0:T(8,128)(2,1)} %bitcast.443, f32[8,104,128]{2,1,0:T(8,128)S(1)} %broadcast_in_dim.77.refs_3_, ...), custom_call_target="tpu_custom_call" | custom-call | bytes 22400000 | tf_op jit(solution)/shard_map/pallas_call | solution.py:65
  220.4 7.4 %shard_map.512 = (bf16[2,8,96,768]{3,2,1,0:T(8,128)(2,1)}, bf16[2,8,96,768]{3,2,1,0:T(8,128)(2,1)}) custom-call(bf16[832,768]{1,0:T(8,128)(2,1)S(1)} %multiply_convert_fusion.2.refs_0_, bf16[832,2304]{1,0:T(8,128)(2,1)} %bitcast.452, s32[1]{0:T(128)} %bitcast.64.refs_2_.refs_1_, bf16[8,104,768]{2,1,0:T(8,128)(2,1)S(1)} %get-tuple-element.155.refs_3_), custom_call_target="tpu_custom_call" | custom-call | bytes 24137964 | tf_op jit(solution)/shard_map/pallas_call | solution.py:65
  235.3 7.3 %multiply_reduce_fusion.1 = (bf16[768]{0:T(1024)(128)(2,1)}, f32[832]{0:T(1024)S(1)}, f32[832]{0:T(1024)S(1)}, f32[832,768]{1,0:T(8,128)S(1)}) fusion(f32[832,768]{1,0:T(8,128)S(1)} %copy-done.115, f32[832]{0:T(1024)S(1)} %add_rsqrt_fusion.1, f32[832]{0:T(1024)S(1)} %broadcast_multiply_fusion.8, f32[768]{0:T(1024)S(1)} %reshape.933, ...), kind=kOutput, calls=%fused_computation.24 | convolution fusion | flops 2960766720 | bytes 15058432 | tf_op jit(solution)/shard_map/dot_general | solution.py:39
  250.4 10.3 %fusion.60 = (bf16[3072]{0:T(1024)(128)(2,1)}, bf16[832,3072]{1,0:T(8,128)(2,1)}) fusion(bf16[832,768]{1,0:T(8,128)(2,1)S(1)} %get-tuple-element.288.refs_1_, bf16[3072,768]{1,0:T(8,128)(2,1)} %bitcast.463, bf16[832,3072]{1,0:T(8,128)(2,1)} %get-tuple-element.158), kind=kOutput, calls=%fused_computation.201 | convolution fusion | flops 3936089088 | bytes 16226304 | tf_op jit(solution)/shard_map/dot_general | solution.py:39
  260.7 9.0 %shard_map.515 = (bf16[2,8,96,768]{3,2,1,0:T(8,128)(2,1)}, bf16[2,8,96,768]{3,2,1,0:T(8,128)(2,1)}) custom-call(bf16[832,768]{1,0:T(8,128)(2,1)S(1)} %copy-done.28, bf16[832,3072]{1,0:T(8,128)(2,1)} %get-tuple-element.362.refs_1_, s32[1]{0:T(128)} %bitcast.64.refs_2_.refs_1_, bf16[1,2,4,96,384]{4,3,2,1,0:T(8,128)(2,1)S(1)} %get-tuple-element.164.refs_3_), custom_call_target="tpu_custom_call" | custom-call | bytes 31117288 | tf_op jit(solution)/shard_map/pallas_call | solution.py:65
  270.6 10.1 %shard_map.517 = (bf16[2,8,96,768]{3,2,1,0:T(8,128)(2,1)}, bf16[2,8,96,768]{3,2,1,0:T(8,128)(2,1)}) custom-call(bf16[832,3072]{1,0:T(8,128)(2,1)} %copy-done.133, bf16[832,768]{1,0:T(8,128)(2,1)S(1)} %get-tuple-element.288.refs_1_, s32[1]{0:T(128)} %bitcast.64.refs_2_.refs_1_, bf16[1,4,96,384]{3,2,1,0:T(8,128)(2,1)S(1)} %get-tuple-element.168.refs_3_), custom_call_target="tpu_custom_call" | custom-call | bytes 31117288 | tf_op jit(solution)/shard_map/pallas_call | solution.py:65
  281.4 8.8 %multiply_reduce_fusion.2 = (bf16[768]{0:T(1024)(128)(2,1)}, f32[832]{0:T(1024)S(1)}, f32[832]{0:T(1024)S(1)}, f32[832,768]{1,0:T(8,128)S(1)}) fusion(f32[832,768]{1,0:T(8,128)S(1)} %copy-done.113, f32[832]{0:T(1024)S(1)} %add_rsqrt_fusion.2, f32[832]{0:T(1024)S(1)} %broadcast_multiply_fusion.9, f32[768]{0:T(1024)S(1)} %reshape.931, ...), kind=kOutput, calls=%fused_computation.25 | convolution fusion | flops 3950491392 | bytes 17516032 | tf_op jit(solution)/shard_map/dot_general | solution.py:39
  314.8 6.4 %shard_map.519 = (bf16[8,104,1024]{2,1,0:T(8,128)(2,1)S(1)}, bf16[8,40,1024]{2,1,0:T(8,128)(2,1)S(1)}, bf16[8,40,1024]{2,1,0:T(8,128)(2,1)S(1)}) custom-call(bf16[8,104,1024]{2,1,0:T(8,128)(2,1)} %bitcast.460, bf16[8,40,2048]{2,1,0:T(8,128)(2,1)S(1)} %bitcast.295, bf16[8,40,2048]{2,1,0:T(8,128)(2,1)S(1)} %bitcast.296, ...), custom_call_target="tpu_custom_call" | custom-call | bytes 22400000 | tf_op jit(solution)/shard_map/pallas_call | solution.py:65
  322.4 8.9 %shard_map.520 = (bf16[1,2,4,224,384]{4,3,2,1,0:T(8,128)(2,1)}, bf16[1,2,4,224,384]{4,3,2,1,0:T(8,128)(2,1)S(1)}, bf16[1,4,2,224,384]{4,3,2,1,0:T(8,128)(2,1)}, bf16[1,4,2,224,384]{4,3,2,1,0:T(8,128)(2,1)}) custom-call(s32[2]{0:T(128)S(1)} %pad_add_fusion.2.refs_0_, bf16[1,2,4,2,96,768]{5,4,3,2,1,0:T(8,128)(2,1)} %bitcast.465, ...), custom_call_target="tpu_custom_call" | custom-call | bytes 24662508 | tf_op jit(solution)/shard_map/pallas_call | solution.py:65
  347.5 12.1 %fusion.44 = (bf16[32,32,1024]{2,1,0:T(8,128)(2,1)}, bf16[32,32,1024]{2,1,0:T(8,128)(2,1)}, bf16[32,32,1024]{2,1,0:T(8,128)(2,1)}, bf16[32,32,1024]{2,1,0:T(8,12...) fusion(bf16[32,304,1024]{2,1,0:T(8,128)(2,1)} %bitcast.447), kind=kLoop, calls=%fused_computation.185 | loop fusion | bytes 33554432 | tf_op jit(solution)/shard_map/slice | solution.py:838
  398.4 6.0 %shard_map.531 = (bf16[2,8,128,1024]{3,2,1,0:T(8,128)(2,1)}, bf16[2,8,128,1024]{3,2,1,0:T(8,128)(2,1)}) custom-call(bf16[320,1024]{1,0:T(8,128)(2,1)S(1)} %multiply_convert_fusion.5.refs_0_, bf16[320,3072]{1,0:T(8,128)(2,1)S(1)} %bitcast.316, s32[1]{0:T(128)} %bitcast.64.refs_2_.refs_1_, bf16[8,40,1024]{2,1,0:T(8,128)(2,1)S(1)} %get-tuple-element.190.refs_3_), custom_call_target="tpu_custom_call" | custom-call | bytes 17516556 | tf_op jit(solution)/shard_map/pallas_call | solution.py:65
  431.8 7.6 %shard_map.534 = (bf16[1,2,4,128,512]{4,3,2,1,0:T(8,128)(2,1)}, bf16[1,2,4,128,512]{4,3,2,1,0:T(8,128)(2,1)S(1)}, bf16[1,4,2,128,512]{4,3,2,1,0:T(8,128)(2,1)}, bf16[1,4,2,128,512]{4,3,2,1,0:T(8,128)(2,1)S(1)}) custom-call(s32[2]{0:T(128)S(1)} %pad_add_fusion.2.refs_0_, bf16[1,2,4,2,128,1024]{5,4,3,2,1,0:T(8,128)(2,1)} %bitcast.448, ...), custom_call_target="tpu_custom_call" | custom-call | bytes 18790480 | tf_op jit(solution)/shard_map/pallas_call | solution.py:65
  456.5 7.0 %shard_map.538 = (bf16[8,40,1024]{2,1,0:T(8,128)(2,1)S(1)}, bf16[8,104,1024]{2,1,0:T(8,128)(2,1)S(1)}, bf16[8,104,1024]{2,1,0:T(8,128)(2,1)S(1)}) custom-call(bf16[8,40,1024]{2,1,0:T(8,128)(2,1)S(1)} %bitcast.332, bf16[8,104,2048]{2,1,0:T(8,128)(2,1)} %bitcast.291, bf16[8,104,2048]{2,1,0:T(8,128)(2,1)} %bitcast.292, f32[8,104,128]{2,1,0:T(8,128)S(1)} %copy-done.15, ...), custom_call_target="tpu_custom_call" | custom-call | bytes 22400000 | tf_op jit(solution)/shard_map/pallas_call | solution.py:65
  533.0 8.5 %collective-permute-done.31 = bf16[2,2,2,96,512]{4,3,2,1,0:T(8,128)(2,1)S(1)} collective-permute-done((bf16[2,2,2,96,512]{4,3,2,1,0:T(8,128)(2,1)S(1)}, bf16[2,2,2,96,512]{4,3,2,1,0:T(8,128)(2,1)S(1)}, u32[]{:S(2)}, u32[]{:S(2)}) %collective-permute-start.31) | collective-permute-done | bytes 786464 | tf_op jit(solution)/shard_map/ppermute | solution.py:198
  565.0 10.6 %collective-permute-done.41 = bf16[2,96,1024]{2,1,0:T(8,128)(2,1)S(1)} collective-permute-done((bf16[2,96,1024]{2,1,0:T(8,128)(2,1)S(1)}, bf16[2,96,1024]{2,1,0:T(8,128)(2,1)S(1)}, u32[]{:S(2)}, u32[]{:S(2)}) %collective-permute-start.41) | collective-permute-done | bytes 393248 | tf_op jit(solution)/shard_map/ppermute | solution.py:198
  576.7 8.5 %collective-permute-done.43.refs_1_ = bf16[96,1024]{1,0:T(8,128)(2,1)S(1)} collective-permute-done((bf16[96,1024]{1,0:T(8,128)(2,1)S(1)}, bf16[96,1024]{1,0:T(8,128)(2,1)S(1)}, u32[]{:S(2)}, u32[]{:S(2)}) %collective-permute-start.43) | collective-permute-done | bytes 196640 | tf_op jit(solution)/shard_map/ppermute | solution.py:198
  (641 shorter events, 337.3 us)
Async XLA Ops:
  7.2 135.4 %all-gather.5.cloned.1.call-start = ((), (), s32[]{:S(2)}) async-start(), calls=%async_computation.2 | async-start | bytes 16220160 | tf_op jit(solution)/shard_map/all_gather | solution.py:177
  12.5 332.8 %all-gather.7.cloned.1.call-start = ((), (), s32[]{:S(2)}) async-start(), calls=%async_computation.3 | async-start | bytes 20545536 | tf_op jit(solution)/shard_map/all_gather | solution.py:177
  20.3 20.9 %collective-permute-start = (bf16[96,1024]{1,0:T(8,128)(2,1)S(1)}, bf16[96,1024]{1,0:T(8,128)(2,1)S(1)}, u32[]{:S(2)}, u32[]{:S(2)}) collective-permute-start(bf16[96,1024]{1,0:T(8,128)(2,1)S(1)} %shard_map.502.refs_8_), channel_id=1, source_target_pairs={{0,4},{1,5},{2,6},{3,7},{4,0},{5,1},{6,2},{7,3},{8,12},{9,13},{10,... | collective-permute-start | bytes 589832 | tf_op jit(solution)/shard_map/ppermute | solution.py:198
  115.5 366.1 %reduce-scatter.2.cloned.1.call-start = ((), (), s32[]{:S(2)}) async-start(), calls=%async_computation.1 | async-start | bytes 6488064 | tf_op jit(solution)/shard_map/reduce_scatter | solution.py:511
  248.8 20.9 %collective-permute-start.9 = (bf16[2,2,2,96,384]{4,3,2,1,0:T(8,128)(2,1)S(1)}, bf16[2,2,2,96,384]{4,3,2,1,0:T(8,128)(2,1)S(1)}, u32[]{:S(2)}, u32[]{:S(2)}) collective-permute-start(bf16[2,2,2,96,384]{4,3,2,1,0:T(8,128)(2,1)S(1)} %bitcast.371), channel_id=1, source_target_pairs={{0,1},{1,0},{2,3},{3,2},{4,5},{5,4},{6,7},{7,6},{8,9},{9,8},{10,11... | collective-permute-start | bytes 1769480 | tf_op jit(solution)/shard_map/ppermute | solution.py:198
  269.7 52.7 %collective-permute-start.13 = (bf16[2,8,96,768]{3,2,1,0:T(8,128)(2,1)}, bf16[2,8,96,768]{3,2,1,0:T(8,128)(2,1)}, u32[]{:S(2)}, u32[]{:S(2)}) collective-permute-start(bf16[2,8,96,768]{3,2,1,0:T(8,128)(2,1)} %get-tuple-element.167.refs_5_), channel_id=1, source_target_pairs={{0,8},{8,0},{16,24},{24,16},{1,9},{9,1},{17,25},{25,17},{2,10},{10... | collective-permute-start | bytes 7077896 | tf_op jit(solution)/shard_map/ppermute | solution.py:198
  280.7 41.7 %collective-permute-start.14 = (bf16[2,8,96,768]{3,2,1,0:T(8,128)(2,1)}, bf16[2,8,96,768]{3,2,1,0:T(8,128)(2,1)}, u32[]{:S(2)}, u32[]{:S(2)}) collective-permute-start(bf16[2,8,96,768]{3,2,1,0:T(8,128)(2,1)} %get-tuple-element.169.refs_3_), channel_id=1, source_target_pairs={{0,8},{8,0},{16,24},{24,16},{1,9},{9,1},{17,25},{25,17},{2,10},{10... | collective-permute-start | bytes 7077896 | tf_op jit(solution)/shard_map/ppermute | solution.py:198
  295.4 27.0 %collective-permute-start.15 = (bf16[2,8,32,768]{3,2,1,0:T(8,128)(2,1)}, bf16[2,8,32,768]{3,2,1,0:T(8,128)(2,1)}, u32[]{:S(2)}, u32[]{:S(2)}) collective-permute-start(bf16[2,8,32,768]{3,2,1,0:T(8,128)(2,1)} %get-tuple-element.170.refs_5_), channel_id=1, source_target_pairs={{0,8},{8,0},{16,24},{24,16},{1,9},{9,1},{17,25},{25,17},{2,10},{10... | collective-permute-start | bytes 2359304 | tf_op jit(solution)/shard_map/ppermute | solution.py:198
  308.3 24.3 %collective-permute-start.11 = (bf16[2,2,96,384]{3,2,1,0:T(8,128)(2,1)}, bf16[2,2,96,384]{3,2,1,0:T(8,128)(2,1)S(1)}, u32[]{:S(2)}, u32[]{:S(2)}) collective-permute-start(bf16[2,2,96,384]{3,2,1,0:T(8,128)(2,1)} %bitcast.408), channel_id=1, source_target_pairs={{0,16},{8,24},{16,0},{24,8},{1,17},{9,25},{17,1},{25,9},{2,18},{10... | collective-permute-start | bytes 884744 | tf_op jit(solution)/shard_map/ppermute | solution.py:198
  309.8 22.8 %collective-permute-start.12 = (bf16[2,2,96,384]{3,2,1,0:T(8,128)(2,1)}, bf16[2,2,96,384]{3,2,1,0:T(8,128)(2,1)S(1)}, u32[]{:S(2)}, u32[]{:S(2)}) collective-permute-start(bf16[2,2,96,384]{3,2,1,0:T(8,128)(2,1)} %bitcast.436), channel_id=1, source_target_pairs={{0,1},{1,0},{2,3},{3,2},{4,5},{5,4},{6,7},{7,6},{8,9},{9,8},{10,11... | collective-permute-start | bytes 884744 | tf_op jit(solution)/shard_map/ppermute | solution.py:198
  336.2 37.9 %collective-permute-start.16 = (bf16[2,96,768]{2,1,0:T(8,128)(2,1)S(1)}, bf16[2,96,768]{2,1,0:T(8,128)(2,1)}, u32[]{:S(2)}, u32[]{:S(2)}) collective-permute-start(bf16[2,96,768]{2,1,0:T(8,128)(2,1)S(1)} %bitcast.402), channel_id=1, source_target_pairs={{0,2},{1,3},{2,0},{3,1},{4,6},{5,7},{6,4},{7,5},{8,10},{9,11},{10,... | collective-permute-start | bytes 884744 | tf_op jit(solution)/shard_map/ppermute | solution.py:198
  337.2 53.7 %collective-permute-start.18 = (bf16[2,2,2,224,384]{4,3,2,1,0:T(8,128)(2,1)}, bf16[2,2,2,224,384]{4,3,2,1,0:T(8,128)(2,1)}, u32[]{:S(2)}, u32[]{:S(2)}) collective-permute-start(bf16[2,2,2,224,384]{4,3,2,1,0:T(8,128)(2,1)} %bitcast.106), channel_id=1, source_target_pairs={{0,1},{1,0},{2,3},{3,2},{4,5},{5,4},{6,7},{7,6},{8,9},{9,8},{10,11... | collective-permute-start | bytes 4128776 | tf_op jit(solution)/shard_map/ppermute | solution.py:198
  338.4 52.5 %collective-permute-start.19 = (bf16[2,2,2,224,384]{4,3,2,1,0:T(8,128)(2,1)}, bf16[2,2,2,224,384]{4,3,2,1,0:T(8,128)(2,1)}, u32[]{:S(2)}, u32[]{:S(2)}) collective-permute-start(bf16[2,2,2,224,384]{4,3,2,1,0:T(8,128)(2,1)} %bitcast.109), channel_id=1, source_target_pairs={{0,16},{8,24},{16,0},{24,8},{1,17},{9,25},{17,1},{25,9},{2,18},{10... | collective-permute-start | bytes 4128776 | tf_op jit(solution)/shard_map/ppermute | solution.py:198
  407.3 24.5 %collective-permute-start.20 = (bf16[2,8,128,1024]{3,2,1,0:T(8,128)(2,1)}, bf16[2,8,128,1024]{3,2,1,0:T(8,128)(2,1)}, u32[]{:S(2)}, u32[]{:S(2)}) collective-permute-start(bf16[2,8,128,1024]{3,2,1,0:T(8,128)(2,1)} %get-tuple-element.197.refs_5_), channel_id=1, source_target_pairs={{0,8},{8,0},{16,24},{24,16},{1,9},{9,1},{17,25},{25,17},{2,10},{10... | collective-permute-start | bytes 12582920 | tf_op jit(solution)/shard_map/ppermute | solution.py:198
  439.5 27.4 %collective-permute-start.23 = (bf16[2,2,2,128,512]{4,3,2,1,0:T(8,128)(2,1)}, bf16[2,2,2,128,512]{4,3,2,1,0:T(8,128)(2,1)S(1)}, u32[]{:S(2)}, u32[]{:S(2)}) collective-permute-start(bf16[2,2,2,128,512]{4,3,2,1,0:T(8,128)(2,1)} %bitcast.136), channel_id=1, source_target_pairs={{0,1},{1,0},{2,3},{3,2},{4,5},{5,4},{6,7},{7,6},{8,9},{9,8},{10,11... | collective-permute-start | bytes 3145736 | tf_op jit(solution)/shard_map/ppermute | solution.py:198
  440.5 27.4 %collective-permute-start.24 = (bf16[2,2,2,128,512]{4,3,2,1,0:T(8,128)(2,1)}, bf16[2,2,2,128,512]{4,3,2,1,0:T(8,128)(2,1)}, u32[]{:S(2)}, u32[]{:S(2)}) collective-permute-start(bf16[2,2,2,128,512]{4,3,2,1,0:T(8,128)(2,1)} %bitcast.139), channel_id=1, source_target_pairs={{0,16},{8,24},{16,0},{24,8},{1,17},{9,25},{17,1},{25,9},{2,18},{10... | collective-permute-start | bytes 3145736 | tf_op jit(solution)/shard_map/ppermute | solution.py:198
  441.9 21.7 %collective-permute-start.25 = (bf16[2,224,768]{2,1,0:T(8,128)(2,1)}, bf16[2,224,768]{2,1,0:T(8,128)(2,1)}, u32[]{:S(2)}, u32[]{:S(2)}) collective-permute-start(bf16[2,224,768]{2,1,0:T(8,128)(2,1)} %bitcast.142), channel_id=1, source_target_pairs={{0,2},{1,3},{2,0},{3,1},{4,6},{5,7},{6,4},{7,5},{8,10},{9,11},{10,... | collective-permute-start | bytes 2064392 | tf_op jit(solution)/shard_map/ppermute | solution.py:198
  454.9 43.2 %collective-permute-start.30 = (bf16[2,8,96,1024]{3,2,1,0:T(8,128)(2,1)S(1)}, bf16[2,8,96,1024]{3,2,1,0:T(8,128)(2,1)}, u32[]{:S(2)}, u32[]{:S(2)}) collective-permute-start(bf16[2,8,96,1024]{3,2,1,0:T(8,128)(2,1)S(1)} %get-tuple-element.207.refs_5_), channel_id=1, source_target_pairs={{0,8},{8,0},{16,24},{24,16},{1,9},{9,1},{17,25},{25,17},{2,10},{10... | collective-permute-start | bytes 9437192 | tf_op jit(solution)/shard_map/ppermute | solution.py:198
  482.5 21.7 %collective-permute-start.29 = (bf16[2,8,96,1024]{3,2,1,0:T(8,128)(2,1)}, bf16[2,8,96,1024]{3,2,1,0:T(8,128)(2,1)}, u32[]{:S(2)}, u32[]{:S(2)}) collective-permute-start(bf16[2,8,96,1024]{3,2,1,0:T(8,128)(2,1)} %shard_map.546.refs_3_), channel_id=1, source_target_pairs={{0,8},{8,0},{16,24},{24,16},{1,9},{9,1},{17,25},{25,17},{2,10},{10... | collective-permute-start | bytes 9437192 | tf_op jit(solution)/shard_map/ppermute | solution.py:198
  487.6 32.4 %collective-permute-start.26 = (bf16[224,768]{1,0:T(8,128)(2,1)}, bf16[224,768]{1,0:T(8,128)(2,1)S(1)}, u32[]{:S(2)}, u32[]{:S(2)}) collective-permute-start(bf16[224,768]{1,0:T(8,128)(2,1)} %bitcast.145), channel_id=1, source_target_pairs={{0,4},{1,5},{2,6},{3,7},{4,0},{5,1},{6,2},{7,3},{8,12},{9,13},{10,... | collective-permute-start | bytes 1032200 | tf_op jit(solution)/shard_map/ppermute | solution.py:198
  503.5 25.5 %collective-permute-start.34 = (bf16[2,2,2,96,512]{4,3,2,1,0:T(8,128)(2,1)S(1)}, bf16[2,2,2,96,512]{4,3,2,1,0:T(8,128)(2,1)S(1)}, u32[]{:S(2)}, u32[]{:S(2)}) collective-permute-start(bf16[2,2,2,96,512]{4,3,2,1,0:T(8,128)(2,1)S(1)} %bitcast.345), channel_id=1, source_target_pairs={{0,1},{1,0},{2,3},{3,2},{4,5},{5,4},{6,7},{7,6},{8,9},{9,8},{10,11... | collective-permute-start | bytes 2359304 | tf_op jit(solution)/shard_map/ppermute | solution.py:198
  504.2 24.8 %collective-permute-start.35 = (bf16[2,2,2,96,512]{4,3,2,1,0:T(8,128)(2,1)S(1)}, bf16[2,2,2,96,512]{4,3,2,1,0:T(8,128)(2,1)S(1)}, u32[]{:S(2)}, u32[]{:S(2)}) collective-permute-start(bf16[2,2,2,96,512]{4,3,2,1,0:T(8,128)(2,1)S(1)} %bitcast.430), channel_id=1, source_target_pairs={{0,16},{8,24},{16,0},{24,8},{1,17},{9,25},{17,1},{25,9},{2,18},{10... | collective-permute-start | bytes 2359304 | tf_op jit(solution)/shard_map/ppermute | solution.py:198
  511.2 30.3 %collective-permute-start.31 = (bf16[2,2,2,96,512]{4,3,2,1,0:T(8,128)(2,1)S(1)}, bf16[2,2,2,96,512]{4,3,2,1,0:T(8,128)(2,1)S(1)}, u32[]{:S(2)}, u32[]{:S(2)}) collective-permute-start(bf16[2,2,2,96,512]{4,3,2,1,0:T(8,128)(2,1)S(1)} %bitcast.349), channel_id=1, source_target_pairs={{0,1},{1,0},{2,3},{3,2},{4,5},{5,4},{6,7},{7,6},{8,9},{9,8},{10,11... | collective-permute-start | bytes 2359304 | tf_op jit(solution)/shard_map/ppermute | solution.py:198
  512.6 28.9 %collective-permute-start.32 = (bf16[2,2,2,96,512]{4,3,2,1,0:T(8,128)(2,1)S(1)}, bf16[2,2,2,96,512]{4,3,2,1,0:T(8,128)(2,1)S(1)}, u32[]{:S(2)}, u32[]{:S(2)}) collective-permute-start(bf16[2,2,2,96,512]{4,3,2,1,0:T(8,128)(2,1)S(1)} %bitcast.429), channel_id=1, source_target_pairs={{0,16},{8,24},{16,0},{24,8},{1,17},{9,25},{17,1},{25,9},{2,18},{10... | collective-permute-start | bytes 2359304 | tf_op jit(solution)/shard_map/ppermute | solution.py:198
  (197 other events, 1539.5 us)
Sparse Core Ops, SparseCore 0:
  12.6 129.9 all-gather.4
  145.5 130.1 all-gather.6
  345.4 114.6 reduce-scatter.1
